TPU v7x, 32 devices: a whole 2x2x4 slice. The times are simulated.
32 devices in a mesh: feat: 8 (over y, x, core), layer: 4 (over z).
Axes of the slice: x: 2, y: 2, z: 4, core: 2. Of those that a mesh axis runs over, the one named last changes fastest.
Arguments:
- residual_in: bfloat16 [4, 24, 2304], P('layer', 'feat'), as said below
- enc_weight: bfloat16 [4, 2304, 8192], P('layer', None, 'feat'), as said below
- thresholds: int32 [4, 8192], P('layer', 'feat'), may hold values from -2016 to 7341, as said below
- dec_weight: bfloat16 [4, 4, 8192, 2304], P(None, 'layer', 'feat'), may hold values from -0.03125 to 0.03125
- target: bfloat16 [4, 24, 2304], P('layer', 'feat')
Outputs:
- loss_value: float32 [], replicated
- reconstruction: bfloat16 [4, 24, 2304], P('layer', 'feat')
- dec_grad: bfloat16 [4, 4, 8192, 2304], P(None, 'layer', 'feat')
- enc_grad: bfloat16 [4, 2304, 8192], P('layer', None, 'feat')
Inputs may be any that keep to these rules, and one draw needn't show every extreme that they name: `residual_in`: every entry is a multiple of 1/8. `enc_weight`: every entry is a multiple of 1/256. `thresholds`: whole numbers.
All inputs are finite; a program needn't handle non-finite values.
Results may differ from a plain program's by a relative error of at most 0.007.
Values may be sent and summed in bfloat16 or wider, within the bound.
No kernel may reach another device: no remote copies, remote signals or barrier semaphores. Data moves between devices by JAX's collectives and lax.ppermute only.
A program may use at most 128 MiB of HBM per device.

v0:
```python
import jax
import jax.numpy as jnp
from jax import lax
from jax.sharding import PartitionSpec as P

ERROR_SCALE = 32.0
PENALTY_WEIGHT = 4.0


def body(residual_in, enc_weight, thresholds, dec_weight, target):
    local_rows = residual_in[0]
    encoder = enc_weight[0]
    jump_level = (thresholds[0].astype(jnp.float32) + 0.5) / 2048.0
    preactivation = jnp.dot(
        lax.all_gather(local_rows, "feat", axis=0, tiled=True),
        encoder,
        preferred_element_type=jnp.float32,
    )
    active_mask = preactivation > jump_level[None, :]
    layer_activations = jnp.where(active_mask, preactivation, 0.0).astype(jnp.bfloat16)
    token_count = preactivation.shape[0]
    magnitude = jnp.mean(jnp.abs(layer_activations.astype(jnp.float32)), axis=0)
    penalty_local = jnp.sum(magnitude * magnitude)
    penalty_total = lax.psum(penalty_local, ("feat", "layer"))
    all_acts = lax.all_gather(layer_activations[None], "layer", axis=0, tiled=True)
    decoder = dec_weight[:, 0]
    recon = lax.psum_scatter(
        jnp.einsum("sif,sfd->id", all_acts, decoder, preferred_element_type=jnp.float32),
        "feat",
        scatter_dimension=0,
        tiled=True,
    )
    error_rows = recon - target[0].astype(jnp.float32)
    grad_local = (error_rows / ERROR_SCALE).astype(jnp.bfloat16)
    grad_all = lax.all_gather(grad_local, "feat", axis=0, tiled=True)
    squares_local = jnp.sum(error_rows * error_rows)
    squares_total = lax.psum(squares_local, ("feat", "layer"))
    dec_grad = jnp.einsum(
        "sif,id->sfd", all_acts, grad_all, preferred_element_type=jnp.float32
    ).astype(jnp.bfloat16)
    act_part = jnp.einsum("id,sfd->sif", grad_all, decoder, preferred_element_type=jnp.float32)
    activation_gradient = lax.psum_scatter(act_part, "layer", scatter_dimension=0, tiled=True)[0]
    sparsity_gradient = (
        2.0
        * PENALTY_WEIGHT
        * magnitude[None, :]
        * jnp.sign(layer_activations.astype(jnp.float32))
        / token_count
    )
    preactivation_gradient = jnp.where(
        active_mask, activation_gradient + sparsity_gradient, 0.0
    ).astype(jnp.bfloat16)
    enc_grad = jnp.einsum(
        "id,if->df",
        lax.all_gather(local_rows, "feat", axis=0, tiled=True),
        preactivation_gradient,
        preferred_element_type=jnp.float32,
    )
    loss_value = (squares_total + 2.0 * ERROR_SCALE * PENALTY_WEIGHT * penalty_total) / (
        lax.axis_size("layer") * token_count * local_rows.shape[1]
    )
    return (
        loss_value,
        recon.astype(jnp.bfloat16)[None],
        dec_grad[:, None],
        enc_grad.astype(jnp.bfloat16)[None],
    )


def solution(mesh):
    return jax.shard_map(
        body,
        mesh=mesh,
        in_specs=(
            P("layer", "feat", None),
            P("layer", None, "feat"),
            P("layer", "feat"),
            P(None, "layer", "feat", None),
            P("layer", "feat", None),
        ),
        out_specs=(
            P(),
            P("layer", "feat", None),
            P(None, "layer", "feat", None),
            P("layer", None, "feat"),
        ),
        check_vma=False,
    )
```

profile of v0, /device:TPU:0, one launch (start us, length us, event | category | flops | bytes accessed | tf_op | source)
XLA Modules:
  0.0 193.5 jit_solution(4813231889663786020)
XLA Ops:
  7.2 0.0 copy-start.1
  7.2 0.0 all-reduce.4.cloned.1.call-start
  7.2 0.7 add_multiply_fusion
  7.9 0.7 copy.16
  8.7 10.8 %all-gather = bf16[1,24,2304]{2,0,1:T(2,128)(2,1)S(1)} all-gather(bf16[1,3,2304]{2,0,1:T(2,128)(2,1)S(1)} %copy.16), channel_id=2, replica_groups=mesh['feat'=8,'layer'=4] {'feat'}, dimensions={1}, use_global_device_ids=true | all-gather | bytes 124416 | tf_op jit(solution)/shard_map/all_gather | solution.py:15
  19.4 3.1 %fusion.16 = (f32[1024]{0:T(1024)S(1)}, bf16[24,1024]{1,0:T(8,128)(2,1)S(1)}, f32[24,1024]{1,0:T(8,128)S(1)}) fusion(f32[1024]{0:T(1024)S(1)} %bitcast.53, bf16[1,2304,1024]{2,1,0:T(8,128)(2,1)} %param.6, bf16[1,24,2304]{2,0,1:T(2,128)(2,1)S(1)} %all-gather), kind=kOutput, calls=%fused_computation.18 | convolution fusion | flops 113392640 | bytes 4984832 | tf_op jit(solution)/shard_map/dot_general | solution.py:14
  22.5 13.9 %all-gather.1 = bf16[96,1024]{1,0:T(8,128)(2,1)S(1)} all-gather(bf16[24,1024]{1,0:T(8,128)(2,1)S(1)} %get-tuple-element.23), channel_id=3, replica_groups=mesh['feat'=8,'layer'=4] {'layer'}, dimensions={0}, use_global_device_ids=true | all-gather | bytes 245760 | tf_op jit(solution)/shard_map/all_gather | solution.py:25
  36.4 9.6 %fusion.8 = f32[24,2304]{1,0:T(8,128)} fusion(bf16[4,24,1024]{2,1,0:T(8,128)(2,1)S(1)} %bitcast.51, bf16[4,1,1024,2304]{3,2,1,0:T(8,128)(2,1)} %param.8), kind=kOutput, calls=%fused_computation.10 | convolution fusion | flops 452984832 | bytes 19292160 | tf_op jit(solution)/shard_map/sif,sfd->id/dot_general | solution.py:28
  46.0 0.0 all-reduce.4.cloned.1.call-update
  46.1 0.0 reduce-scatter.2.cloned.1.call-start
  46.1 0.6 broadcast_multiply_fusion
  46.7 0.0 copy-done.1
  46.7 0.6 dynamic-slice
  47.9 50.7 %all-reduce.4.cloned.1.call-done = f32[24,2304]{1,0:T(8,128)} async-done(((f32[24,2304]{1,0:T(8,128)}), f32[24,2304]{1,0:T(8,128)}) %all-reduce.4.cloned.1.call-update) | async-done | bytes 221200
  98.7 1.5 fusion.30
  100.2 10.0 %all-gather.2 = bf16[8,3,2304]{2,1,0:T(4,128)(2,1)S(1)} all-gather(bf16[1,3,2304]{2,1,0:T(4,128)(2,1)S(1)} %get-tuple-element.24), channel_id=1, replica_groups=mesh['feat'=8,'layer'=4] {'feat'}, dimensions={0}, use_global_device_ids=true | all-gather | bytes 124416 | tf_op jit(solution)/shard_map/all_gather | solution.py:35
  110.2 0.1 reshape.20
  110.3 12.1 %fusion.11 = f32[4,24,1024]{2,1,0:T(8,128)} fusion(bf16[24,2304,1]{1,0,2:T(8,128)(2,1)S(1)} %reshape.20, bf16[4,1,1024,2304]{3,2,1,0:T(8,128)(2,1)} %param.8), kind=kOutput, calls=%fused_computation.11 | convolution fusion | flops 452984832 | bytes 19378176 | tf_op jit(solution)/shard_map/id,sfd->sif/dot_general | solution.py:41
  122.4 0.0 reduce-scatter.2.cloned.1.call-update
  122.4 39.6 %all-reduce.1 = (f32[]{:T(128)}, f32[]{:T(128)}) all-reduce(f32[]{:T(128)} %get-tuple-element.25, f32[]{:T(128)} %get-tuple-element.27), channel_id=1, replica_groups=mesh['feat'=8,'layer'=4] {'feat','layer'}, use_global_device_ids=true, to_apply=%region_2.3 | all-reduce | flops 2 | bytes 16 | tf_op jit(solution)/shard_map/psum | solution.py:37
  163.4 1.5 fusion.29
  164.9 9.5 %fusion.4 = bf16[4,1,1024,2304]{3,2,1,0:T(8,128)(2,1)} fusion(bf16[4,24,1024]{2,1,0:T(8,128)(2,1)S(1)} %bitcast.52, bf16[24,2304,1]{1,0,2:T(8,128)(2,1)S(1)} %reshape.20), kind=kOutput, calls=%fused_computation.5 | convolution fusion | flops 462422016 | bytes 19181568 | tf_op jit(solution)/shard_map/sif,id->sfd/dot_general | solution.py:38
  174.4 4.5 %fusion.5 = bf16[1,2304,1024]{1,2,0:T(8,128)(2,1)} fusion(bf16[24,1024]{1,0:T(8,128)(2,1)S(1)} %get-tuple-element.23, f32[24,1024]{1,0:T(8,128)S(1)} %get-tuple-element.28, f32[1,24,1024]{2,1,0:T(8,128)} %reduce-scatter.2.cloned.1.call-done, f32[1024]{0:T(1024)S(1)} %get-tuple-element.26, f32[1024]{0:T(1024)S(1)} %bitcast.54, ...), kind=kOutput, calls=%fused_computation.7 | convolution fusion | flops 115802112 | bytes 5083136 | tf_op jit(solution)/shard_map/id,if->df/dot_general | solution.py:53
  178.9 6.6 %copy.18 = bf16[1,2304,1024]{2,1,0:T(8,128)(2,1)} copy(bf16[1,2304,1024]{1,2,0:T(8,128)(2,1)} %fusion.5) | data formatting | bytes 9437184
  (3 shorter events, 0.0 us)
Async XLA Ops:
  7.2 39.5 %copy-start.1 = (u32[32]{0:T(128)S(1)}, u32[32]{0:T(128)}, u32[]{:S(2)}) copy-start(u32[32]{0:T(128)} %constant.30) | copy-start | bytes 388
  7.2 91.5 %copy-start = (bf16[1,3,2304]{2,1,0:T(4,128)(2,1)S(1)}, bf16[1,3,2304]{2,1,0:T(4,128)(2,1)}, u32[]{:S(2)}) copy-start(bf16[1,3,2304]{2,1,0:T(4,128)(2,1)} %param.9) | copy-start | bytes 41476
  7.2 91.5 %all-reduce.4.cloned.1.call-start = ((), (), s32[]{:S(2)}) async-start(), calls=%async_computation.2 | async-start | bytes 442368
  46.1 128.4 %reduce-scatter.2.cloned.1.call-start = ((), (), s32[]{:S(2)}) async-start(), calls=%async_computation.1 | async-start | bytes 491520 | tf_op jit(solution)/shard_map/reduce_scatter | solution.py:42
Sparse Core Ops, SparseCore 0:
  46.2 52.4 all-reduce.3
  122.5 20.6 reduce-scatter.1
where the time goes:
time: 194 us; the launch traced here: 193 us
  blocking collectives  74.3 us (38%)
  waiting for transfers between devices  50.8 us (26%)
  matrix products  38.8 us (20%)
  between operations  17.2 us (9%)
  local copies, waits for them, and re-layouts  9.58 us (5%)
  other arithmetic  2.83 us (1%)
    unnamed x3, waiting for transfers between devices  50.8 us
    psum x1, blocking collectives, body(): squares_total = lax.psum(squares_local, ('feat', 'layer'))  39.6 us
    all_gather x1, blocking collectives, body(): lax.all_gather(layer_activations[None], 'layer', axis=0, tiled=True)  13.9 us
    dot_general x1, matrix products, body(): jnp.einsum('id,sfd->sif', grad_all, decoder, preferred_element_type=jnp.f...  12.1 us
    all_gather x1, blocking collectives, body(): lax.all_gather(local_rows, 'feat', axis=0, tiled=True)  10.8 us
    all_gather x1, blocking collectives, body(): grad_all = lax.all_gather(grad_local, 'feat', axis=0, tiled=True)  9.99 us
    dot_general x1, matrix products, body(): jnp.einsum('sif,sfd->id', all_acts, decoder, preferred_element_type=jnp.f...  9.61 us
    dot_general x1, matrix products, body(): jnp.einsum('sif,id->sfd', all_acts, grad_all, preferred_element_type=jnp....  9.52 us
  transfers between devices with their start and end apart: 2, of which 1 were waited for; matrix products, arithmetic and copies ran while one was open for 6% of the time, Pallas kernels for 0%

commit v1 on v0

v1 whole, which is shorter than its diff:
```python
import functools

import jax
import jax.numpy as jnp
from jax import lax
from jax.experimental import pallas as pl
from jax.experimental.pallas import tpu as pltpu
from jax.sharding import PartitionSpec as P

ERROR_SCALE = 32.0
PENALTY_WEIGHT = 4.0
F32 = jnp.float32
BF16 = jnp.bfloat16
LANES = 128
MIB = 1 << 20
WHOLE = pl.BlockSpec(memory_space=pltpu.VMEM)
ANY = pl.BlockSpec(memory_space=pl.ANY)
NT = (((1,), (1,)), ((), ()))
TN = (((0,), (0,)), ((), ()))


def in_vmem(x):
    return pltpu.with_memory_space_constraint(x, pltpu.VMEM)


def shape(dims, dtype):
    return jax.ShapeDtypeStruct(dims, dtype)


def call(body, outs, args, name, scratch=(), limit=16, in_specs=None, out_specs=None, flops=0, bytes_accessed=0):
    return pl.pallas_call(
        body,
        out_shape=outs,
        in_specs=in_specs or [WHOLE] * len(args),
        out_specs=out_specs or [WHOLE] * len(outs),
        scratch_shapes=list(scratch),
        compiler_params=pltpu.CompilerParams(vmem_limit_bytes=limit * MIB),
        cost_estimate=pl.CostEstimate(flops=flops, bytes_accessed=bytes_accessed, transcendentals=0),
        name=name,
    )(*args)


def swap(x, axis, bits):
    size = lax.axis_size(axis)
    return lax.ppermute(x, axis, [(i, i ^ bits) for i in range(size)])


def split3(value):
    high = value.astype(BF16)
    rest = value - high.astype(F32)
    middle = rest.astype(BF16)
    low = (rest - middle.astype(F32)).astype(BF16)
    return high, middle, low


def spread3(value, dims):
    high, middle, low = (part.astype(F32) for part in split3(value))
    lane = lax.broadcasted_iota(jnp.int32, dims, 1)
    block = jnp.where(lane == 0, high, jnp.where(lane == 1, middle, jnp.where(lane == 2, low, 0.0)))
    return block.astype(BF16)


def encode(x_ref, enc_ref, thr_ref, acts_ref, gate_ref, sparse_ref, pen_ref):
    tokens = x_ref.shape[0]
    cutoff = (thr_ref[...].astype(F32) + 0.5) / 2048.0
    preact = jnp.dot(x_ref[...], enc_ref[...], preferred_element_type=F32)
    firing = preact > cutoff
    acts = jnp.where(firing, preact, 0.0).astype(BF16)
    acts_ref[...] = acts
    wide = acts.astype(F32)
    magnitude = jnp.sum(jnp.abs(wide), axis=0, keepdims=True) / tokens
    sign = jnp.where(wide > 0, 1.0, jnp.where(wide < 0, -1.0, 0.0))
    gate_ref[...] = firing.astype(F32)
    sparse_ref[...] = 2.0 * PENALTY_WEIGHT * magnitude * sign / tokens
    pen = jnp.sum(magnitude * magnitude, axis=1, keepdims=True)
    pen_ref[...] = jnp.broadcast_to(pen, pen_ref.shape)


def recon_own(acts_ref, dec_hbm, dec_ref, total_ref, sems):
    sources = dec_hbm.shape[0]
    me = lax.axis_index("layer")
    copies = []
    for k in range(sources):
        copies.append(pltpu.make_async_copy(dec_hbm.at[me ^ k], dec_ref.at[me ^ k], sems.at[k]))
        copies[-1].start()
    copies[0].wait()
    total_ref[...] = jnp.dot(acts_ref[...], dec_ref[me], preferred_element_type=F32)
    for k in range(1, sources):
        copies[k].wait()


def recon_rest(*refs):
    total_ref, pen_ref, dec_ref, *acts = refs[:-2]
    keep_ref, send_ref = refs[-2:]
    me = lax.axis_index("layer")
    half = dec_ref.shape[2] // 2
    total = total_ref[...]
    for k, acts_ref in enumerate(acts, 1):
        total = total + jnp.dot(acts_ref[...], dec_ref[me ^ k], preferred_element_type=F32)
    first, second = total[:, :half], total[:, half:]
    low = lax.axis_index("feat") % 2 == 0
    pen = jnp.broadcast_to(pen_ref[0:1, :], (total.shape[0], LANES))
    keep_ref[:, :half] = jnp.where(low, first, second)
    send_ref[:, :half] = jnp.where(low, second, first)
    keep_ref[:, half:] = pen
    send_ref[:, half:] = pen


def pair_sum(keep_ref, got_ref, msg_ref):
    half = keep_ref.shape[1] - LANES
    msg_ref[:, :half] = (keep_ref[:, :half] + got_ref[:, :half]).astype(BF16)
    pen = keep_ref[0:1, half : half + 1] + got_ref[0:1, half : half + 1]
    msg_ref[:, half:] = spread3(pen, (keep_ref.shape[0], LANES))


def sum_messages(refs):
    terms = [ref[...].astype(F32) for ref in refs]
    while len(terms) > 1:
        terms = [terms[i] + terms[i + 1] for i in range(0, len(terms), 2)]
    return terms[0]


def group_sum(*refs):
    half = refs[0].shape[1] - LANES
    total = sum_messages(refs[:-1])
    refs[-1][:, :half] = total[:, :half].astype(BF16)
    pen = jnp.sum(total[0:1, half:], axis=1, keepdims=True)
    refs[-1][:, half:] = spread3(pen, (total.shape[0], LANES))


def pick_rows(device, rows, tokens):
    row = lax.broadcasted_iota(jnp.int32, (8, tokens), 0)
    column = lax.broadcasted_iota(jnp.int32, (8, tokens), 1)
    return jnp.where((column == device * rows + row) & (row < rows), 1.0, 0.0).astype(BF16)


def error_half(rows, target_ref, *refs):
    *msgs, out_ref, own_ref, pen_ref = refs
    tokens, half = target_ref.shape[0], target_ref.shape[1] // 2
    me = lax.axis_index("feat")
    total = sum_messages(msgs)
    recon = total[:, :half]
    target = jnp.where(me % 2 == 0, target_ref[:, :half], target_ref[:, half:]).astype(F32)
    error = recon - target
    squares = jnp.sum(jnp.sum(error * error, axis=1, keepdims=True), axis=0, keepdims=True)
    narrow = recon.astype(BF16)
    own_ref[...] = jnp.dot(pick_rows(me, rows, tokens), narrow, preferred_element_type=F32)
    theirs = jnp.dot(pick_rows(me ^ 1, rows, tokens), narrow, preferred_element_type=F32)
    row = lax.broadcasted_iota(jnp.int32, (8, half), 0)
    parts = spread3(squares, (8, LANES)).astype(F32)
    parts = jnp.concatenate([parts, jnp.zeros((8, half - LANES), F32)], axis=1)
    out_ref[:tokens, :] = (error / ERROR_SCALE).astype(BF16)
    out_ref[tokens:, :] = jnp.where(row < rows, theirs, jnp.where(row == rows, parts, 0.0)).astype(BF16)
    pen = jnp.sum(total[0:1, half:], axis=1, keepdims=True)
    pen_ref[...] = jnp.broadcast_to(pen, pen_ref.shape)


def act_grads(rows, mine_ref, got_ref, own_ref, pen_ref, dec_ref, *outs):
    recon_ref, grad_ref, score_ref, part_ref, *msgs = outs
    tokens, half = grad_ref.shape[0], grad_ref.shape[1] // 2
    low = lax.axis_index("feat") % 2 == 0
    me = lax.axis_index("layer")
    first = jnp.where(low, mine_ref[:tokens, :], got_ref[:tokens, :])
    second = jnp.where(low, got_ref[:tokens, :], mine_ref[:tokens, :])
    grad_ref[:, :half] = first
    grad_ref[:, half:] = second
    extra = got_ref[tokens:, :].astype(F32)
    own = own_ref[...]
    recon_ref[:, :half] = jnp.where(low, own, extra)[:rows].astype(BF16)
    recon_ref[:, half:] = jnp.where(low, extra, own)[:rows].astype(BF16)
    mine_extra = mine_ref[tokens:, :].astype(F32)
    squares = jnp.sum(mine_extra[rows : rows + 1, :LANES], axis=1, keepdims=True)
    squares = squares + jnp.sum(extra[rows : rows + 1, :LANES], axis=1, keepdims=True)
    score = squares + 2.0 * ERROR_SCALE * PENALTY_WEIGHT * pen_ref[0:1, 0:1]
    score_ref[...] = jnp.broadcast_to(score, score_ref.shape)
    grad = grad_ref[...]
    width = dec_ref.shape[1]
    for k in range(len(msgs), -1, -1):
        part = lax.dot_general(grad, dec_ref[me ^ k], NT, preferred_element_type=F32)
        if k:
            msgs[k - 1][:, :width] = part.astype(BF16)
            msgs[k - 1][:, width:] = spread3(score, (tokens, LANES))
        else:
            part_ref[...] = part


def decoder_grads(steps, grad_ref, *refs):
    *acts, out_hbm, buf, sems = refs
    me = lax.axis_index("layer")
    features = acts[0].shape[1]
    block = features // steps
    grad = grad_ref[...]
    copies = []
    for k, acts_ref in enumerate(acts):
        for i in range(steps):
            slot = len(copies) % 2
            if len(copies) >= 2:
                copies[-2].wait()
            span = pl.ds(i * block, block)
            value = lax.dot_general(acts_ref[:, span], grad, TN, preferred_element_type=F32)
            buf[slot] = value.astype(BF16)
            copies.append(pltpu.make_async_copy(buf.at[slot], out_hbm.at[me ^ k, span], sems.at[slot]))
            copies[-1].start()
    for copy in copies[-2:]:
        copy.wait()


def encoder_grad(count, x_ref, part_ref, gate_ref, sparse_ref, score_ref, *refs):
    *msgs, out_ref, loss_ref, pre_ref = refs
    width = part_ref.shape[1]

    @pl.when(pl.program_id(0) == 0)
    def _():
        total = part_ref[...]
        for msg in msgs:
            total = total + msg[:, :width].astype(F32)
        pre = jnp.where(gate_ref[...] > 0, total + sparse_ref[...], 0.0)
        pre_ref[...] = pre.astype(BF16)
        scores = [score_ref[0:1, 0:1]]
        for msg in msgs:
            scores.append(jnp.sum(msg[0:1, width:].astype(F32), axis=1, keepdims=True))
        while len(scores) > 1:
            scores = [scores[i] + scores[i + 1] for i in range(0, len(scores), 2)]
        loss_ref[...] = scores[0] / count

    out_ref[...] = lax.dot_general(x_ref[...], pre_ref[...], TN, preferred_element_type=F32).astype(BF16)


def body(residual_in, enc_weight, thresholds, dec_weight, target):
    layers, feats = lax.axis_size("layer"), lax.axis_size("feat")
    rows, width = residual_in.shape[1:]
    features = enc_weight.shape[2]
    tokens, half = rows * feats, width // 2
    sources = dec_weight.shape[0]
    decoder = dec_weight[:, 0]

    inputs = lax.all_gather(jnp.concatenate([residual_in, target]), "feat", axis=1, tiled=True)
    x, targets = inputs[0], inputs[1]

    acts, gate, sparse, pen = call(
        encode,
        [shape((tokens, features), BF16), shape((tokens, features), F32), shape((tokens, features), F32), shape((8, LANES), F32)],
        (x, in_vmem(enc_weight[0]), thresholds),
        "encode",
        flops=2 * tokens * width * features,
        bytes_accessed=2 * width * features,
    )
    others = [swap(acts, "layer", k) for k in range(1, layers)]
    dec, total = call(
        recon_own,
        [pltpu.VMEM((sources, features, width), BF16), shape((tokens, width), F32)],
        (acts, decoder),
        "recon_own",
        scratch=[pltpu.SemaphoreType.DMA((sources,))],
        in_specs=[WHOLE, ANY],
        flops=2 * tokens * width * features,
        bytes_accessed=2 * sources * width * features,
    )
    dec = in_vmem(dec)
    keep, send = call(
        recon_rest,
        [shape((tokens, half + LANES), F32)] * 2,
        (total, pen, dec, *others),
        "recon_rest",
        flops=2 * tokens * width * features * (sources - 1),
        bytes_accessed=2 * (sources - 1) * width * features,
    )
    (msg,) = call(pair_sum, [shape((tokens, half + LANES), BF16)], (keep, swap(send, "feat", 1)), "pair_sum")
    bit = 2
    while bit < feats:
        pair = (bit, 2 * bit, 3 * bit) if 2 * bit < feats else (bit,)
        msgs = [msg] + [swap(msg, "feat", k) for k in pair]
        bit <<= len(pair) // 2 + 1
        if bit < feats:
            (msg,) = call(group_sum, [shape((tokens, half + LANES), BF16)], msgs, "group_sum")
    mine, own_rows, pen_all = call(
        functools.partial(error_half, rows),
        [shape((tokens + 8, half), BF16), shape((8, half), F32), shape((8, LANES), F32)],
        (targets, *msgs),
        "error_half",
    )
    recon, grad, score, part, *sends = call(
        functools.partial(act_grads, rows),
        [shape((rows, width), BF16), shape((tokens, width), BF16), shape((8, LANES), F32), shape((tokens, features), F32)]
        + [shape((tokens, features + LANES), BF16)] * (layers - 1),
        (mine, swap(mine, "feat", 1), own_rows, pen_all, dec),
        "act_grads",
        flops=2 * tokens * width * features * sources,
        bytes_accessed=2 * sources * width * features,
    )
    gots = [swap(sends[k - 1], "layer", k) for k in range(1, layers)]
    steps = max(1, features // 256)
    (dec_grad,) = call(
        functools.partial(decoder_grads, steps),
        [shape((sources, features, width), BF16)],
        (grad, acts, *others),
        "decoder_grads",
        scratch=[pltpu.VMEM((2, features // steps, width), BF16), pltpu.SemaphoreType.DMA((2,))],
        out_specs=[ANY],
        flops=2 * tokens * width * features * sources,
        bytes_accessed=2 * sources * width * features,
    )
    block = 256
    enc_grad, loss = pl.pallas_call(
        functools.partial(encoder_grad, layers * tokens * width),
        out_shape=[shape((width, features), BF16), shape((1, 1), F32)],
        grid=(width // block,),
        in_specs=[pl.BlockSpec((tokens, block), lambda i: (0, i))] + [WHOLE] * (3 + layers),
        out_specs=[pl.BlockSpec((block, features), lambda i: (i, 0)), pl.BlockSpec((1, 1), lambda i: (0, 0))],
        scratch_shapes=[pltpu.VMEM((tokens, features), BF16)],
        compiler_params=pltpu.CompilerParams(vmem_limit_bytes=16 * MIB),
        cost_estimate=pl.CostEstimate(flops=2 * tokens * width * features, bytes_accessed=2 * width * features, transcendentals=0),
        name="encoder_grad",
    )(x, part, gate, sparse, score, *gots)
    return loss[0, 0], recon[None], dec_grad[:, None], enc_grad[None]


def solution(mesh):
    return jax.shard_map(
        body,
        mesh=mesh,
        in_specs=(
            P("layer", "feat", None),
            P("layer", None, "feat"),
            P("layer", "feat"),
            P(None, "layer", "feat", None),
            P("layer", "feat", None),
        ),
        out_specs=(
            P(),
            P("layer", "feat", None),
            P(None, "layer", "feat", None),
            P("layer", None, "feat"),
        ),
        check_vma=False,
    )
```

time: 194 us -> 85.6 us (0.44)
  blocking collectives: 74.3 us -> 10.8 us
  waiting for transfers between devices: 50.8 us -> 6.26 us
  matrix products: 38.8 us -> 0 us
  Pallas kernels: 0 us -> 30.6 us
  between operations: 17.2 us -> 0.76 us
  local copies, waits for them, and re-layouts: 9.58 us -> 24.4 us
  starting transfers between devices: 0.08 us -> 12.4 us
  other arithmetic: 2.83 us -> 0.07 us
    unnamed x3 -> x0, waiting for transfers between devices: 50.8 us -> none
    psum x1 -> x0, blocking collectives: 39.6 us -> none  [body(): squares_total = lax.psum(squares_local, ('feat', 'layer'))]
    dot_general x5 -> x0, matrix products: 38.8 us -> none  [the longest x1 12.1 us: body(): jnp.einsum('id,sfd->sif', grad_all, decoder, preferred_element_type=jnp.f...]
    pallas_call x0 -> x8, Pallas kernels: none -> 30.6 us  [the longest x7 24.9 us: call(): pl.pallas_call(body, out_shape=outs, in_specs=in_specs or [WHOLE] * len(a...]
    all_gather x3 -> x1, blocking collectives: 34.6 us -> 10.8 us  [body(): lax.all_gather(jnp.concatenate([residual_in, target]), 'feat', axis=1, ti...]
    unnamed x8 -> x16, local copies, waits for them, and re-layouts: 8.04 us -> 24.1 us
    ppermute x0 -> x11, starting transfers between devices: none -> 12.4 us  [swap(): return lax.ppermute(x, axis, [(i, i ^ bits) for i in range(size)])]
    ppermute x0 -> x11, waiting for transfers between devices: none -> 6.26 us  [swap(): return lax.ppermute(x, axis, [(i, i ^ bits) for i in range(size)])]
  transfers between devices with their start and end apart: 2 -> 11, of which waited for: 1 -> 5; matrix products, arithmetic and copies ran while one was open for 6% -> 0% of each run, Pallas kernels for 0% -> 18%
where the time goes in v1:
time: 85.6 us; the launch traced here: 85.3 us
  Pallas kernels  30.6 us (36%)
  local copies, waits for them, and re-layouts  24.4 us (29%)
  starting transfers between devices  12.4 us (14%)
  blocking collectives  10.8 us (13%)
  waiting for transfers between devices  6.26 us (7%)
    pallas_call x7, Pallas kernels, call(): pl.pallas_call(body, out_shape=outs, in_specs=in_specs or [WHOLE] * len(a...  24.9 us
    unnamed x16, local copies, waits for them, and re-layouts  24.1 us
    ppermute x11, starting transfers between devices, swap(): return lax.ppermute(x, axis, [(i, i ^ bits) for i in range(size)])  12.4 us
    all_gather x1, blocking collectives, body(): lax.all_gather(jnp.concatenate([residual_in, target]), 'feat', axis=1, ti...  10.8 us
    ppermute x11, waiting for transfers between devices, swap(): return lax.ppermute(x, axis, [(i, i ^ bits) for i in range(size)])  6.26 us
    pallas_call x1, Pallas kernels, body(): pl.pallas_call(functools.partial(encoder_grad, layers * tokens * width),...  5.69 us
  transfers between devices with their start and end apart: 11, of which 5 were waited for; matrix products, arithmetic and copies ran while one was open for 0% of the time, Pallas kernels for 18%

profile of v1, /device:TPU:0, one launch (start us, length us, event | category | flops | bytes accessed | tf_op | source)
XLA Modules:
  0.0 85.3 jit_solution(8951309703405853589)
XLA Ops:
  0.6 0.7 copy.10
  1.4 0.7 copy.11
  2.2 10.8 %all_gather.3 = bf16[2,24,2304]{2,0,1:T(2,128)(2,1)S(1)} all-gather(bf16[2,3,2304]{2,0,1:T(2,128)(2,1)S(1)} %pad_maximum_fusion), channel_id=1, replica_groups=mesh['feat'=8,'layer'=4] {'feat'}, dimensions={1}, use_global_device_ids=true | all-gather | bytes 248832 | tf_op jit(solution)/shard_map/all_gather | solution.py:237
  13.3 2.3 %copy-done.4 = bf16[1,2304,1024]{2,1,0:T(8,128)(2,1)S(1)} copy-done((bf16[1,2304,1024]{2,1,0:T(8,128)(2,1)S(1)}, bf16[1,2304,1024]{2,1,0:T(8,128)(2,1)}, u32[]{:S(2)}) %copy-start.4) | copy-done | bytes 4718616
  16.3 1.0 %encode.1 = (bf16[24,1024]{1,0:T(8,128)(2,1)S(1)}, f32[24,1024]{1,0:T(8,128)S(1)}, f32[24,1024]{1,0:T(8,128)S(1)}, f32[8,128]{1,0:T(8,128)S(1)}) custom-call(bf16[24,2304]{1,0:T(8,128)(2,1)S(1)} %bitcast.16, bf16[2304,1024]{1,0:T(8,128)(2,1)S(1)} %bitcast.15, s32[1,1024]{1,0:T(1,128)S(1)} %copy-done.5), custom_call_target="tpu_custom_call" | custom-call | flops 113246208 | bytes 4718592 | tf_op jit(solution)/shard_map/encode/pallas_call | solution.py:31
  17.3 3.6 %collective-permute-start.2 = (bf16[24,1024]{1,0:T(8,128)(2,1)S(1)}, bf16[24,1024]{1,0:T(8,128)(2,1)S(1)}, u32[]{:S(2)}, u32[]{:S(2)}) collective-permute-start(bf16[24,1024]{1,0:T(8,128)(2,1)S(1)} %get-tuple-element.24.acts_ref.refs_0_), channel_id=1, source_target_pairs={{0,3},{1,2},{2,1},{3,0},{4,7},{5,6},{6,5},{7,4},{8,11},{9,10},{10,... | collective-permute-start | bytes 147464 | tf_op jit(solution)/shard_map/ppermute | solution.py:45
  21.0 0.8 collective-permute-start
  21.7 6.4 %copy-done.3 = bf16[4,1,1024,2304]{3,2,1,0:T(8,128)(2,1)S(1)} copy-done((bf16[4,1,1024,2304]{3,2,1,0:T(8,128)(2,1)S(1)}, bf16[4,1,1024,2304]{3,2,1,0:T(8,128)(2,1)}, u32[]{:S(2)}) %copy-start.3) | copy-done | bytes 18874392
  28.1 2.2 %recon_own.1 = (bf16[4,1024,2304]{2,1,0:T(8,128)(2,1)S(1)}, f32[24,2304]{1,0:T(8,128)S(1)}) custom-call(bf16[24,1024]{1,0:T(8,128)(2,1)S(1)} %get-tuple-element.24.acts_ref.refs_0_, bf16[4,1024,2304]{2,1,0:T(8,128)(2,1)S(1)} %bitcast.14), custom_call_target="tpu_custom_call" | custom-call | flops 113246208 | bytes 18874368 | tf_op jit(solution)/shard_map/recon_own/pallas_call | solution.py:31
  30.3 6.8 %copy-done = bf16[4,1024,2304]{2,1,0:T(8,128)(2,1)} copy-done((bf16[4,1024,2304]{2,1,0:T(8,128)(2,1)}, bf16[4,1024,2304]{2,1,0:T(8,128)(2,1)S(1)}, u32[]{:S(2)}) %copy-start) | copy-done | bytes 18874392
  37.2 6.4 %copy-done.1 = bf16[4,1024,2304]{2,1,0:T(8,128)(2,1)S(1)} copy-done((bf16[4,1024,2304]{2,1,0:T(8,128)(2,1)S(1)}, bf16[4,1024,2304]{2,1,0:T(8,128)(2,1)}, u32[]{:S(2)}) %copy-start.1) | copy-done | bytes 18874392
  43.6 2.5 %recon_rest.1 = (f32[24,1280]{1,0:T(8,128)S(1)}, f32[24,1280]{1,0:T(8,128)S(1)}) custom-call(f32[24,2304]{1,0:T(8,128)S(1)} %get-tuple-element.25.refs_0_, f32[8,128]{1,0:T(8,128)S(1)} %get-tuple-element.26.refs_1_, bf16[4,1024,2304]{2,1,0:T(8,128)(2,1)S(1)} %copy-done.1, bf16[24,1024]{1,0:T(8,128)(2,1)S(1)} %collective-permute-done.refs_3_.refs_1_, ...), custom_call_target="tpu_custom_call" | custom-call | flops 339738624 | bytes 14155776 | tf_op jit(solution)/shard_map/recon_rest/pallas_call | solution.py:31
  46.1 1.3 %collective-permute-done.3.got_ref = f32[24,1280]{1,0:T(8,128)S(1)} collective-permute-done((f32[24,1280]{1,0:T(8,128)S(1)}, f32[24,1280]{1,0:T(8,128)S(1)}, u32[]{:S(2)}, u32[]{:S(2)}) %collective-permute-start.3) | collective-permute-done | bytes 122912 | tf_op jit(solution)/shard_map/ppermute | solution.py:45
  47.6 1.5 %collective-permute-start.6 = (bf16[24,1280]{1,0:T(8,128)(2,1)S(1)}, bf16[24,1280]{1,0:T(8,128)(2,1)S(1)}, u32[]{:S(2)}, u32[]{:S(2)}) collective-permute-start(bf16[24,1280]{1,0:T(8,128)(2,1)S(1)} %pair_sum.1.refs_0_), channel_id=1, source_target_pairs={{0,24},{4,28},{8,16},{12,20},{16,8},{20,12},{24,0},{28,4},{1,25},{... | collective-permute-start | bytes 184328 | tf_op jit(solution)/shard_map/ppermute | solution.py:45
  49.0 1.5 %collective-permute-start.5 = (bf16[24,1280]{1,0:T(8,128)(2,1)S(1)}, bf16[24,1280]{1,0:T(8,128)(2,1)S(1)}, u32[]{:S(2)}, u32[]{:S(2)}) collective-permute-start(bf16[24,1280]{1,0:T(8,128)(2,1)S(1)} %pair_sum.1.refs_0_), channel_id=1, source_target_pairs={{0,16},{4,20},{8,24},{12,28},{16,0},{20,4},{24,8},{28,12},{1,17},{... | collective-permute-start | bytes 184328 | tf_op jit(solution)/shard_map/ppermute | solution.py:45
  51.1 1.7 %collective-permute-done.6.refs_3_ = bf16[24,1280]{1,0:T(8,128)(2,1)S(1)} collective-permute-done((bf16[24,1280]{1,0:T(8,128)(2,1)S(1)}, bf16[24,1280]{1,0:T(8,128)(2,1)S(1)}, u32[]{:S(2)}, u32[]{:S(2)}) %collective-permute-start.6) | collective-permute-done | bytes 61472 | tf_op jit(solution)/shard_map/ppermute | solution.py:45
  52.8 1.1 %collective-permute-done.5.refs_2_ = bf16[24,1280]{1,0:T(8,128)(2,1)S(1)} collective-permute-done((bf16[24,1280]{1,0:T(8,128)(2,1)S(1)}, bf16[24,1280]{1,0:T(8,128)(2,1)S(1)}, u32[]{:S(2)}, u32[]{:S(2)}) %collective-permute-start.5) | collective-permute-done | bytes 61472 | tf_op jit(solution)/shard_map/ppermute | solution.py:45
  53.8 0.9 %collective-permute-done.4.refs_1_ = bf16[24,1280]{1,0:T(8,128)(2,1)S(1)} collective-permute-done((bf16[24,1280]{1,0:T(8,128)(2,1)S(1)}, bf16[24,1280]{1,0:T(8,128)(2,1)S(1)}, u32[]{:S(2)}, u32[]{:S(2)}) %collective-permute-start.4) | collective-permute-done | bytes 61472 | tf_op jit(solution)/shard_map/ppermute | solution.py:45
  55.0 1.3 %collective-permute-done.7.got_ref = bf16[32,1152]{1,0:T(8,128)(2,1)S(1)} collective-permute-done((bf16[32,1152]{1,0:T(8,128)(2,1)S(1)}, bf16[32,1152]{1,0:T(8,128)(2,1)S(1)}, u32[]{:S(2)}, u32[]{:S(2)}) %collective-permute-start.7) | collective-permute-done | bytes 73760 | tf_op jit(solution)/shard_map/ppermute | solution.py:45
  56.2 6.1 %act_grads.1 = (bf16[3,2304]{1,0:T(4,128)(2,1)}, bf16[24,2304]{1,0:T(8,128)(2,1)S(1)}, f32[8,128]{1,0:T(8,128)S(1)}, f32[24,1024]{1,0:T(8,128)S(1)}, bf16[24,115...) custom-call(bf16[32,1152]{1,0:T(8,128)(2,1)S(1)} %get-tuple-element.30.mine_ref, ...), custom_call_target="tpu_custom_call" | custom-call | flops 452984832 | bytes 18874368 | tf_op jit(solution)/shard_map/act_grads/pallas_call | solution.py:31
  62.3 1.2 %collective-permute-start.8 = (bf16[24,1152]{1,0:T(8,128)(2,1)S(1)}, bf16[24,1152]{1,0:T(8,128)(2,1)S(1)}, u32[]{:S(2)}, u32[]{:S(2)}) collective-permute-start(bf16[24,1152]{1,0:T(8,128)(2,1)S(1)} %get-tuple-element.37), channel_id=1, source_target_pairs={{0,1},{1,0},{2,3},{3,2},{4,5},{5,4},{6,7},{7,6},{8,9},{9,8},{10,11... | collective-permute-start | bytes 165896 | tf_op jit(solution)/shard_map/ppermute | solution.py:45
  63.6 2.9 %collective-permute-start.9 = (bf16[24,1152]{1,0:T(8,128)(2,1)S(1)}, bf16[24,1152]{1,0:T(8,128)(2,1)S(1)}, u32[]{:S(2)}, u32[]{:S(2)}) collective-permute-start(bf16[24,1152]{1,0:T(8,128)(2,1)S(1)} %get-tuple-element.38), channel_id=1, source_target_pairs={{0,2},{1,3},{2,0},{3,1},{4,6},{5,7},{6,4},{7,5},{8,10},{9,11},{10,... | collective-permute-start | bytes 165896 | tf_op jit(solution)/shard_map/ppermute | solution.py:45
  66.7 12.8 %decoder_grads.1 = bf16[4,1024,2304]{2,1,0:T(8,128)(2,1)} custom-call(bf16[24,2304]{1,0:T(8,128)(2,1)S(1)} %get-tuple-element.42.grad_ref, bf16[24,1024]{1,0:T(8,128)(2,1)S(1)} %get-tuple-element.24.acts_ref.refs_0_, bf16[24,1024]{1,0:T(8,128)(2,1)S(1)} %collective-permute-done.refs_3_.refs_1_, bf16[24,1024]{1,0:T(8,128)(2,1)S(1)} %collective-permute-done.1.refs_4_.refs_2_, ...), custom_call_target="tpu_custom_call" | custom-call | flops 452984832 | bytes 18874368 | tf_op jit(solution)/shard_map/decoder_grads/pallas_call | solution.py:31
  79.6 5.7 %encoder_grad.1 = (bf16[2304,1024]{1,0:T(8,128)(2,1)}, f32[1,1]{1,0:T(1,128)}) custom-call(bf16[24,2304]{1,0:T(8,128)(2,1)S(1)} %bitcast.17, f32[24,1024]{1,0:T(8,128)S(1)} %get-tuple-element.33.part_ref, f32[24,1024]{1,0:T(8,128)S(1)} %get-tuple-element.34.gate_ref, f32[24,1024]{1,0:T(8,128)S(1)} %get-tuple-element.35.sparse_ref, ...), custom_call_target="tpu_custom_call" | custom-call | flops 113246208 | bytes 4718592 | tf_op jit(solution)/shard_map/encoder_grad/pallas_call | solution.py:304
  (25 shorter events, 2.3 us)
Async XLA Ops:
  13.3 2.3 %copy-start.4 = (bf16[1,2304,1024]{2,1,0:T(8,128)(2,1)S(1)}, bf16[1,2304,1024]{2,1,0:T(8,128)(2,1)}, u32[]{:S(2)}) copy-start(bf16[1,2304,1024]{2,1,0:T(8,128)(2,1)} %param.6) | copy-start | bytes 14155780
  15.6 0.7 copy-start.5
  17.3 19.8 %collective-permute-start.2 = (bf16[24,1024]{1,0:T(8,128)(2,1)S(1)}, bf16[24,1024]{1,0:T(8,128)(2,1)S(1)}, u32[]{:S(2)}, u32[]{:S(2)}) collective-permute-start(bf16[24,1024]{1,0:T(8,128)(2,1)S(1)} %get-tuple-element.24.acts_ref.refs_0_), channel_id=1, source_target_pairs={{0,3},{1,2},{2,1},{3,0},{4,7},{5,6},{6,5},{7,4},{8,11},{9,10},{10,... | collective-permute-start | bytes 147464 | tf_op jit(solution)/shard_map/ppermute | solution.py:45
  21.0 16.2 %collective-permute-start.1 = (bf16[24,1024]{1,0:T(8,128)(2,1)S(1)}, bf16[24,1024]{1,0:T(8,128)(2,1)S(1)}, u32[]{:S(2)}, u32[]{:S(2)}) collective-permute-start(bf16[24,1024]{1,0:T(8,128)(2,1)S(1)} %get-tuple-element.24.acts_ref.refs_0_), channel_id=1, source_target_pairs={{0,2},{1,3},{2,0},{3,1},{4,6},{5,7},{6,4},{7,5},{8,10},{9,11},{10,... | collective-permute-start | bytes 147464 | tf_op jit(solution)/shard_map/ppermute | solution.py:45
  21.0 16.2 %collective-permute-start = (bf16[24,1024]{1,0:T(8,128)(2,1)S(1)}, bf16[24,1024]{1,0:T(8,128)(2,1)S(1)}, u32[]{:S(2)}, u32[]{:S(2)}) collective-permute-start(bf16[24,1024]{1,0:T(8,128)(2,1)S(1)} %get-tuple-element.24.acts_ref.refs_0_), channel_id=1, source_target_pairs={{0,1},{1,0},{2,3},{3,2},{4,5},{5,4},{6,7},{7,6},{8,9},{9,8},{10,11... | collective-permute-start | bytes 147464 | tf_op jit(solution)/shard_map/ppermute | solution.py:45
  21.7 6.4 %copy-start.3 = (bf16[4,1,1024,2304]{3,2,1,0:T(8,128)(2,1)S(1)}, bf16[4,1,1024,2304]{3,2,1,0:T(8,128)(2,1)}, u32[]{:S(2)}) copy-start(bf16[4,1,1024,2304]{3,2,1,0:T(8,128)(2,1)} %param.8) | copy-start | bytes 56623108
  30.3 6.9 %copy-start = (bf16[4,1024,2304]{2,1,0:T(8,128)(2,1)}, bf16[4,1024,2304]{2,1,0:T(8,128)(2,1)S(1)}, u32[]{:S(2)}) copy-start(bf16[4,1024,2304]{2,1,0:T(8,128)(2,1)S(1)} %get-tuple-element.27.refs_2_.dec_ref) | copy-start | bytes 56623108
  37.2 6.4 %copy-start.1 = (bf16[4,1024,2304]{2,1,0:T(8,128)(2,1)S(1)}, bf16[4,1024,2304]{2,1,0:T(8,128)(2,1)}, u32[]{:S(2)}) copy-start(bf16[4,1024,2304]{2,1,0:T(8,128)(2,1)} %copy-done) | copy-start | bytes 56623108
  43.6 12.7 %copy-start.2 = (bf16[4,1024,2304]{2,1,0:T(8,128)(2,1)S(1)}, bf16[4,1024,2304]{2,1,0:T(8,128)(2,1)}, u32[]{:S(2)}) copy-start(bf16[4,1024,2304]{2,1,0:T(8,128)(2,1)} %copy-done) | copy-start | bytes 56623108
  46.1 1.4 %collective-permute-start.3 = (f32[24,1280]{1,0:T(8,128)S(1)}, f32[24,1280]{1,0:T(8,128)S(1)}, u32[]{:S(2)}, u32[]{:S(2)}) collective-permute-start(f32[24,1280]{1,0:T(8,128)S(1)} %get-tuple-element.29), channel_id=1, source_target_pairs={{0,4},{4,0},{8,12},{12,8},{16,20},{20,16},{24,28},{28,24},{1,5},{5... | collective-permute-start | bytes 368648 | tf_op jit(solution)/shard_map/ppermute | solution.py:45
  47.6 5.2 %collective-permute-start.6 = (bf16[24,1280]{1,0:T(8,128)(2,1)S(1)}, bf16[24,1280]{1,0:T(8,128)(2,1)S(1)}, u32[]{:S(2)}, u32[]{:S(2)}) collective-permute-start(bf16[24,1280]{1,0:T(8,128)(2,1)S(1)} %pair_sum.1.refs_0_), channel_id=1, source_target_pairs={{0,24},{4,28},{8,16},{12,20},{16,8},{20,12},{24,0},{28,4},{1,25},{... | collective-permute-start | bytes 184328 | tf_op jit(solution)/shard_map/ppermute | solution.py:45
  49.0 4.8 %collective-permute-start.5 = (bf16[24,1280]{1,0:T(8,128)(2,1)S(1)}, bf16[24,1280]{1,0:T(8,128)(2,1)S(1)}, u32[]{:S(2)}, u32[]{:S(2)}) collective-permute-start(bf16[24,1280]{1,0:T(8,128)(2,1)S(1)} %pair_sum.1.refs_0_), channel_id=1, source_target_pairs={{0,16},{4,20},{8,24},{12,28},{16,0},{20,4},{24,8},{28,12},{1,17},{... | collective-permute-start | bytes 184328 | tf_op jit(solution)/shard_map/ppermute | solution.py:45
  50.5 4.2 %collective-permute-start.4 = (bf16[24,1280]{1,0:T(8,128)(2,1)S(1)}, bf16[24,1280]{1,0:T(8,128)(2,1)S(1)}, u32[]{:S(2)}, u32[]{:S(2)}) collective-permute-start(bf16[24,1280]{1,0:T(8,128)(2,1)S(1)} %pair_sum.1.refs_0_), channel_id=1, source_target_pairs={{0,8},{4,12},{8,0},{12,4},{16,24},{20,28},{24,16},{28,20},{1,9},{5... | collective-permute-start | bytes 184328 | tf_op jit(solution)/shard_map/ppermute | solution.py:45
  54.9 1.3 %collective-permute-start.7 = (bf16[32,1152]{1,0:T(8,128)(2,1)S(1)}, bf16[32,1152]{1,0:T(8,128)(2,1)S(1)}, u32[]{:S(2)}, u32[]{:S(2)}) collective-permute-start(bf16[32,1152]{1,0:T(8,128)(2,1)S(1)} %get-tuple-element.30.mine_ref), channel_id=1, source_target_pairs={{0,4},{4,0},{8,12},{12,8},{16,20},{20,16},{24,28},{28,24},{1,5},{5... | collective-permute-start | bytes 221192 | tf_op jit(solution)/shard_map/ppermute | solution.py:45
  62.3 17.2 %collective-permute-start.8 = (bf16[24,1152]{1,0:T(8,128)(2,1)S(1)}, bf16[24,1152]{1,0:T(8,128)(2,1)S(1)}, u32[]{:S(2)}, u32[]{:S(2)}) collective-permute-start(bf16[24,1152]{1,0:T(8,128)(2,1)S(1)} %get-tuple-element.37), channel_id=1, source_target_pairs={{0,1},{1,0},{2,3},{3,2},{4,5},{5,4},{6,7},{7,6},{8,9},{9,8},{10,11... | collective-permute-start | bytes 165896 | tf_op jit(solution)/shard_map/ppermute | solution.py:45
  63.6 16.0 %collective-permute-start.9 = (bf16[24,1152]{1,0:T(8,128)(2,1)S(1)}, bf16[24,1152]{1,0:T(8,128)(2,1)S(1)}, u32[]{:S(2)}, u32[]{:S(2)}) collective-permute-start(bf16[24,1152]{1,0:T(8,128)(2,1)S(1)} %get-tuple-element.38), channel_id=1, source_target_pairs={{0,2},{1,3},{2,0},{3,1},{4,6},{5,7},{6,4},{7,5},{8,10},{9,11},{10,... | collective-permute-start | bytes 165896 | tf_op jit(solution)/shard_map/ppermute | solution.py:45
  66.5 13.1 %collective-permute-start.10 = (bf16[24,1152]{1,0:T(8,128)(2,1)S(1)}, bf16[24,1152]{1,0:T(8,128)(2,1)S(1)}, u32[]{:S(2)}, u32[]{:S(2)}) collective-permute-start(bf16[24,1152]{1,0:T(8,128)(2,1)S(1)} %get-tuple-element.39), channel_id=1, source_target_pairs={{0,3},{1,2},{2,1},{3,0},{4,7},{5,6},{6,5},{7,4},{8,11},{9,10},{10,... | collective-permute-start | bytes 165896 | tf_op jit(solution)/shard_map/ppermute | solution.py:45

commit v2 on v1

--- a/solution.py
+++ b/solution.py
@@ -19,8 +19,8 @@
 TN = (((0,), (0,)), ((), ()))
 
 
-def in_vmem(x):
-    return pltpu.with_memory_space_constraint(x, pltpu.VMEM)
+def in_hbm(x):
+    return pltpu.with_memory_space_constraint(x, pltpu.HBM)
 
 
 def shape(dims, dtype):
@@ -60,11 +60,50 @@
     return block.astype(BF16)
 
 
-def encode(x_ref, enc_ref, thr_ref, acts_ref, gate_ref, sparse_ref, pen_ref):
+def pack(res_hbm, target_hbm, thr_hbm, out_ref, cutoff_ref, res_ref, target_ref, thr_ref, sems):
+    copies = [
+        pltpu.make_async_copy(res_hbm, res_ref, sems.at[0]),
+        pltpu.make_async_copy(target_hbm, target_ref, sems.at[1]),
+        pltpu.make_async_copy(thr_hbm, thr_ref, sems.at[2]),
+    ]
+    for copy in copies:
+        copy.start()
+    for copy in copies:
+        copy.wait()
+    rows = res_ref.shape[0]
+    out_ref[...] = jnp.zeros_like(out_ref)
+    out_ref[:rows] = res_ref[...]
+    out_ref[rows : 2 * rows] = target_ref[...]
+    cutoff_ref[...] = (thr_ref[...].astype(F32) + 0.5) / 2048.0
+
+
+def stack(*refs):
+    out_ref = refs[-1]
+    height = refs[0].shape[0]
+    for i, ref in enumerate(refs[:-1]):
+        out_ref[i * height : (i + 1) * height] = ref[...]
+
+
+def gather_rows(rows, height, tokens, first, blocks):
+    dims = (tokens, blocks.shape[0])
+    token = lax.broadcasted_iota(jnp.int32, dims, 0)
+    place = lax.broadcasted_iota(jnp.int32, dims, 1)
+    row = place % height - first
+    device = (place // height) ^ lax.axis_index("feat")
+    chosen = (row >= 0) & (row < rows) & (device * rows + row == token)
+    picked = jnp.dot(jnp.where(chosen, 1.0, 0.0).astype(BF16), blocks, preferred_element_type=F32)
+    return picked.astype(BF16)
+
+
+def encode(rows, height, *refs):
+    *block_refs, enc_ref, cutoff_ref, x_ref, target_ref, acts_ref, gate_ref, sparse_ref, pen_ref = refs
     tokens = x_ref.shape[0]
-    cutoff = (thr_ref[...].astype(F32) + 0.5) / 2048.0
-    preact = jnp.dot(x_ref[...], enc_ref[...], preferred_element_type=F32)
-    firing = preact > cutoff
+    blocks = jnp.concatenate([ref[...] for ref in block_refs], axis=0)
+    x = gather_rows(rows, height, tokens, 0, blocks)
+    x_ref[...] = x
+    target_ref[...] = gather_rows(rows, height, tokens, rows, blocks)
+    preact = jnp.dot(x, enc_ref[...], preferred_element_type=F32)
+    firing = preact > cutoff_ref[...]
     acts = jnp.where(firing, preact, 0.0).astype(BF16)
     acts_ref[...] = acts
     wide = acts.astype(F32)
@@ -76,17 +115,19 @@
     pen_ref[...] = jnp.broadcast_to(pen, pen_ref.shape)
 
 
-def recon_own(acts_ref, dec_hbm, dec_ref, total_ref, sems):
-    sources = dec_hbm.shape[0]
+def recon_own(acts_ref, dec_hbm, total_ref, buf, sems):
     me = lax.axis_index("layer")
+    pieces = buf.shape[0]
+    block = buf.shape[1]
     copies = []
-    for k in range(sources):
-        copies.append(pltpu.make_async_copy(dec_hbm.at[me ^ k], dec_ref.at[me ^ k], sems.at[k]))
+    for i in range(pieces):
+        copies.append(pltpu.make_async_copy(dec_hbm.at[me, pl.ds(i * block, block)], buf.at[i], sems.at[i]))
         copies[-1].start()
-    copies[0].wait()
-    total_ref[...] = jnp.dot(acts_ref[...], dec_ref[me], preferred_element_type=F32)
-    for k in range(1, sources):
-        copies[k].wait()
+    total = jnp.zeros(total_ref.shape, F32)
+    for i in range(pieces):
+        copies[i].wait()
+        total = total + jnp.dot(acts_ref[:, i * block : (i + 1) * block], buf[i], preferred_element_type=F32)
+    total_ref[...] = total
 
 
 def recon_rest(*refs):
@@ -176,7 +217,7 @@
     grad = grad_ref[...]
     width = dec_ref.shape[1]
     for k in range(len(msgs), -1, -1):
-        part = lax.dot_general(grad, dec_ref[me ^ k], NT, preferred_element_type=F32)
+        part = lax.dot_general(dec_ref[me ^ k], grad, NT, preferred_element_type=F32).T
         if k:
             msgs[k - 1][:, :width] = part.astype(BF16)
             msgs[k - 1][:, width:] = spread3(score, (tokens, LANES))
@@ -184,46 +225,47 @@
             part_ref[...] = part
 
 
-def decoder_grads(steps, grad_ref, *refs):
+def decoder_grads(grad_ref, *refs):
     *acts, out_hbm, buf, sems = refs
     me = lax.axis_index("layer")
-    features = acts[0].shape[1]
-    block = features // steps
-    grad = grad_ref[...]
+    block = buf.shape[1]
+    steps = acts[0].shape[1] // block
     copies = []
     for k, acts_ref in enumerate(acts):
+        turned = acts_ref[...].T
         for i in range(steps):
-            slot = len(copies) % 2
-            if len(copies) >= 2:
-                copies[-2].wait()
-            span = pl.ds(i * block, block)
-            value = lax.dot_general(acts_ref[:, span], grad, TN, preferred_element_type=F32)
-            buf[slot] = value.astype(BF16)
-            copies.append(pltpu.make_async_copy(buf.at[slot], out_hbm.at[me ^ k, span], sems.at[slot]))
+            n = len(copies)
+            span = slice(i * block, (i + 1) * block)
+            buf[n] = jnp.dot(turned[span], grad_ref[...], preferred_element_type=F32).astype(BF16)
+            copies.append(pltpu.make_async_copy(buf.at[n], out_hbm.at[me ^ k, pl.ds(i * block, block)], sems.at[n]))
             copies[-1].start()
-    for copy in copies[-2:]:
+    for copy in copies:
         copy.wait()
 
 
 def encoder_grad(count, x_ref, part_ref, gate_ref, sparse_ref, score_ref, *refs):
-    *msgs, out_ref, loss_ref, pre_ref = refs
+    *msgs, out_hbm, loss_ref, buf, sems = refs
     width = part_ref.shape[1]
-
-    @pl.when(pl.program_id(0) == 0)
-    def _():
-        total = part_ref[...]
-        for msg in msgs:
-            total = total + msg[:, :width].astype(F32)
-        pre = jnp.where(gate_ref[...] > 0, total + sparse_ref[...], 0.0)
-        pre_ref[...] = pre.astype(BF16)
-        scores = [score_ref[0:1, 0:1]]
-        for msg in msgs:
-            scores.append(jnp.sum(msg[0:1, width:].astype(F32), axis=1, keepdims=True))
-        while len(scores) > 1:
-            scores = [scores[i] + scores[i + 1] for i in range(0, len(scores), 2)]
-        loss_ref[...] = scores[0] / count
-
-    out_ref[...] = lax.dot_general(x_ref[...], pre_ref[...], TN, preferred_element_type=F32).astype(BF16)
+    total = part_ref[...]
+    for msg in msgs:
+        total = total + msg[:, :width].astype(F32)
+    pre = jnp.where(gate_ref[...] > 0, total + sparse_ref[...], 0.0).astype(BF16)
+    turned = x_ref[...].T
+    block = buf.shape[1]
+    copies = []
+    for i in range(buf.shape[0]):
+        span = slice(i * block, (i + 1) * block)
+        buf[i] = jnp.dot(turned[span], pre, preferred_element_type=F32).astype(BF16)
+        copies.append(pltpu.make_async_copy(buf.at[i], out_hbm.at[pl.ds(i * block, block)], sems.at[i]))
+        copies[-1].start()
+    scores = [score_ref[0:1, 0:1]]
+    for msg in msgs:
+        scores.append(jnp.sum(msg[0:1, width:].astype(F32), axis=1, keepdims=True))
+    while len(scores) > 1:
+        scores = [scores[i] + scores[i + 1] for i in range(0, len(scores), 2)]
+    loss_ref[...] = scores[0] / count
+    for copy in copies:
+        copy.wait()
 
 
 def body(residual_in, enc_weight, thresholds, dec_weight, target):
@@ -234,33 +276,48 @@
     sources = dec_weight.shape[0]
     decoder = dec_weight[:, 0]
 
-    inputs = lax.all_gather(jnp.concatenate([residual_in, target]), "feat", axis=1, tiled=True)
-    x, targets = inputs[0], inputs[1]
-
-    acts, gate, sparse, pen = call(
-        encode,
-        [shape((tokens, features), BF16), shape((tokens, features), F32), shape((tokens, features), F32), shape((8, LANES), F32)],
-        (x, in_vmem(enc_weight[0]), thresholds),
+    height = -(-2 * rows // 8) * 8
+    block, cutoff = call(
+        pack,
+        [shape((height, width), BF16), shape((1, features), F32)],
+        (in_hbm(residual_in[0]), in_hbm(target[0]), in_hbm(thresholds)),
+        "pack",
+        scratch=[pltpu.VMEM((rows, width), BF16)] * 2 + [pltpu.VMEM((1, features), jnp.int32), pltpu.SemaphoreType.DMA((3,))],
+        in_specs=[ANY] * 3,
+        bytes_accessed=0,
+    )
+    blocks, bit = [block, swap(block, "feat", 1)], 2
+    while bit < feats:
+        (block,) = call(stack, [shape((bit * height, width), BF16)], blocks, "stack")
+        pair = (bit, 2 * bit, 3 * bit) if 2 * bit < feats else (bit,)
+        blocks = [block] + [swap(block, "feat", k) for k in pair]
+        bit <<= len(pair) // 2 + 1
+    x, targets, acts, gate, sparse, pen = call(
+        functools.partial(encode, rows, height),
+        [shape((tokens, width), BF16)] * 2
+        + [shape((tokens, features), BF16), shape((tokens, features), F32), shape((tokens, features), F32), shape((8, LANES), F32)],
+        (*blocks, enc_weight[0], cutoff),
         "encode",
         flops=2 * tokens * width * features,
         bytes_accessed=2 * width * features,
     )
     others = [swap(acts, "layer", k) for k in range(1, layers)]
-    dec, total = call(
+    pieces = max(1, features // 256)
+    (total,) = call(
         recon_own,
-        [pltpu.VMEM((sources, features, width), BF16), shape((tokens, width), F32)],
-        (acts, decoder),
+        [shape((tokens, width), F32)],
+        (acts, in_hbm(decoder)),
         "recon_own",
-        scratch=[pltpu.SemaphoreType.DMA((sources,))],
+        scratch=[pltpu.VMEM((pieces, features // pieces, width), BF16), pltpu.SemaphoreType.DMA((pieces,))],
         in_specs=[WHOLE, ANY],
+        limit=12,
         flops=2 * tokens * width * features,
-        bytes_accessed=2 * sources * width * features,
-    )
-    dec = in_vmem(dec)
+        bytes_accessed=2 * width * features,
+    )
     keep, send = call(
         recon_rest,
         [shape((tokens, half + LANES), F32)] * 2,
-        (total, pen, dec, *others),
+        (total, pen, decoder, *others),
         "recon_rest",
         flops=2 * tokens * width * features * (sources - 1),
         bytes_accessed=2 * (sources - 1) * width * features,
@@ -283,7 +340,7 @@
         functools.partial(act_grads, rows),
         [shape((rows, width), BF16), shape((tokens, width), BF16), shape((8, LANES), F32), shape((tokens, features), F32)]
         + [shape((tokens, features + LANES), BF16)] * (layers - 1),
-        (mine, swap(mine, "feat", 1), own_rows, pen_all, dec),
+        (mine, swap(mine, "feat", 1), own_rows, pen_all, decoder),
         "act_grads",
         flops=2 * tokens * width * features * sources,
         bytes_accessed=2 * sources * width * features,
@@ -291,27 +348,27 @@
     gots = [swap(sends[k - 1], "layer", k) for k in range(1, layers)]
     steps = max(1, features // 256)
     (dec_grad,) = call(
-        functools.partial(decoder_grads, steps),
+        decoder_grads,
         [shape((sources, features, width), BF16)],
         (grad, acts, *others),
         "decoder_grads",
-        scratch=[pltpu.VMEM((2, features // steps, width), BF16), pltpu.SemaphoreType.DMA((2,))],
+        scratch=[pltpu.VMEM((sources * steps, features // steps, width), BF16), pltpu.SemaphoreType.DMA((sources * steps,))],
+        limit=24,
         out_specs=[ANY],
         flops=2 * tokens * width * features * sources,
         bytes_accessed=2 * sources * width * features,
     )
     block = 256
-    enc_grad, loss = pl.pallas_call(
+    enc_grad, loss = call(
         functools.partial(encoder_grad, layers * tokens * width),
-        out_shape=[shape((width, features), BF16), shape((1, 1), F32)],
-        grid=(width // block,),
-        in_specs=[pl.BlockSpec((tokens, block), lambda i: (0, i))] + [WHOLE] * (3 + layers),
-        out_specs=[pl.BlockSpec((block, features), lambda i: (i, 0)), pl.BlockSpec((1, 1), lambda i: (0, 0))],
-        scratch_shapes=[pltpu.VMEM((tokens, features), BF16)],
-        compiler_params=pltpu.CompilerParams(vmem_limit_bytes=16 * MIB),
-        cost_estimate=pl.CostEstimate(flops=2 * tokens * width * features, bytes_accessed=2 * width * features, transcendentals=0),
-        name="encoder_grad",
-    )(x, part, gate, sparse, score, *gots)
+        [shape((width, features), BF16), shape((1, 1), F32)],
+        (x, part, gate, sparse, score, *gots),
+        "encoder_grad",
+        scratch=[pltpu.VMEM((width // block, block, features), BF16), pltpu.SemaphoreType.DMA((width // block,))],
+        out_specs=[ANY, WHOLE],
+        flops=2 * tokens * width * features,
+        bytes_accessed=2 * width * features,
+    )
     return loss[0, 0], recon[None], dec_grad[:, None], enc_grad[None]
 
 

time: 85.6 us -> 56.4 us (0.66)
  local copies, waits for them, and re-layouts: 24.4 us -> 2.34 us
  blocking collectives: 10.8 us -> 0 us
  Pallas kernels: 30.6 us -> 23.4 us
  waiting for transfers between devices: 6.26 us -> 12.4 us
  starting transfers between devices: 12.4 us -> 17.3 us
    unnamed x16 -> x4, local copies, waits for them, and re-layouts: 24.1 us -> 2.34 us
    all_gather x1 -> x0, blocking collectives: 10.8 us -> none  [body(): lax.all_gather(jnp.concatenate([residual_in, target]), 'feat', axis=1, ti...]
    ppermute x11 -> x15, waiting for transfers between devices: 6.26 us -> 12.4 us  [swap(): return lax.ppermute(x, axis, [(i, i ^ bits) for i in range(size)])]
    pallas_call x1 -> x0, Pallas kernels: 5.69 us -> none  [body(): pl.pallas_call(functools.partial(encoder_grad, layers * tokens * width),...]
    ppermute x11 -> x15, starting transfers between devices: 12.4 us -> 17.3 us  [swap(): return lax.ppermute(x, axis, [(i, i ^ bits) for i in range(size)])]
    pallas_call x7 -> x10, Pallas kernels: 24.9 us -> 23.4 us  [call(): pl.pallas_call(body, out_shape=outs, in_specs=in_specs or [WHOLE] * len(a...]
  transfers between devices with their start and end apart: 11 -> 15, of which waited for: 5 -> 10; matrix products, arithmetic and copies ran while one was open for 0% -> 0% of each run, Pallas kernels for 18% -> 17%
where the time goes in v2:
time: 56.4 us; the launch traced here: 56.2 us
  Pallas kernels  23.4 us (41%)
  starting transfers between devices  17.3 us (31%)
  waiting for transfers between devices  12.4 us (22%)
  local copies, waits for them, and re-layouts  2.34 us (4%)
  between operations  0.73 us (1%)
    pallas_call x10, Pallas kernels, call(): pl.pallas_call(body, out_shape=outs, in_specs=in_specs or [WHOLE] * len(a...  23.4 us
    ppermute x15, starting transfers between devices, swap(): return lax.ppermute(x, axis, [(i, i ^ bits) for i in range(size)])  17.3 us
    ppermute x15, waiting for transfers between devices, swap(): return lax.ppermute(x, axis, [(i, i ^ bits) for i in range(size)])  12.4 us
    unnamed x4, local copies, waits for them, and re-layouts  2.34 us
  transfers between devices with their start and end apart: 15, of which 10 were waited for; matrix products, arithmetic and copies ran while one was open for 0% of the time, Pallas kernels for 17%

profile of v2, /device:TPU:0, one launch (start us, length us, event | category | flops | bytes accessed | tf_op | source)
XLA Modules:
  0.0 56.2 jit_solution(3658914797432817292)
XLA Ops:
  0.6 0.9 %pack.1 = (bf16[8,2304]{1,0:T(8,128)(2,1)S(1)}, f32[1,1024]{1,0:T(1,128)S(1)}) custom-call(bf16[3,2304]{1,0:T(4,128)(2,1)} %bitcast.15, bf16[3,2304]{1,0:T(4,128)(2,1)} %bitcast.16, s32[1,1024]{1,0:T(1,128)} %thr_hbm.1), custom_call_target="tpu_custom_call" | custom-call | tf_op jit(solution)/shard_map/pack/pallas_call | solution.py:31
  2.1 0.9 %collective-permute-done.refs_1_ = bf16[8,2304]{1,0:T(8,128)(2,1)S(1)} collective-permute-done((bf16[8,2304]{1,0:T(8,128)(2,1)S(1)}, bf16[8,2304]{1,0:T(8,128)(2,1)S(1)}, u32[]{:S(2)}, u32[]{:S(2)}) %collective-permute-start) | collective-permute-done | bytes 36896 | tf_op jit(solution)/shard_map/ppermute | solution.py:45
  3.0 3.8 %collective-permute-start.3 = (bf16[16,2304]{1,0:T(8,128)(2,1)S(1)}, bf16[16,2304]{1,0:T(8,128)(2,1)S(1)}, u32[]{:S(2)}, u32[]{:S(2)}) collective-permute-start(bf16[16,2304]{1,0:T(8,128)(2,1)S(1)} %stack.1.refs_0_), channel_id=1, source_target_pairs={{0,24},{4,28},{8,16},{12,20},{16,8},{20,12},{24,0},{28,4},{1,25},{... | collective-permute-start | bytes 221192 | tf_op jit(solution)/shard_map/ppermute | solution.py:45
  7.4 2.0 %collective-permute-done.3.refs_3_ = bf16[16,2304]{1,0:T(8,128)(2,1)S(1)} collective-permute-done((bf16[16,2304]{1,0:T(8,128)(2,1)S(1)}, bf16[16,2304]{1,0:T(8,128)(2,1)S(1)}, u32[]{:S(2)}, u32[]{:S(2)}) %collective-permute-start.3) | collective-permute-done | bytes 73760 | tf_op jit(solution)/shard_map/ppermute | solution.py:45
  9.4 1.7 %collective-permute-done.2.refs_2_ = bf16[16,2304]{1,0:T(8,128)(2,1)S(1)} collective-permute-done((bf16[16,2304]{1,0:T(8,128)(2,1)S(1)}, bf16[16,2304]{1,0:T(8,128)(2,1)S(1)}, u32[]{:S(2)}, u32[]{:S(2)}) %collective-permute-start.2) | collective-permute-done | bytes 73760 | tf_op jit(solution)/shard_map/ppermute | solution.py:45
  11.6 2.3 %copy-done.1 = bf16[1,2304,1024]{2,1,0:T(8,128)(2,1)S(1)} copy-done((bf16[1,2304,1024]{2,1,0:T(8,128)(2,1)S(1)}, bf16[1,2304,1024]{2,1,0:T(8,128)(2,1)}, u32[]{:S(2)}) %copy-start.1) | copy-done | bytes 4718616
  14.0 1.1 %encode.1 = (bf16[24,2304]{1,0:T(8,128)(2,1)S(1)}, bf16[24,2304]{1,0:T(8,128)(2,1)S(1)}, bf16[24,1024]{1,0:T(8,128)(2,1)S(1)}, f32[24,1024]{1,0:T(8,128)S(1)}, f...) custom-call(bf16[16,2304]{1,0:T(8,128)(2,1)S(1)} %stack.1.refs_0_, bf16[16,2304]{1,0:T(8,128)(2,1)S(1)} %collective-permute-done.1.refs_1_, ...), custom_call_target="tpu_custom_call" | custom-call | flops 113246208 | bytes 4718592 | tf_op jit(solution)/shard_map/encode/pallas_call | solution.py:31
  15.1 3.6 %collective-permute-start.6 = (bf16[24,1024]{1,0:T(8,128)(2,1)S(1)}, bf16[24,1024]{1,0:T(8,128)(2,1)S(1)}, u32[]{:S(2)}, u32[]{:S(2)}) collective-permute-start(bf16[24,1024]{1,0:T(8,128)(2,1)S(1)} %get-tuple-element.30.acts_ref.refs_0_), channel_id=1, source_target_pairs={{0,3},{1,2},{2,1},{3,0},{4,7},{5,6},{6,5},{7,4},{8,11},{9,10},{10,... | collective-permute-start | bytes 147464 | tf_op jit(solution)/shard_map/ppermute | solution.py:45
  18.7 0.8 %collective-permute-start.4 = (bf16[24,1024]{1,0:T(8,128)(2,1)S(1)}, bf16[24,1024]{1,0:T(8,128)(2,1)S(1)}, u32[]{:S(2)}, u32[]{:S(2)}) collective-permute-start(bf16[24,1024]{1,0:T(8,128)(2,1)S(1)} %get-tuple-element.30.acts_ref.refs_0_), channel_id=1, source_target_pairs={{0,1},{1,0},{2,3},{3,2},{4,5},{5,4},{6,7},{7,6},{8,9},{9,8},{10,11... | collective-permute-start | bytes 147464 | tf_op jit(solution)/shard_map/ppermute | solution.py:45
  19.5 2.7 %recon_own.1.refs_0_ = f32[24,2304]{1,0:T(8,128)S(1)} custom-call(bf16[24,1024]{1,0:T(8,128)(2,1)S(1)} %get-tuple-element.30.acts_ref.refs_0_, bf16[4,1024,2304]{2,1,0:T(8,128)(2,1)} %bitcast.10), custom_call_target="tpu_custom_call" | custom-call | flops 113246208 | bytes 4718592 | tf_op jit(solution)/shard_map/recon_own/pallas_call | solution.py:31
  22.2 1.5 %collective-permute-done.5.refs_4_.refs_2_ = bf16[24,1024]{1,0:T(8,128)(2,1)S(1)} collective-permute-done((bf16[24,1024]{1,0:T(8,128)(2,1)S(1)}, bf16[24,1024]{1,0:T(8,128)(2,1)S(1)}, u32[]{:S(2)}, u32[]{:S(2)}) %collective-permute-start.5) | collective-permute-done | bytes 49184 | tf_op jit(solution)/shard_map/ppermute | solution.py:45
  23.7 2.5 %recon_rest.1 = (f32[24,1280]{1,0:T(8,128)S(1)}, f32[24,1280]{1,0:T(8,128)S(1)}) custom-call(f32[24,2304]{1,0:T(8,128)S(1)} %recon_own.1.refs_0_, f32[8,128]{1,0:T(8,128)S(1)} %get-tuple-element.31.refs_1_, bf16[4,1024,2304]{2,1,0:T(8,128)(2,1)S(1)} %bitcast.11, bf16[24,1024]{1,0:T(8,128)(2,1)S(1)} %collective-permute-done.4.refs_3_.refs_1_, ...), custom_call_target="tpu_custom_call" | custom-call | flops 339738624 | bytes 14155776 | tf_op jit(solution)/shard_map/recon_rest/pallas_call | solution.py:31
  26.3 1.3 %collective-permute-done.7.got_ref = f32[24,1280]{1,0:T(8,128)S(1)} collective-permute-done((f32[24,1280]{1,0:T(8,128)S(1)}, f32[24,1280]{1,0:T(8,128)S(1)}, u32[]{:S(2)}, u32[]{:S(2)}) %collective-permute-start.7) | collective-permute-done | bytes 122912 | tf_op jit(solution)/shard_map/ppermute | solution.py:45
  27.7 1.5 %collective-permute-start.10 = (bf16[24,1280]{1,0:T(8,128)(2,1)S(1)}, bf16[24,1280]{1,0:T(8,128)(2,1)S(1)}, u32[]{:S(2)}, u32[]{:S(2)}) collective-permute-start(bf16[24,1280]{1,0:T(8,128)(2,1)S(1)} %pair_sum.1.refs_0_), channel_id=1, source_target_pairs={{0,24},{4,28},{8,16},{12,20},{16,8},{20,12},{24,0},{28,4},{1,25},{... | collective-permute-start | bytes 184328 | tf_op jit(solution)/shard_map/ppermute | solution.py:45
  29.2 1.0 %collective-permute-start.9 = (bf16[24,1280]{1,0:T(8,128)(2,1)S(1)}, bf16[24,1280]{1,0:T(8,128)(2,1)S(1)}, u32[]{:S(2)}, u32[]{:S(2)}) collective-permute-start(bf16[24,1280]{1,0:T(8,128)(2,1)S(1)} %pair_sum.1.refs_0_), channel_id=1, source_target_pairs={{0,16},{4,20},{8,24},{12,28},{16,0},{20,4},{24,8},{28,12},{1,17},{... | collective-permute-start | bytes 184328 | tf_op jit(solution)/shard_map/ppermute | solution.py:45
  30.2 1.0 %collective-permute-start.8 = (bf16[24,1280]{1,0:T(8,128)(2,1)S(1)}, bf16[24,1280]{1,0:T(8,128)(2,1)S(1)}, u32[]{:S(2)}, u32[]{:S(2)}) collective-permute-start(bf16[24,1280]{1,0:T(8,128)(2,1)S(1)} %pair_sum.1.refs_0_), channel_id=1, source_target_pairs={{0,8},{4,12},{8,0},{12,4},{16,24},{20,28},{24,16},{28,20},{1,9},{5... | collective-permute-start | bytes 184328 | tf_op jit(solution)/shard_map/ppermute | solution.py:45
  31.2 1.7 %collective-permute-done.10.refs_3_ = bf16[24,1280]{1,0:T(8,128)(2,1)S(1)} collective-permute-done((bf16[24,1280]{1,0:T(8,128)(2,1)S(1)}, bf16[24,1280]{1,0:T(8,128)(2,1)S(1)}, u32[]{:S(2)}, u32[]{:S(2)}) %collective-permute-start.10) | collective-permute-done | bytes 61472 | tf_op jit(solution)/shard_map/ppermute | solution.py:45
  32.9 1.1 %collective-permute-done.9.refs_2_ = bf16[24,1280]{1,0:T(8,128)(2,1)S(1)} collective-permute-done((bf16[24,1280]{1,0:T(8,128)(2,1)S(1)}, bf16[24,1280]{1,0:T(8,128)(2,1)S(1)}, u32[]{:S(2)}, u32[]{:S(2)}) %collective-permute-start.9) | collective-permute-done | bytes 61472 | tf_op jit(solution)/shard_map/ppermute | solution.py:45
  34.7 1.3 %collective-permute-done.11.got_ref = bf16[32,1152]{1,0:T(8,128)(2,1)S(1)} collective-permute-done((bf16[32,1152]{1,0:T(8,128)(2,1)S(1)}, bf16[32,1152]{1,0:T(8,128)(2,1)S(1)}, u32[]{:S(2)}, u32[]{:S(2)}) %collective-permute-start.11) | collective-permute-done | bytes 73760 | tf_op jit(solution)/shard_map/ppermute | solution.py:45
  36.0 5.6 %act_grads.1 = (bf16[3,2304]{1,0:T(4,128)(2,1)}, bf16[24,2304]{1,0:T(8,128)(2,1)S(1)}, f32[8,128]{1,0:T(8,128)S(1)}, f32[24,1024]{1,0:T(8,128)S(1)}, bf16[24,115...) custom-call(bf16[32,1152]{1,0:T(8,128)(2,1)S(1)} %get-tuple-element.34.mine_ref, ...), custom_call_target="tpu_custom_call" | custom-call | flops 452984832 | bytes 18874368 | tf_op jit(solution)/shard_map/act_grads/pallas_call | solution.py:31
  42.4 1.9 %collective-permute-start.13 = (bf16[24,1152]{1,0:T(8,128)(2,1)S(1)}, bf16[24,1152]{1,0:T(8,128)(2,1)S(1)}, u32[]{:S(2)}, u32[]{:S(2)}) collective-permute-start(bf16[24,1152]{1,0:T(8,128)(2,1)S(1)} %get-tuple-element.42), channel_id=1, source_target_pairs={{0,2},{1,3},{2,0},{3,1},{4,6},{5,7},{6,4},{7,5},{8,10},{9,11},{10,... | collective-permute-start | bytes 165896 | tf_op jit(solution)/shard_map/ppermute | solution.py:45
  44.3 1.7 %collective-permute-start.14 = (bf16[24,1152]{1,0:T(8,128)(2,1)S(1)}, bf16[24,1152]{1,0:T(8,128)(2,1)S(1)}, u32[]{:S(2)}, u32[]{:S(2)}) collective-permute-start(bf16[24,1152]{1,0:T(8,128)(2,1)S(1)} %get-tuple-element.43), channel_id=1, source_target_pairs={{0,3},{1,2},{2,1},{3,0},{4,7},{5,6},{6,5},{7,4},{8,11},{9,10},{10,... | collective-permute-start | bytes 165896 | tf_op jit(solution)/shard_map/ppermute | solution.py:45
  46.0 7.1 %decoder_grads.1 = bf16[4,1024,2304]{2,1,0:T(8,128)(2,1)} custom-call(bf16[24,2304]{1,0:T(8,128)(2,1)S(1)} %get-tuple-element.46.grad_ref, bf16[24,1024]{1,0:T(8,128)(2,1)S(1)} %get-tuple-element.30.acts_ref.refs_0_, bf16[24,1024]{1,0:T(8,128)(2,1)S(1)} %collective-permute-done.4.refs_3_.refs_1_, ...), custom_call_target="tpu_custom_call" | custom-call | flops 452984832 | bytes 18874368 | tf_op jit(solution)/shard_map/decoder_grads/pallas_call | solution.py:31
  53.1 3.1 %encoder_grad.1 = (bf16[2304,1024]{1,0:T(8,128)(2,1)}, f32[1,1]{1,0:T(1,128)}) custom-call(bf16[24,2304]{1,0:T(8,128)(2,1)S(1)} %get-tuple-element.28.x_ref, f32[24,1024]{1,0:T(8,128)S(1)} %get-tuple-element.37.part_ref, f32[24,1024]{1,0:T(8,128)S(1)} %get-tuple-element.38.gate_ref, f32[24,1024]{1,0:T(8,128)S(1)} %get-tuple-element.39.sparse_ref, ...), custom_call_target="tpu_custom_call" | custom-call | flops 113246208 | bytes 4718592 | tf_op jit(solution)/shard_map/encoder_grad/pallas_call | solution.py:31
  (20 shorter events, 3.3 us)
Async XLA Ops:
  0.6 23.1 %copy-start = (bf16[4,1,1024,2304]{3,2,1,0:T(8,128)(2,1)S(1)}, bf16[4,1,1024,2304]{3,2,1,0:T(8,128)(2,1)}, u32[]{:S(2)}) copy-start(bf16[4,1,1024,2304]{3,2,1,0:T(8,128)(2,1)} %param.8) | copy-start | bytes 56623108
  1.6 1.4 %collective-permute-start = (bf16[8,2304]{1,0:T(8,128)(2,1)S(1)}, bf16[8,2304]{1,0:T(8,128)(2,1)S(1)}, u32[]{:S(2)}, u32[]{:S(2)}) collective-permute-start(bf16[8,2304]{1,0:T(8,128)(2,1)S(1)} %get-tuple-element.26.refs_0_), channel_id=1, source_target_pairs={{0,4},{4,0},{8,12},{12,8},{16,20},{20,16},{24,28},{28,24},{1,5},{5... | collective-permute-start | bytes 110600 | tf_op jit(solution)/shard_map/ppermute | solution.py:45
  3.0 6.4 %collective-permute-start.3 = (bf16[16,2304]{1,0:T(8,128)(2,1)S(1)}, bf16[16,2304]{1,0:T(8,128)(2,1)S(1)}, u32[]{:S(2)}, u32[]{:S(2)}) collective-permute-start(bf16[16,2304]{1,0:T(8,128)(2,1)S(1)} %stack.1.refs_0_), channel_id=1, source_target_pairs={{0,24},{4,28},{8,16},{12,20},{16,8},{20,12},{24,0},{28,4},{1,25},{... | collective-permute-start | bytes 221192 | tf_op jit(solution)/shard_map/ppermute | solution.py:45
  6.8 4.4 %collective-permute-start.2 = (bf16[16,2304]{1,0:T(8,128)(2,1)S(1)}, bf16[16,2304]{1,0:T(8,128)(2,1)S(1)}, u32[]{:S(2)}, u32[]{:S(2)}) collective-permute-start(bf16[16,2304]{1,0:T(8,128)(2,1)S(1)} %stack.1.refs_0_), channel_id=1, source_target_pairs={{0,16},{4,20},{8,24},{12,28},{16,0},{20,4},{24,8},{28,12},{1,17},{... | collective-permute-start | bytes 221192 | tf_op jit(solution)/shard_map/ppermute | solution.py:45
  7.3 4.4 %collective-permute-start.1 = (bf16[16,2304]{1,0:T(8,128)(2,1)S(1)}, bf16[16,2304]{1,0:T(8,128)(2,1)S(1)}, u32[]{:S(2)}, u32[]{:S(2)}) collective-permute-start(bf16[16,2304]{1,0:T(8,128)(2,1)S(1)} %stack.1.refs_0_), channel_id=1, source_target_pairs={{0,8},{4,12},{8,0},{12,4},{16,24},{20,28},{24,16},{28,20},{1,9},{5... | collective-permute-start | bytes 221192 | tf_op jit(solution)/shard_map/ppermute | solution.py:45
  11.6 2.3 %copy-start.1 = (bf16[1,2304,1024]{2,1,0:T(8,128)(2,1)S(1)}, bf16[1,2304,1024]{2,1,0:T(8,128)(2,1)}, u32[]{:S(2)}) copy-start(bf16[1,2304,1024]{2,1,0:T(8,128)(2,1)} %param.6) | copy-start | bytes 14155780
  15.1 7.1 %collective-permute-start.6 = (bf16[24,1024]{1,0:T(8,128)(2,1)S(1)}, bf16[24,1024]{1,0:T(8,128)(2,1)S(1)}, u32[]{:S(2)}, u32[]{:S(2)}) collective-permute-start(bf16[24,1024]{1,0:T(8,128)(2,1)S(1)} %get-tuple-element.30.acts_ref.refs_0_), channel_id=1, source_target_pairs={{0,3},{1,2},{2,1},{3,0},{4,7},{5,6},{6,5},{7,4},{8,11},{9,10},{10,... | collective-permute-start | bytes 147464 | tf_op jit(solution)/shard_map/ppermute | solution.py:45
  18.7 5.0 %collective-permute-start.5 = (bf16[24,1024]{1,0:T(8,128)(2,1)S(1)}, bf16[24,1024]{1,0:T(8,128)(2,1)S(1)}, u32[]{:S(2)}, u32[]{:S(2)}) collective-permute-start(bf16[24,1024]{1,0:T(8,128)(2,1)S(1)} %get-tuple-element.30.acts_ref.refs_0_), channel_id=1, source_target_pairs={{0,2},{1,3},{2,0},{3,1},{4,6},{5,7},{6,4},{7,5},{8,10},{9,11},{10,... | collective-permute-start | bytes 147464 | tf_op jit(solution)/shard_map/ppermute | solution.py:45
  18.7 5.0 %collective-permute-start.4 = (bf16[24,1024]{1,0:T(8,128)(2,1)S(1)}, bf16[24,1024]{1,0:T(8,128)(2,1)S(1)}, u32[]{:S(2)}, u32[]{:S(2)}) collective-permute-start(bf16[24,1024]{1,0:T(8,128)(2,1)S(1)} %get-tuple-element.30.acts_ref.refs_0_), channel_id=1, source_target_pairs={{0,1},{1,0},{2,3},{3,2},{4,5},{5,4},{6,7},{7,6},{8,9},{9,8},{10,11... | collective-permute-start | bytes 147464 | tf_op jit(solution)/shard_map/ppermute | solution.py:45
  26.2 1.4 %collective-permute-start.7 = (f32[24,1280]{1,0:T(8,128)S(1)}, f32[24,1280]{1,0:T(8,128)S(1)}, u32[]{:S(2)}, u32[]{:S(2)}) collective-permute-start(f32[24,1280]{1,0:T(8,128)S(1)} %get-tuple-element.33), channel_id=1, source_target_pairs={{0,4},{4,0},{8,12},{12,8},{16,20},{20,16},{24,28},{28,24},{1,5},{5... | collective-permute-start | bytes 368648 | tf_op jit(solution)/shard_map/ppermute | solution.py:45
  27.7 5.2 %collective-permute-start.10 = (bf16[24,1280]{1,0:T(8,128)(2,1)S(1)}, bf16[24,1280]{1,0:T(8,128)(2,1)S(1)}, u32[]{:S(2)}, u32[]{:S(2)}) collective-permute-start(bf16[24,1280]{1,0:T(8,128)(2,1)S(1)} %pair_sum.1.refs_0_), channel_id=1, source_target_pairs={{0,24},{4,28},{8,16},{12,20},{16,8},{20,12},{24,0},{28,4},{1,25},{... | collective-permute-start | bytes 184328 | tf_op jit(solution)/shard_map/ppermute | solution.py:45
  29.2 4.8 %collective-permute-start.9 = (bf16[24,1280]{1,0:T(8,128)(2,1)S(1)}, bf16[24,1280]{1,0:T(8,128)(2,1)S(1)}, u32[]{:S(2)}, u32[]{:S(2)}) collective-permute-start(bf16[24,1280]{1,0:T(8,128)(2,1)S(1)} %pair_sum.1.refs_0_), channel_id=1, source_target_pairs={{0,16},{4,20},{8,24},{12,28},{16,0},{20,4},{24,8},{28,12},{1,17},{... | collective-permute-start | bytes 184328 | tf_op jit(solution)/shard_map/ppermute | solution.py:45
  30.2 4.2 %collective-permute-start.8 = (bf16[24,1280]{1,0:T(8,128)(2,1)S(1)}, bf16[24,1280]{1,0:T(8,128)(2,1)S(1)}, u32[]{:S(2)}, u32[]{:S(2)}) collective-permute-start(bf16[24,1280]{1,0:T(8,128)(2,1)S(1)} %pair_sum.1.refs_0_), channel_id=1, source_target_pairs={{0,8},{4,12},{8,0},{12,4},{16,24},{20,28},{24,16},{28,20},{1,9},{5... | collective-permute-start | bytes 184328 | tf_op jit(solution)/shard_map/ppermute | solution.py:45
  34.6 1.3 %collective-permute-start.11 = (bf16[32,1152]{1,0:T(8,128)(2,1)S(1)}, bf16[32,1152]{1,0:T(8,128)(2,1)S(1)}, u32[]{:S(2)}, u32[]{:S(2)}) collective-permute-start(bf16[32,1152]{1,0:T(8,128)(2,1)S(1)} %get-tuple-element.34.mine_ref), channel_id=1, source_target_pairs={{0,4},{4,0},{8,12},{12,8},{16,20},{20,16},{24,28},{28,24},{1,5},{5... | collective-permute-start | bytes 221192 | tf_op jit(solution)/shard_map/ppermute | solution.py:45
  41.6 11.5 %collective-permute-start.12 = (bf16[24,1152]{1,0:T(8,128)(2,1)S(1)}, bf16[24,1152]{1,0:T(8,128)(2,1)S(1)}, u32[]{:S(2)}, u32[]{:S(2)}) collective-permute-start(bf16[24,1152]{1,0:T(8,128)(2,1)S(1)} %get-tuple-element.41), channel_id=1, source_target_pairs={{0,1},{1,0},{2,3},{3,2},{4,5},{5,4},{6,7},{7,6},{8,9},{9,8},{10,11... | collective-permute-start | bytes 165896 | tf_op jit(solution)/shard_map/ppermute | solution.py:45
  42.4 10.8 %collective-permute-start.13 = (bf16[24,1152]{1,0:T(8,128)(2,1)S(1)}, bf16[24,1152]{1,0:T(8,128)(2,1)S(1)}, u32[]{:S(2)}, u32[]{:S(2)}) collective-permute-start(bf16[24,1152]{1,0:T(8,128)(2,1)S(1)} %get-tuple-element.42), channel_id=1, source_target_pairs={{0,2},{1,3},{2,0},{3,1},{4,6},{5,7},{6,4},{7,5},{8,10},{9,11},{10,... | collective-permute-start | bytes 165896 | tf_op jit(solution)/shard_map/ppermute | solution.py:45
  44.3 8.8 %collective-permute-start.14 = (bf16[24,1152]{1,0:T(8,128)(2,1)S(1)}, bf16[24,1152]{1,0:T(8,128)(2,1)S(1)}, u32[]{:S(2)}, u32[]{:S(2)}) collective-permute-start(bf16[24,1152]{1,0:T(8,128)(2,1)S(1)} %get-tuple-element.43), channel_id=1, source_target_pairs={{0,3},{1,2},{2,1},{3,0},{4,7},{5,6},{6,5},{7,4},{8,11},{9,10},{10,... | collective-permute-start | bytes 165896 | tf_op jit(solution)/shard_map/ppermute | solution.py:45

commit v3 on v2

--- a/solution.py
+++ b/solution.py
@@ -27,13 +27,14 @@
     return jax.ShapeDtypeStruct(dims, dtype)
 
 
-def call(body, outs, args, name, scratch=(), limit=16, in_specs=None, out_specs=None, flops=0, bytes_accessed=0):
+def call(body, outs, args, name, scratch=(), limit=16, in_specs=None, out_specs=None, aliases=None, flops=0, bytes_accessed=0):
     return pl.pallas_call(
         body,
         out_shape=outs,
         in_specs=in_specs or [WHOLE] * len(args),
         out_specs=out_specs or [WHOLE] * len(outs),
         scratch_shapes=list(scratch),
+        input_output_aliases=aliases or {},
         compiler_params=pltpu.CompilerParams(vmem_limit_bytes=limit * MIB),
         cost_estimate=pl.CostEstimate(flops=flops, bytes_accessed=bytes_accessed, transcendentals=0),
         name=name,
@@ -60,21 +61,26 @@
     return block.astype(BF16)
 
 
-def pack(res_hbm, target_hbm, thr_hbm, out_ref, cutoff_ref, res_ref, target_ref, thr_ref, sems):
-    copies = [
-        pltpu.make_async_copy(res_hbm, res_ref, sems.at[0]),
-        pltpu.make_async_copy(target_hbm, target_ref, sems.at[1]),
-        pltpu.make_async_copy(thr_hbm, thr_ref, sems.at[2]),
-    ]
+def load_own(res_hbm, target_hbm, thr_hbm, out_ref, cutoff_ref, res_ref, target_ref, thr_ref, sems):
+    places = ((res_hbm, res_ref), (target_hbm, target_ref), (thr_hbm, thr_ref))
+    copies = [pltpu.make_async_copy(*place, sems.at[i]) for i, place in enumerate(places)]
     for copy in copies:
         copy.start()
+    rows = res_ref.shape[0]
+    out_ref[...] = jnp.zeros_like(out_ref)
     for copy in copies:
         copy.wait()
-    rows = res_ref.shape[0]
-    out_ref[...] = jnp.zeros_like(out_ref)
     out_ref[:rows] = res_ref[...]
     out_ref[rows : 2 * rows] = target_ref[...]
     cutoff_ref[...] = (thr_ref[...].astype(F32) + 0.5) / 2048.0
+
+
+def pack(own_ref, res_ref, target_ref, out_ref):
+    height, rows = own_ref.shape[0], res_ref.shape[0]
+    out_ref[:height] = own_ref[...]
+    out_ref[height:] = jnp.zeros_like(own_ref)
+    out_ref[height : height + rows] = res_ref[...]
+    out_ref[height + rows : height + 2 * rows] = target_ref[...]
 
 
 def stack(*refs):
@@ -82,6 +88,12 @@
     height = refs[0].shape[0]
     for i, ref in enumerate(refs[:-1]):
         out_ref[i * height : (i + 1) * height] = ref[...]
+
+
+def fetch(_, src_hbm, out_ref, sem):
+    copy = pltpu.make_async_copy(src_hbm, out_ref, sem)
+    copy.start()
+    copy.wait()
 
 
 def gather_rows(rows, height, tokens, first, blocks):
@@ -130,21 +142,16 @@
     total_ref[...] = total
 
 
-def recon_rest(*refs):
-    total_ref, pen_ref, dec_ref, *acts = refs[:-2]
-    keep_ref, send_ref = refs[-2:]
+def recon_half(theirs, total_ref, pen_ref, dec_ref, *refs):
+    *acts, out_ref = refs
     me = lax.axis_index("layer")
     half = dec_ref.shape[2] // 2
-    total = total_ref[...]
+    span = pl.ds(pl.multiple_of((lax.axis_index("feat") + theirs) % 2 * half, half), half)
+    total = total_ref[:, span]
     for k, acts_ref in enumerate(acts, 1):
-        total = total + jnp.dot(acts_ref[...], dec_ref[me ^ k], preferred_element_type=F32)
-    first, second = total[:, :half], total[:, half:]
-    low = lax.axis_index("feat") % 2 == 0
-    pen = jnp.broadcast_to(pen_ref[0:1, :], (total.shape[0], LANES))
-    keep_ref[:, :half] = jnp.where(low, first, second)
-    send_ref[:, :half] = jnp.where(low, second, first)
-    keep_ref[:, half:] = pen
-    send_ref[:, half:] = pen
+        total = total + jnp.dot(acts_ref[...], dec_ref[me ^ k, :, span], preferred_element_type=F32)
+    out_ref[:, :half] = total
+    out_ref[:, half:] = jnp.broadcast_to(pen_ref[0:1, :], (total.shape[0], LANES))
 
 
 def pair_sum(keep_ref, got_ref, msg_ref):
@@ -196,42 +203,53 @@
     pen_ref[...] = jnp.broadcast_to(pen, pen_ref.shape)
 
 
-def act_grads(rows, mine_ref, got_ref, own_ref, pen_ref, dec_ref, *outs):
-    recon_ref, grad_ref, score_ref, part_ref, *msgs = outs
+def act_grad(grad, dec):
+    return lax.dot_general(dec, grad, NT, preferred_element_type=F32).T
+
+
+def act_half(grad, dec_ref, source, theirs):
+    half = grad.shape[1]
+    span = pl.ds(pl.multiple_of((lax.axis_index("feat") + theirs) % 2 * half, half), half)
+    return act_grad(grad, dec_ref[source, :, span])
+
+
+def act_first(mine_ref, dec_ref, *outs):
+    tokens = outs[0].shape[0]
+    me = lax.axis_index("layer")
+    for k, out_ref in enumerate(outs, 1):
+        out_ref[...] = act_half(mine_ref[:tokens, :], dec_ref, me ^ k, 0)
+
+
+def act_second(rows, count, mine_ref, got_ref, own_ref, pen_ref, dec_ref, *refs):
+    parts = refs[:count]
+    recon_ref, grad_ref, score_ref, *msgs = refs[count:]
     tokens, half = grad_ref.shape[0], grad_ref.shape[1] // 2
     low = lax.axis_index("feat") % 2 == 0
     me = lax.axis_index("layer")
-    first = jnp.where(low, mine_ref[:tokens, :], got_ref[:tokens, :])
-    second = jnp.where(low, got_ref[:tokens, :], mine_ref[:tokens, :])
-    grad_ref[:, :half] = first
-    grad_ref[:, half:] = second
+    mine, got = mine_ref[:tokens, :], got_ref[:tokens, :]
     extra = got_ref[tokens:, :].astype(F32)
-    own = own_ref[...]
-    recon_ref[:, :half] = jnp.where(low, own, extra)[:rows].astype(BF16)
-    recon_ref[:, half:] = jnp.where(low, extra, own)[:rows].astype(BF16)
     mine_extra = mine_ref[tokens:, :].astype(F32)
     squares = jnp.sum(mine_extra[rows : rows + 1, :LANES], axis=1, keepdims=True)
     squares = squares + jnp.sum(extra[rows : rows + 1, :LANES], axis=1, keepdims=True)
     score = squares + 2.0 * ERROR_SCALE * PENALTY_WEIGHT * pen_ref[0:1, 0:1]
     score_ref[...] = jnp.broadcast_to(score, score_ref.shape)
-    grad = grad_ref[...]
     width = dec_ref.shape[1]
-    for k in range(len(msgs), -1, -1):
-        part = lax.dot_general(dec_ref[me ^ k], grad, NT, preferred_element_type=F32).T
-        if k:
-            msgs[k - 1][:, :width] = part.astype(BF16)
-            msgs[k - 1][:, width:] = spread3(score, (tokens, LANES))
-        else:
-            part_ref[...] = part
-
-
-def decoder_grads(grad_ref, *refs):
-    *acts, out_hbm, buf, sems = refs
+    for k, (part_ref, msg) in enumerate(zip(parts, msgs), 1):
+        msg[:, :width] = (part_ref[...] + act_half(got, dec_ref, me ^ k, 1)).astype(BF16)
+        msg[:, width:] = spread3(score, (tokens, LANES))
+    grad_ref[:, :half] = jnp.where(low, mine, got)
+    grad_ref[:, half:] = jnp.where(low, got, mine)
+    own = own_ref[...]
+    recon_ref[:, :half] = jnp.where(low, own, extra)[:rows].astype(BF16)
+    recon_ref[:, half:] = jnp.where(low, extra, own)[:rows].astype(BF16)
+
+
+def write_decoder_grads(first, grad_ref, acts, out_hbm, buf, sems):
     me = lax.axis_index("layer")
     block = buf.shape[1]
     steps = acts[0].shape[1] // block
     copies = []
-    for k, acts_ref in enumerate(acts):
+    for k, acts_ref in enumerate(acts, first):
         turned = acts_ref[...].T
         for i in range(steps):
             n = len(copies)
@@ -239,24 +257,32 @@
             buf[n] = jnp.dot(turned[span], grad_ref[...], preferred_element_type=F32).astype(BF16)
             copies.append(pltpu.make_async_copy(buf.at[n], out_hbm.at[me ^ k, pl.ds(i * block, block)], sems.at[n]))
             copies[-1].start()
+    return copies
+
+
+def first_grads(grad_ref, dec_ref, *refs):
+    *acts, out_hbm, part_ref, buf, sems = refs
+    copies = write_decoder_grads(0, grad_ref, acts, out_hbm, buf, sems)
+    part_ref[...] = act_grad(grad_ref[...], dec_ref[lax.axis_index("layer")])
     for copy in copies:
         copy.wait()
 
 
-def encoder_grad(count, x_ref, part_ref, gate_ref, sparse_ref, score_ref, *refs):
-    *msgs, out_hbm, loss_ref, buf, sems = refs
+def last_grads(count, first, last, grad_ref, x_ref, part_ref, gate_ref, sparse_ref, score_ref, *refs):
+    *rest, _, dec_hbm, enc_hbm, loss_ref, dec_buf, dec_sems, enc_buf, enc_sems = refs
+    acts, msgs = rest[:last], rest[last:]
+    copies = write_decoder_grads(first, grad_ref, acts, dec_hbm, dec_buf, dec_sems)
     width = part_ref.shape[1]
     total = part_ref[...]
     for msg in msgs:
         total = total + msg[:, :width].astype(F32)
     pre = jnp.where(gate_ref[...] > 0, total + sparse_ref[...], 0.0).astype(BF16)
     turned = x_ref[...].T
-    block = buf.shape[1]
-    copies = []
-    for i in range(buf.shape[0]):
+    block = enc_buf.shape[1]
+    for i in range(enc_buf.shape[0]):
         span = slice(i * block, (i + 1) * block)
-        buf[i] = jnp.dot(turned[span], pre, preferred_element_type=F32).astype(BF16)
-        copies.append(pltpu.make_async_copy(buf.at[i], out_hbm.at[pl.ds(i * block, block)], sems.at[i]))
+        enc_buf[i] = jnp.dot(turned[span], pre, preferred_element_type=F32).astype(BF16)
+        copies.append(pltpu.make_async_copy(enc_buf.at[i], enc_hbm.at[pl.ds(i * block, block)], enc_sems.at[i]))
         copies[-1].start()
     scores = [score_ref[0:1, 0:1]]
     for msg in msgs:
@@ -277,27 +303,40 @@
     decoder = dec_weight[:, 0]
 
     height = -(-2 * rows // 8) * 8
-    block, cutoff = call(
-        pack,
+    mine = (residual_in[0], target[0])
+    own, cutoff = call(
+        load_own,
         [shape((height, width), BF16), shape((1, features), F32)],
-        (in_hbm(residual_in[0]), in_hbm(target[0]), in_hbm(thresholds)),
-        "pack",
+        [in_hbm(part) for part in (*mine, thresholds)],
+        "load_own",
         scratch=[pltpu.VMEM((rows, width), BF16)] * 2 + [pltpu.VMEM((1, features), jnp.int32), pltpu.SemaphoreType.DMA((3,))],
         in_specs=[ANY] * 3,
-        bytes_accessed=0,
-    )
-    blocks, bit = [block, swap(block, "feat", 1)], 2
+        bytes_accessed=2 * width * features,
+    )
+    (block,) = call(pack, [shape((2 * height, width), BF16)], (own, *(swap(part, "feat", 1) for part in mine)), "pack")
+    (encoder,) = call(
+        fetch,
+        [shape((width, features), BF16)],
+        (block, in_hbm(enc_weight[0])),
+        "fetch",
+        scratch=[pltpu.SemaphoreType.DMA(())],
+        in_specs=[ANY] * 2,
+        bytes_accessed=4 * width * features,
+    )
+    blocks, bit = [block], 2
     while bit < feats:
-        (block,) = call(stack, [shape((bit * height, width), BF16)], blocks, "stack")
         pair = (bit, 2 * bit, 3 * bit) if 2 * bit < feats else (bit,)
         blocks = [block] + [swap(block, "feat", k) for k in pair]
         bit <<= len(pair) // 2 + 1
+        if bit < feats:
+            (block,) = call(stack, [shape((bit * height, width), BF16)], blocks, "stack")
     x, targets, acts, gate, sparse, pen = call(
         functools.partial(encode, rows, height),
         [shape((tokens, width), BF16)] * 2
         + [shape((tokens, features), BF16), shape((tokens, features), F32), shape((tokens, features), F32), shape((8, LANES), F32)],
-        (*blocks, enc_weight[0], cutoff),
+        (*blocks, encoder, cutoff),
         "encode",
+        limit=48,
         flops=2 * tokens * width * features,
         bytes_accessed=2 * width * features,
     )
@@ -314,13 +353,16 @@
         flops=2 * tokens * width * features,
         bytes_accessed=2 * width * features,
     )
-    keep, send = call(
-        recon_rest,
-        [shape((tokens, half + LANES), F32)] * 2,
-        (total, pen, decoder, *others),
-        "recon_rest",
-        flops=2 * tokens * width * features * (sources - 1),
-        bytes_accessed=2 * (sources - 1) * width * features,
+    send, keep = (
+        call(
+            functools.partial(recon_half, theirs),
+            [shape((tokens, half + LANES), F32)],
+            (total, pen, decoder, *others),
+            name,
+            flops=tokens * width * features * (sources - 1),
+            bytes_accessed=(sources - 1) * width * features,
+        )[0]
+        for theirs, name in ((1, "recon_send"), (0, "recon_keep"))
     )
     (msg,) = call(pair_sum, [shape((tokens, half + LANES), BF16)], (keep, swap(send, "feat", 1)), "pair_sum")
     bit = 2
@@ -336,38 +378,55 @@
         (targets, *msgs),
         "error_half",
     )
-    recon, grad, score, part, *sends = call(
-        functools.partial(act_grads, rows),
-        [shape((rows, width), BF16), shape((tokens, width), BF16), shape((8, LANES), F32), shape((tokens, features), F32)]
+    parts = call(
+        act_first,
+        [shape((tokens, features), F32)] * (layers - 1),
+        (mine, decoder),
+        "act_first",
+        flops=tokens * width * features * (sources - 1),
+        bytes_accessed=(sources - 1) * width * features,
+    )
+    recon, grad, score, *sends = call(
+        functools.partial(act_second, rows, layers - 1),
+        [shape((rows, width), BF16), shape((tokens, width), BF16), shape((8, LANES), F32)]
         + [shape((tokens, features + LANES), BF16)] * (layers - 1),
-        (mine, swap(mine, "feat", 1), own_rows, pen_all, decoder),
-        "act_grads",
-        flops=2 * tokens * width * features * sources,
-        bytes_accessed=2 * sources * width * features,
+        (mine, swap(mine, "feat", 1), own_rows, pen_all, decoder, *parts),
+        "act_second",
+        flops=tokens * width * features * (sources - 1),
+        bytes_accessed=(sources - 1) * width * features,
     )
     gots = [swap(sends[k - 1], "layer", k) for k in range(1, layers)]
-    steps = max(1, features // 256)
-    (dec_grad,) = call(
-        decoder_grads,
-        [shape((sources, features, width), BF16)],
-        (grad, acts, *others),
-        "decoder_grads",
-        scratch=[pltpu.VMEM((sources * steps, features // steps, width), BF16), pltpu.SemaphoreType.DMA((sources * steps,))],
+    first, steps, block = sources - 1, max(1, features // 128), 128
+    last = sources - first
+    dec_grad, part = call(
+        first_grads,
+        [shape((sources, features, width), BF16), shape((tokens, features), F32)],
+        (grad, decoder, acts, *others[: first - 1]),
+        "first_grads",
+        scratch=[pltpu.VMEM((first * steps, features // steps, width), BF16), pltpu.SemaphoreType.DMA((first * steps,))],
         limit=24,
-        out_specs=[ANY],
-        flops=2 * tokens * width * features * sources,
-        bytes_accessed=2 * sources * width * features,
-    )
-    block = 256
-    enc_grad, loss = call(
-        functools.partial(encoder_grad, layers * tokens * width),
-        [shape((width, features), BF16), shape((1, 1), F32)],
-        (x, part, gate, sparse, score, *gots),
-        "encoder_grad",
-        scratch=[pltpu.VMEM((width // block, block, features), BF16), pltpu.SemaphoreType.DMA((width // block,))],
         out_specs=[ANY, WHOLE],
-        flops=2 * tokens * width * features,
-        bytes_accessed=2 * width * features,
+        flops=2 * tokens * width * features * (first + 1),
+        bytes_accessed=2 * first * width * features,
+    )
+    args = (grad, x, part, gate, sparse, score, *others[first - 1 :], *gots, dec_grad)
+    dec_grad, enc_grad, loss = call(
+        functools.partial(last_grads, layers * tokens * width, first, last),
+        [shape((sources, features, width), BF16), shape((width, features), BF16), shape((1, 1), F32)],
+        args,
+        "last_grads",
+        scratch=[
+            pltpu.VMEM((last * steps, features // steps, width), BF16),
+            pltpu.SemaphoreType.DMA((last * steps,)),
+            pltpu.VMEM((width // block, block, features), BF16),
+            pltpu.SemaphoreType.DMA((width // block,)),
+        ],
+        in_specs=[WHOLE] * (len(args) - 1) + [ANY],
+        out_specs=[ANY, ANY, WHOLE],
+        limit=24,
+        aliases={len(args) - 1: 0},
+        flops=2 * tokens * width * features * (last + 1),
+        bytes_accessed=2 * (last + 1) * width * features,
     )
     return loss[0, 0], recon[None], dec_grad[:, None], enc_grad[None]
 

time: 56.4 us -> 50.4 us (0.89)
  waiting for transfers between devices: 12.4 us -> 6.62 us
  local copies, waits for them, and re-layouts: 2.34 us -> 0.01 us
  Pallas kernels: 23.4 us -> 25.5 us
    ppermute x15 -> x16, waiting for transfers between devices: 12.4 us -> 6.62 us  [swap(): return lax.ppermute(x, axis, [(i, i ^ bits) for i in range(size)])]
    unnamed x4 -> x2, local copies, waits for them, and re-layouts: 2.34 us -> 0.01 us
    pallas_call x10 -> x13, Pallas kernels: 23.4 us -> 25.5 us  [call(): pl.pallas_call(body, out_shape=outs, in_specs=in_specs or [WHOLE] * len(a...]
    ppermute x15 -> x16, starting transfers between devices: 17.3 us -> 17.3 us  [swap(): return lax.ppermute(x, axis, [(i, i ^ bits) for i in range(size)])]
  transfers between devices with their start and end apart: 15 -> 16, of which waited for: 10 -> 8; matrix products, arithmetic and copies ran while one was open for 0% -> 0% of each run, Pallas kernels for 17% -> 31%
where the time goes in v3:
time: 50.4 us; the launch traced here: 50.2 us
  Pallas kernels  25.5 us (51%)
  starting transfers between devices  17.3 us (34%)
  waiting for transfers between devices  6.62 us (13%)
  between operations  0.76 us (2%)
    pallas_call x13, Pallas kernels, call(): pl.pallas_call(body, out_shape=outs, in_specs=in_specs or [WHOLE] * len(a...  25.5 us
    ppermute x16, starting transfers between devices, swap(): return lax.ppermute(x, axis, [(i, i ^ bits) for i in range(size)])  17.3 us
    ppermute x16, waiting for transfers between devices, swap(): return lax.ppermute(x, axis, [(i, i ^ bits) for i in range(size)])  6.62 us
  transfers between devices with their start and end apart: 16, of which 8 were waited for; matrix products, arithmetic and copies ran while one was open for 0% of the time, Pallas kernels for 31%

profile of v3, /device:TPU:0, one launch (start us, length us, event | category | flops | bytes accessed | tf_op | source)
XLA Modules:
  0.0 50.2 jit_solution(4931947539304883874)
XLA Ops:
  0.6 0.5 %collective-permute-start = (bf16[3,2304]{1,0:T(4,128)(2,1)}, bf16[3,2304]{1,0:T(4,128)(2,1)S(1)}, u32[]{:S(2)}, u32[]{:S(2)}) collective-permute-start(bf16[3,2304]{1,0:T(4,128)(2,1)} %bitcast.18), channel_id=1, source_target_pairs={{0,4},{4,0},{8,12},{12,8},{16,20},{20,16},{24,28},{28,24},{1,5},{5... | collective-permute-start | bytes 41480 | tf_op jit(solution)/shard_map/ppermute | solution.py:46
  1.2 0.8 %load_own.1 = (bf16[8,2304]{1,0:T(8,128)(2,1)S(1)}, f32[1,1024]{1,0:T(1,128)S(1)}) custom-call(bf16[3,2304]{1,0:T(4,128)(2,1)} %bitcast.19, bf16[3,2304]{1,0:T(4,128)(2,1)} %bitcast.21, s32[1,1024]{1,0:T(1,128)} %thr_hbm.1), custom_call_target="tpu_custom_call" | custom-call | bytes 4718592 | tf_op jit(solution)/shard_map/load_own/pallas_call | solution.py:31
  2.6 3.7 %collective-permute-start.4 = (bf16[16,2304]{1,0:T(8,128)(2,1)S(1)}, bf16[16,2304]{1,0:T(8,128)(2,1)S(1)}, u32[]{:S(2)}, u32[]{:S(2)}) collective-permute-start(bf16[16,2304]{1,0:T(8,128)(2,1)S(1)} %pack.1._.refs_0_), channel_id=1, source_target_pairs={{0,24},{4,28},{8,16},{12,20},{16,8},{20,12},{24,0},{28,4},{1,25},{... | collective-permute-start | bytes 221192 | tf_op jit(solution)/shard_map/ppermute | solution.py:46
  6.9 2.3 %fetch.1.refs_4_ = bf16[2304,1024]{1,0:T(8,128)(2,1)S(1)} custom-call(bf16[16,2304]{1,0:T(8,128)(2,1)S(1)} %pack.1._.refs_0_, bf16[2304,1024]{1,0:T(8,128)(2,1)} %bitcast.17), custom_call_target="tpu_custom_call" | custom-call | bytes 9437184 | tf_op jit(solution)/shard_map/fetch/pallas_call | solution.py:31
  9.2 1.4 %collective-permute-done.3.refs_2_ = bf16[16,2304]{1,0:T(8,128)(2,1)S(1)} collective-permute-done((bf16[16,2304]{1,0:T(8,128)(2,1)S(1)}, bf16[16,2304]{1,0:T(8,128)(2,1)S(1)}, u32[]{:S(2)}, u32[]{:S(2)}) %collective-permute-start.3) | collective-permute-done | bytes 73760 | tf_op jit(solution)/shard_map/ppermute | solution.py:46
  11.1 1.1 %encode.1 = (bf16[24,2304]{1,0:T(8,128)(2,1)S(1)}, bf16[24,2304]{1,0:T(8,128)(2,1)S(1)}, bf16[24,1024]{1,0:T(8,128)(2,1)S(1)}, f32[24,1024]{1,0:T(8,128)S(1)}, f...) custom-call(bf16[16,2304]{1,0:T(8,128)(2,1)S(1)} %pack.1._.refs_0_, bf16[16,2304]{1,0:T(8,128)(2,1)S(1)} %collective-permute-done.2.refs_1_, ...), custom_call_target="tpu_custom_call" | custom-call | flops 113246208 | bytes 4718592 | tf_op jit(solution)/shard_map/encode/pallas_call | solution.py:31
  12.2 3.6 %collective-permute-start.7 = (bf16[24,1024]{1,0:T(8,128)(2,1)S(1)}, bf16[24,1024]{1,0:T(8,128)(2,1)S(1)}, u32[]{:S(2)}, u32[]{:S(2)}) collective-permute-start(bf16[24,1024]{1,0:T(8,128)(2,1)S(1)} %get-tuple-element.32.acts_ref.refs_0_), channel_id=1, source_target_pairs={{0,3},{1,2},{2,1},{3,0},{4,7},{5,6},{6,5},{7,4},{8,11},{9,10},{10,... | collective-permute-start | bytes 147464 | tf_op jit(solution)/shard_map/ppermute | solution.py:46
  15.9 0.8 %collective-permute-start.5 = (bf16[24,1024]{1,0:T(8,128)(2,1)S(1)}, bf16[24,1024]{1,0:T(8,128)(2,1)S(1)}, u32[]{:S(2)}, u32[]{:S(2)}) collective-permute-start(bf16[24,1024]{1,0:T(8,128)(2,1)S(1)} %get-tuple-element.32.acts_ref.refs_0_), channel_id=1, source_target_pairs={{0,1},{1,0},{2,3},{3,2},{4,5},{5,4},{6,7},{7,6},{8,9},{9,8},{10,11... | collective-permute-start | bytes 147464 | tf_op jit(solution)/shard_map/ppermute | solution.py:46
  16.6 3.4 %recon_own.1.total_ref = f32[24,2304]{1,0:T(8,128)S(1)} custom-call(bf16[24,1024]{1,0:T(8,128)(2,1)S(1)} %get-tuple-element.32.acts_ref.refs_0_, bf16[4,1024,2304]{2,1,0:T(8,128)(2,1)} %bitcast.10), custom_call_target="tpu_custom_call" | custom-call | flops 113246208 | bytes 4718592 | tf_op jit(solution)/shard_map/recon_own/pallas_call | solution.py:31
  20.1 0.7 %collective-permute-done.6.refs_1_.refs_2_ = bf16[24,1024]{1,0:T(8,128)(2,1)S(1)} collective-permute-done((bf16[24,1024]{1,0:T(8,128)(2,1)S(1)}, bf16[24,1024]{1,0:T(8,128)(2,1)S(1)}, u32[]{:S(2)}, u32[]{:S(2)}) %collective-permute-start.6) | collective-permute-done | bytes 49184 | tf_op jit(solution)/shard_map/ppermute | solution.py:46
  20.9 1.3 %recon_send.1 = f32[24,1280]{1,0:T(8,128)S(1)} custom-call(f32[24,2304]{1,0:T(8,128)S(1)} %recon_own.1.total_ref, f32[8,128]{1,0:T(8,128)S(1)} %get-tuple-element.33.pen_ref, bf16[4,1024,2304]{2,1,0:T(8,128)(2,1)S(1)} %bitcast.11, bf16[24,1024]{1,0:T(8,128)(2,1)S(1)} %collective-permute-done.5.refs_0_.refs_1_, ...), custom_call_target="tpu_custom_call" | custom-call | flops 169869312 | bytes 7077888 | tf_op jit(solution)/shard_map/recon_send/pallas_call | solution.py:31
  22.2 1.3 %recon_keep.1.keep_ref = f32[24,1280]{1,0:T(8,128)S(1)} custom-call(f32[24,2304]{1,0:T(8,128)S(1)} %recon_own.1.total_ref, f32[8,128]{1,0:T(8,128)S(1)} %get-tuple-element.33.pen_ref, bf16[4,1024,2304]{2,1,0:T(8,128)(2,1)S(1)} %bitcast.12, bf16[24,1024]{1,0:T(8,128)(2,1)S(1)} %collective-permute-done.5.refs_0_.refs_1_, ...), custom_call_target="tpu_custom_call" | custom-call | flops 169869312 | bytes 7077888 | tf_op jit(solution)/shard_map/recon_keep/pallas_call | solution.py:31
  23.7 1.5 %collective-permute-start.11 = (bf16[24,1280]{1,0:T(8,128)(2,1)S(1)}, bf16[24,1280]{1,0:T(8,128)(2,1)S(1)}, u32[]{:S(2)}, u32[]{:S(2)}) collective-permute-start(bf16[24,1280]{1,0:T(8,128)(2,1)S(1)} %pair_sum.1.refs_0_), channel_id=1, source_target_pairs={{0,24},{4,28},{8,16},{12,20},{16,8},{20,12},{24,0},{28,4},{1,25},{... | collective-permute-start | bytes 184328 | tf_op jit(solution)/shard_map/ppermute | solution.py:46
  25.2 1.2 %collective-permute-start.10 = (bf16[24,1280]{1,0:T(8,128)(2,1)S(1)}, bf16[24,1280]{1,0:T(8,128)(2,1)S(1)}, u32[]{:S(2)}, u32[]{:S(2)}) collective-permute-start(bf16[24,1280]{1,0:T(8,128)(2,1)S(1)} %pair_sum.1.refs_0_), channel_id=1, source_target_pairs={{0,16},{4,20},{8,24},{12,28},{16,0},{20,4},{24,8},{28,12},{1,17},{... | collective-permute-start | bytes 184328 | tf_op jit(solution)/shard_map/ppermute | solution.py:46
  26.4 0.7 %collective-permute-start.9 = (bf16[24,1280]{1,0:T(8,128)(2,1)S(1)}, bf16[24,1280]{1,0:T(8,128)(2,1)S(1)}, u32[]{:S(2)}, u32[]{:S(2)}) collective-permute-start(bf16[24,1280]{1,0:T(8,128)(2,1)S(1)} %pair_sum.1.refs_0_), channel_id=1, source_target_pairs={{0,8},{4,12},{8,0},{12,4},{16,24},{20,28},{24,16},{28,20},{1,9},{5... | collective-permute-start | bytes 184328 | tf_op jit(solution)/shard_map/ppermute | solution.py:46
  27.2 1.9 %collective-permute-done.11.refs_3_ = bf16[24,1280]{1,0:T(8,128)(2,1)S(1)} collective-permute-done((bf16[24,1280]{1,0:T(8,128)(2,1)S(1)}, bf16[24,1280]{1,0:T(8,128)(2,1)S(1)}, u32[]{:S(2)}, u32[]{:S(2)}) %collective-permute-start.11) | collective-permute-done | bytes 61472 | tf_op jit(solution)/shard_map/ppermute | solution.py:46
  29.1 1.2 %collective-permute-done.10.refs_2_ = bf16[24,1280]{1,0:T(8,128)(2,1)S(1)} collective-permute-done((bf16[24,1280]{1,0:T(8,128)(2,1)S(1)}, bf16[24,1280]{1,0:T(8,128)(2,1)S(1)}, u32[]{:S(2)}, u32[]{:S(2)}) %collective-permute-start.10) | collective-permute-done | bytes 61472 | tf_op jit(solution)/shard_map/ppermute | solution.py:46
  30.9 2.0 %act_first.1 = (f32[24,1024]{1,0:T(8,128)S(1)}, f32[24,1024]{1,0:T(8,128)S(1)}, f32[24,1024]{1,0:T(8,128)S(1)}) custom-call(bf16[32,1152]{1,0:T(8,128)(2,1)S(1)} %get-tuple-element.34.mine_ref, bf16[4,1024,2304]{2,1,0:T(8,128)(2,1)S(1)} %bitcast.13), custom_call_target="tpu_custom_call" | custom-call | flops 169869312 | bytes 7077888 | tf_op jit(solution)/shard_map/act_first/pallas_call | solution.py:31
  32.9 2.6 %act_second.1 = (bf16[3,2304]{1,0:T(4,128)(2,1)}, bf16[24,2304]{1,0:T(8,128)(2,1)S(1)}, f32[8,128]{1,0:T(8,128)S(1)}, bf16[24,1152]{1,0:T(8,128)(2,1)S(1)}, bf16...) custom-call(bf16[32,1152]{1,0:T(8,128)(2,1)S(1)} %get-tuple-element.34.mine_ref, ...), custom_call_target="tpu_custom_call" | custom-call | flops 169869312 | bytes 7077888 | tf_op jit(solution)/shard_map/act_second/pallas_call | solution.py:31
  35.5 0.7 %collective-permute-start.13 = (bf16[24,1152]{1,0:T(8,128)(2,1)S(1)}, bf16[24,1152]{1,0:T(8,128)(2,1)S(1)}, u32[]{:S(2)}, u32[]{:S(2)}) collective-permute-start(bf16[24,1152]{1,0:T(8,128)(2,1)S(1)} %get-tuple-element.46), channel_id=1, source_target_pairs={{0,1},{1,0},{2,3},{3,2},{4,5},{5,4},{6,7},{7,6},{8,9},{9,8},{10,11... | collective-permute-start | bytes 165896 | tf_op jit(solution)/shard_map/ppermute | solution.py:46
  36.3 2.7 %collective-permute-start.14 = (bf16[24,1152]{1,0:T(8,128)(2,1)S(1)}, bf16[24,1152]{1,0:T(8,128)(2,1)S(1)}, u32[]{:S(2)}, u32[]{:S(2)}) collective-permute-start(bf16[24,1152]{1,0:T(8,128)(2,1)S(1)} %get-tuple-element.47), channel_id=1, source_target_pairs={{0,2},{1,3},{2,0},{3,1},{4,6},{5,7},{6,4},{7,5},{8,10},{9,11},{10,... | collective-permute-start | bytes 165896 | tf_op jit(solution)/shard_map/ppermute | solution.py:46
  39.0 0.9 %collective-permute-start.15 = (bf16[24,1152]{1,0:T(8,128)(2,1)S(1)}, bf16[24,1152]{1,0:T(8,128)(2,1)S(1)}, u32[]{:S(2)}, u32[]{:S(2)}) collective-permute-start(bf16[24,1152]{1,0:T(8,128)(2,1)S(1)} %get-tuple-element.48), channel_id=1, source_target_pairs={{0,3},{1,2},{2,1},{3,0},{4,7},{5,6},{6,5},{7,4},{8,11},{9,10},{10,... | collective-permute-start | bytes 165896 | tf_op jit(solution)/shard_map/ppermute | solution.py:46
  39.9 5.6 %first_grads.1 = (bf16[4,1024,2304]{2,1,0:T(8,128)(2,1)}, f32[24,1024]{1,0:T(8,128)S(1)}) custom-call(bf16[24,2304]{1,0:T(8,128)(2,1)S(1)} %get-tuple-element.40.grad_ref, bf16[4,1024,2304]{2,1,0:T(8,128)(2,1)S(1)} %bitcast.15, bf16[24,1024]{1,0:T(8,128)(2,1)S(1)} %get-tuple-element.32.acts_ref.refs_0_, ...), custom_call_target="tpu_custom_call" | custom-call | flops 452984832 | bytes 14155776 | tf_op jit(solution)/shard_map/first_grads/pallas_call | solution.py:31
  45.6 4.7 %last_grads.1 = (bf16[4,1024,2304]{2,1,0:T(8,128)(2,1)}, bf16[2304,1024]{1,0:T(8,128)(2,1)}, f32[1,1]{1,0:T(1,128)}) custom-call(bf16[24,2304]{1,0:T(8,128)(2,1)S(1)} %get-tuple-element.40.grad_ref, bf16[24,2304]{1,0:T(8,128)(2,1)S(1)} %get-tuple-element.41.x_ref, f32[24,1024]{1,0:T(8,128)S(1)} %get-tuple-element.42.part_ref, ...), custom_call_target="tpu_custom_call", output_to_operand_aliasing={{0}: (10, {})} | custom-call | flops 226492416 | bytes 9437184 | tf_op jit(solution)/shard_map/last_grads/pallas_call | solution.py:31
  (23 shorter events, 2.5 us)
Async XLA Ops:
  0.6 1.6 %collective-permute-start = (bf16[3,2304]{1,0:T(4,128)(2,1)}, bf16[3,2304]{1,0:T(4,128)(2,1)S(1)}, u32[]{:S(2)}, u32[]{:S(2)}) collective-permute-start(bf16[3,2304]{1,0:T(4,128)(2,1)} %bitcast.18), channel_id=1, source_target_pairs={{0,4},{4,0},{8,12},{12,8},{16,20},{20,16},{24,28},{28,24},{1,5},{5... | collective-permute-start | bytes 41480 | tf_op jit(solution)/shard_map/ppermute | solution.py:46
  1.1 1.4 %collective-permute-start.1 = (bf16[3,2304]{1,0:T(4,128)(2,1)}, bf16[3,2304]{1,0:T(4,128)(2,1)S(1)}, u32[]{:S(2)}, u32[]{:S(2)}) collective-permute-start(bf16[3,2304]{1,0:T(4,128)(2,1)} %bitcast.20), channel_id=1, source_target_pairs={{0,4},{4,0},{8,12},{12,8},{16,20},{20,16},{24,28},{28,24},{1,5},{5... | collective-permute-start | bytes 41480 | tf_op jit(solution)/shard_map/ppermute | solution.py:46
  2.6 6.7 %collective-permute-start.4 = (bf16[16,2304]{1,0:T(8,128)(2,1)S(1)}, bf16[16,2304]{1,0:T(8,128)(2,1)S(1)}, u32[]{:S(2)}, u32[]{:S(2)}) collective-permute-start(bf16[16,2304]{1,0:T(8,128)(2,1)S(1)} %pack.1._.refs_0_), channel_id=1, source_target_pairs={{0,24},{4,28},{8,16},{12,20},{16,8},{20,12},{24,0},{28,4},{1,25},{... | collective-permute-start | bytes 221192 | tf_op jit(solution)/shard_map/ppermute | solution.py:46
  6.2 4.4 %collective-permute-start.3 = (bf16[16,2304]{1,0:T(8,128)(2,1)S(1)}, bf16[16,2304]{1,0:T(8,128)(2,1)S(1)}, u32[]{:S(2)}, u32[]{:S(2)}) collective-permute-start(bf16[16,2304]{1,0:T(8,128)(2,1)S(1)} %pack.1._.refs_0_), channel_id=1, source_target_pairs={{0,16},{4,20},{8,24},{12,28},{16,0},{20,4},{24,8},{28,12},{1,17},{... | collective-permute-start | bytes 221192 | tf_op jit(solution)/shard_map/ppermute | solution.py:46
  6.7 4.4 %collective-permute-start.2 = (bf16[16,2304]{1,0:T(8,128)(2,1)S(1)}, bf16[16,2304]{1,0:T(8,128)(2,1)S(1)}, u32[]{:S(2)}, u32[]{:S(2)}) collective-permute-start(bf16[16,2304]{1,0:T(8,128)(2,1)S(1)} %pack.1._.refs_0_), channel_id=1, source_target_pairs={{0,8},{4,12},{8,0},{12,4},{16,24},{20,28},{24,16},{28,20},{1,9},{5... | collective-permute-start | bytes 221192 | tf_op jit(solution)/shard_map/ppermute | solution.py:46
  12.2 8.6 %copy-start = (bf16[4,1,1024,2304]{3,2,1,0:T(8,128)(2,1)S(1)}, bf16[4,1,1024,2304]{3,2,1,0:T(8,128)(2,1)}, u32[]{:S(2)}) copy-start(bf16[4,1,1024,2304]{3,2,1,0:T(8,128)(2,1)} %param.8) | copy-start | bytes 56623108
  12.2 7.9 %collective-permute-start.7 = (bf16[24,1024]{1,0:T(8,128)(2,1)S(1)}, bf16[24,1024]{1,0:T(8,128)(2,1)S(1)}, u32[]{:S(2)}, u32[]{:S(2)}) collective-permute-start(bf16[24,1024]{1,0:T(8,128)(2,1)S(1)} %get-tuple-element.32.acts_ref.refs_0_), channel_id=1, source_target_pairs={{0,3},{1,2},{2,1},{3,0},{4,7},{5,6},{6,5},{7,4},{8,11},{9,10},{10,... | collective-permute-start | bytes 147464 | tf_op jit(solution)/shard_map/ppermute | solution.py:46
  15.9 5.0 %collective-permute-start.6 = (bf16[24,1024]{1,0:T(8,128)(2,1)S(1)}, bf16[24,1024]{1,0:T(8,128)(2,1)S(1)}, u32[]{:S(2)}, u32[]{:S(2)}) collective-permute-start(bf16[24,1024]{1,0:T(8,128)(2,1)S(1)} %get-tuple-element.32.acts_ref.refs_0_), channel_id=1, source_target_pairs={{0,2},{1,3},{2,0},{3,1},{4,6},{5,7},{6,4},{7,5},{8,10},{9,11},{10,... | collective-permute-start | bytes 147464 | tf_op jit(solution)/shard_map/ppermute | solution.py:46
  15.9 5.0 %collective-permute-start.5 = (bf16[24,1024]{1,0:T(8,128)(2,1)S(1)}, bf16[24,1024]{1,0:T(8,128)(2,1)S(1)}, u32[]{:S(2)}, u32[]{:S(2)}) collective-permute-start(bf16[24,1024]{1,0:T(8,128)(2,1)S(1)} %get-tuple-element.32.acts_ref.refs_0_), channel_id=1, source_target_pairs={{0,1},{1,0},{2,3},{3,2},{4,5},{5,4},{6,7},{7,6},{8,9},{9,8},{10,11... | collective-permute-start | bytes 147464 | tf_op jit(solution)/shard_map/ppermute | solution.py:46
  22.2 1.4 %collective-permute-start.8 = (f32[24,1280]{1,0:T(8,128)S(1)}, f32[24,1280]{1,0:T(8,128)S(1)}, u32[]{:S(2)}, u32[]{:S(2)}) collective-permute-start(f32[24,1280]{1,0:T(8,128)S(1)} %recon_send.1), channel_id=1, source_target_pairs={{0,4},{4,0},{8,12},{12,8},{16,20},{20,16},{24,28},{28,24},{1,5},{5... | collective-permute-start | bytes 368648 | tf_op jit(solution)/shard_map/ppermute | solution.py:46
  23.7 5.4 %collective-permute-start.11 = (bf16[24,1280]{1,0:T(8,128)(2,1)S(1)}, bf16[24,1280]{1,0:T(8,128)(2,1)S(1)}, u32[]{:S(2)}, u32[]{:S(2)}) collective-permute-start(bf16[24,1280]{1,0:T(8,128)(2,1)S(1)} %pair_sum.1.refs_0_), channel_id=1, source_target_pairs={{0,24},{4,28},{8,16},{12,20},{16,8},{20,12},{24,0},{28,4},{1,25},{... | collective-permute-start | bytes 184328 | tf_op jit(solution)/shard_map/ppermute | solution.py:46
  25.2 5.1 %collective-permute-start.10 = (bf16[24,1280]{1,0:T(8,128)(2,1)S(1)}, bf16[24,1280]{1,0:T(8,128)(2,1)S(1)}, u32[]{:S(2)}, u32[]{:S(2)}) collective-permute-start(bf16[24,1280]{1,0:T(8,128)(2,1)S(1)} %pair_sum.1.refs_0_), channel_id=1, source_target_pairs={{0,16},{4,20},{8,24},{12,28},{16,0},{20,4},{24,8},{28,12},{1,17},{... | collective-permute-start | bytes 184328 | tf_op jit(solution)/shard_map/ppermute | solution.py:46
  26.4 4.2 %collective-permute-start.9 = (bf16[24,1280]{1,0:T(8,128)(2,1)S(1)}, bf16[24,1280]{1,0:T(8,128)(2,1)S(1)}, u32[]{:S(2)}, u32[]{:S(2)}) collective-permute-start(bf16[24,1280]{1,0:T(8,128)(2,1)S(1)} %pair_sum.1.refs_0_), channel_id=1, source_target_pairs={{0,8},{4,12},{8,0},{12,4},{16,24},{20,28},{24,16},{28,20},{1,9},{5... | collective-permute-start | bytes 184328 | tf_op jit(solution)/shard_map/ppermute | solution.py:46
  30.8 2.1 %collective-permute-start.12 = (bf16[32,1152]{1,0:T(8,128)(2,1)S(1)}, bf16[32,1152]{1,0:T(8,128)(2,1)S(1)}, u32[]{:S(2)}, u32[]{:S(2)}) collective-permute-start(bf16[32,1152]{1,0:T(8,128)(2,1)S(1)} %get-tuple-element.34.mine_ref), channel_id=1, source_target_pairs={{0,4},{4,0},{8,12},{12,8},{16,20},{20,16},{24,28},{28,24},{1,5},{5... | collective-permute-start | bytes 221192 | tf_op jit(solution)/shard_map/ppermute | solution.py:46
  35.5 10.0 %collective-permute-start.13 = (bf16[24,1152]{1,0:T(8,128)(2,1)S(1)}, bf16[24,1152]{1,0:T(8,128)(2,1)S(1)}, u32[]{:S(2)}, u32[]{:S(2)}) collective-permute-start(bf16[24,1152]{1,0:T(8,128)(2,1)S(1)} %get-tuple-element.46), channel_id=1, source_target_pairs={{0,1},{1,0},{2,3},{3,2},{4,5},{5,4},{6,7},{7,6},{8,9},{9,8},{10,11... | collective-permute-start | bytes 165896 | tf_op jit(solution)/shard_map/ppermute | solution.py:46
  36.3 9.3 %collective-permute-start.14 = (bf16[24,1152]{1,0:T(8,128)(2,1)S(1)}, bf16[24,1152]{1,0:T(8,128)(2,1)S(1)}, u32[]{:S(2)}, u32[]{:S(2)}) collective-permute-start(bf16[24,1152]{1,0:T(8,128)(2,1)S(1)} %get-tuple-element.47), channel_id=1, source_target_pairs={{0,2},{1,3},{2,0},{3,1},{4,6},{5,7},{6,4},{7,5},{8,10},{9,11},{10,... | collective-permute-start | bytes 165896 | tf_op jit(solution)/shard_map/ppermute | solution.py:46
  39.0 6.6 %collective-permute-start.15 = (bf16[24,1152]{1,0:T(8,128)(2,1)S(1)}, bf16[24,1152]{1,0:T(8,128)(2,1)S(1)}, u32[]{:S(2)}, u32[]{:S(2)}) collective-permute-start(bf16[24,1152]{1,0:T(8,128)(2,1)S(1)} %get-tuple-element.48), channel_id=1, source_target_pairs={{0,3},{1,2},{2,1},{3,0},{4,7},{5,6},{6,5},{7,4},{8,11},{9,10},{10,... | collective-permute-start | bytes 165896 | tf_op jit(solution)/shard_map/ppermute | solution.py:46

commit v4 on v3

--- a/solution.py
+++ b/solution.py
@@ -46,6 +46,10 @@
     return lax.ppermute(x, axis, [(i, i ^ bits) for i in range(size)])
 
 
+def exchange_order(size):
+    return (1, 3, 2) if size == 4 else tuple(range(1, size))
+
+
 def split3(value):
     high = value.astype(BF16)
     rest = value - high.astype(F32)
@@ -61,26 +65,24 @@
     return block.astype(BF16)
 
 
-def load_own(res_hbm, target_hbm, thr_hbm, out_ref, cutoff_ref, res_ref, target_ref, thr_ref, sems):
+def load_own(res_hbm, target_hbm, thr_hbm, res_ref, target_ref, cutoff_ref, thr_ref, sems):
     places = ((res_hbm, res_ref), (target_hbm, target_ref), (thr_hbm, thr_ref))
     copies = [pltpu.make_async_copy(*place, sems.at[i]) for i, place in enumerate(places)]
     for copy in copies:
         copy.start()
-    rows = res_ref.shape[0]
-    out_ref[...] = jnp.zeros_like(out_ref)
     for copy in copies:
         copy.wait()
-    out_ref[:rows] = res_ref[...]
-    out_ref[rows : 2 * rows] = target_ref[...]
     cutoff_ref[...] = (thr_ref[...].astype(F32) + 0.5) / 2048.0
 
 
-def pack(own_ref, res_ref, target_ref, out_ref):
-    height, rows = own_ref.shape[0], res_ref.shape[0]
-    out_ref[:height] = own_ref[...]
-    out_ref[height:] = jnp.zeros_like(own_ref)
-    out_ref[height : height + rows] = res_ref[...]
-    out_ref[height + rows : height + 2 * rows] = target_ref[...]
+def pack(res_ref, target_ref, res_got_ref, target_got_ref, out_ref):
+    rows, width = res_ref.shape
+    half = width // 2
+    low = lax.axis_index("feat") % 2 == 0
+    out_ref[...] = jnp.zeros_like(out_ref)
+    for start, res, target in ((0, res_ref, target_ref), (rows, res_got_ref, target_got_ref)):
+        out_ref[start : start + rows, :width] = res[...]
+        out_ref[start : start + rows, width:] = jnp.where(low, target[:, :half], target[:, half:])
 
 
 def stack(*refs):
@@ -96,13 +98,14 @@
     copy.wait()
 
 
-def gather_rows(rows, height, tokens, first, blocks):
+def gather_rows(rows, height, tokens, blocks):
     dims = (tokens, blocks.shape[0])
     token = lax.broadcasted_iota(jnp.int32, dims, 0)
     place = lax.broadcasted_iota(jnp.int32, dims, 1)
-    row = place % height - first
-    device = (place // height) ^ lax.axis_index("feat")
-    chosen = (row >= 0) & (row < rows) & (device * rows + row == token)
+    inner = place % height
+    second = (inner >= rows).astype(jnp.int32)
+    device = (place // height * 2 + second) ^ lax.axis_index("feat")
+    chosen = (inner < 2 * rows) & (device * rows + inner - second * rows == token)
     picked = jnp.dot(jnp.where(chosen, 1.0, 0.0).astype(BF16), blocks, preferred_element_type=F32)
     return picked.astype(BF16)
 
@@ -111,9 +114,10 @@
     *block_refs, enc_ref, cutoff_ref, x_ref, target_ref, acts_ref, gate_ref, sparse_ref, pen_ref = refs
     tokens = x_ref.shape[0]
     blocks = jnp.concatenate([ref[...] for ref in block_refs], axis=0)
-    x = gather_rows(rows, height, tokens, 0, blocks)
+    gathered = gather_rows(rows, height, tokens, blocks)
+    x = gathered[:, : x_ref.shape[1]]
     x_ref[...] = x
-    target_ref[...] = gather_rows(rows, height, tokens, rows, blocks)
+    target_ref[...] = gathered[:, x_ref.shape[1] :]
     preact = jnp.dot(x, enc_ref[...], preferred_element_type=F32)
     firing = preact > cutoff_ref[...]
     acts = jnp.where(firing, preact, 0.0).astype(BF16)
@@ -142,13 +146,13 @@
     total_ref[...] = total
 
 
-def recon_half(theirs, total_ref, pen_ref, dec_ref, *refs):
+def recon_half(theirs, order, total_ref, pen_ref, dec_ref, *refs):
     *acts, out_ref = refs
     me = lax.axis_index("layer")
     half = dec_ref.shape[2] // 2
     span = pl.ds(pl.multiple_of((lax.axis_index("feat") + theirs) % 2 * half, half), half)
     total = total_ref[:, span]
-    for k, acts_ref in enumerate(acts, 1):
+    for k, acts_ref in zip(order, acts):
         total = total + jnp.dot(acts_ref[...], dec_ref[me ^ k, :, span], preferred_element_type=F32)
     out_ref[:, :half] = total
     out_ref[:, half:] = jnp.broadcast_to(pen_ref[0:1, :], (total.shape[0], LANES))
@@ -184,12 +188,11 @@
 
 def error_half(rows, target_ref, *refs):
     *msgs, out_ref, own_ref, pen_ref = refs
-    tokens, half = target_ref.shape[0], target_ref.shape[1] // 2
+    tokens, half = target_ref.shape
     me = lax.axis_index("feat")
     total = sum_messages(msgs)
     recon = total[:, :half]
-    target = jnp.where(me % 2 == 0, target_ref[:, :half], target_ref[:, half:]).astype(F32)
-    error = recon - target
+    error = recon - target_ref[...].astype(F32)
     squares = jnp.sum(jnp.sum(error * error, axis=1, keepdims=True), axis=0, keepdims=True)
     narrow = recon.astype(BF16)
     own_ref[...] = jnp.dot(pick_rows(me, rows, tokens), narrow, preferred_element_type=F32)
@@ -213,16 +216,16 @@
     return act_grad(grad, dec_ref[source, :, span])
 
 
-def act_first(mine_ref, dec_ref, *outs):
+def act_first(order, mine_ref, dec_ref, *outs):
     tokens = outs[0].shape[0]
     me = lax.axis_index("layer")
-    for k, out_ref in enumerate(outs, 1):
+    for k, out_ref in zip(order, outs):
         out_ref[...] = act_half(mine_ref[:tokens, :], dec_ref, me ^ k, 0)
 
 
-def act_second(rows, count, mine_ref, got_ref, own_ref, pen_ref, dec_ref, *refs):
-    parts = refs[:count]
-    recon_ref, grad_ref, score_ref, *msgs = refs[count:]
+def act_second(rows, order, mine_ref, got_ref, pen_ref, dec_ref, *refs):
+    parts = refs[: len(order)]
+    grad_ref, score_ref, *msgs = refs[len(order) :]
     tokens, half = grad_ref.shape[0], grad_ref.shape[1] // 2
     low = lax.axis_index("feat") % 2 == 0
     me = lax.axis_index("layer")
@@ -234,22 +237,19 @@
     score = squares + 2.0 * ERROR_SCALE * PENALTY_WEIGHT * pen_ref[0:1, 0:1]
     score_ref[...] = jnp.broadcast_to(score, score_ref.shape)
     width = dec_ref.shape[1]
-    for k, (part_ref, msg) in enumerate(zip(parts, msgs), 1):
+    for k, part_ref, msg in zip(order, parts, msgs):
         msg[:, :width] = (part_ref[...] + act_half(got, dec_ref, me ^ k, 1)).astype(BF16)
         msg[:, width:] = spread3(score, (tokens, LANES))
     grad_ref[:, :half] = jnp.where(low, mine, got)
     grad_ref[:, half:] = jnp.where(low, got, mine)
-    own = own_ref[...]
-    recon_ref[:, :half] = jnp.where(low, own, extra)[:rows].astype(BF16)
-    recon_ref[:, half:] = jnp.where(low, extra, own)[:rows].astype(BF16)
-
-
-def write_decoder_grads(first, grad_ref, acts, out_hbm, buf, sems):
+
+
+def write_decoder_grads(order, grad_ref, acts, out_hbm, buf, sems):
     me = lax.axis_index("layer")
     block = buf.shape[1]
     steps = acts[0].shape[1] // block
     copies = []
-    for k, acts_ref in enumerate(acts, first):
+    for k, acts_ref in zip(order, acts):
         turned = acts_ref[...].T
         for i in range(steps):
             n = len(copies)
@@ -260,19 +260,35 @@
     return copies
 
 
-def first_grads(grad_ref, dec_ref, *refs):
-    *acts, out_hbm, part_ref, buf, sems = refs
-    copies = write_decoder_grads(0, grad_ref, acts, out_hbm, buf, sems)
+def first_grads(order, grad_ref, dec_ref, own_ref, got_ref, *refs):
+    *acts, out_hbm, recon_hbm, part_ref, buf, sems, recon_ref, recon_sem = refs
+    tokens, half = grad_ref.shape[0], grad_ref.shape[1] // 2
+    low = lax.axis_index("feat") % 2 == 0
+    own, extra = own_ref[...], got_ref[tokens:, :].astype(F32)
+    rows = recon_ref.shape[0]
+    recon_ref[:, :half] = jnp.where(low, own, extra)[:rows].astype(BF16)
+    recon_ref[:, half:] = jnp.where(low, extra, own)[:rows].astype(BF16)
+    copies = [pltpu.make_async_copy(recon_ref, recon_hbm, recon_sem)]
+    copies[0].start()
+    copies += write_decoder_grads(order, grad_ref, acts, out_hbm, buf, sems)
     part_ref[...] = act_grad(grad_ref[...], dec_ref[lax.axis_index("layer")])
     for copy in copies:
         copy.wait()
 
 
-def last_grads(count, first, last, grad_ref, x_ref, part_ref, gate_ref, sparse_ref, score_ref, *refs):
-    *rest, _, dec_hbm, enc_hbm, loss_ref, dec_buf, dec_sems, enc_buf, enc_sems = refs
-    acts, msgs = rest[:last], rest[last:]
-    copies = write_decoder_grads(first, grad_ref, acts, dec_hbm, dec_buf, dec_sems)
+def last_grads(count, order, grad_ref, x_ref, part_ref, gate_ref, sparse_ref, score_ref, *refs):
+    *rest, _, dec_hbm, enc_hbm, loss_hbm, dec_buf, dec_sems, enc_buf, enc_sems, loss_ref, loss_sem = refs
+    acts, msgs = rest[: len(order)], rest[len(order) :]
+    copies = write_decoder_grads(order, grad_ref, acts, dec_hbm, dec_buf, dec_sems)
     width = part_ref.shape[1]
+    scores = [score_ref[0:1, 0:1]]
+    for msg in msgs:
+        scores.append(jnp.sum(msg[0:1, width:].astype(F32), axis=1, keepdims=True))
+    while len(scores) > 1:
+        scores = [scores[i] + scores[i + 1] for i in range(0, len(scores), 2)]
+    loss_ref[...] = scores[0] / count
+    copies.append(pltpu.make_async_copy(loss_ref, loss_hbm, loss_sem))
+    copies[-1].start()
     total = part_ref[...]
     for msg in msgs:
         total = total + msg[:, :width].astype(F32)
@@ -284,12 +300,6 @@
         enc_buf[i] = jnp.dot(turned[span], pre, preferred_element_type=F32).astype(BF16)
         copies.append(pltpu.make_async_copy(enc_buf.at[i], enc_hbm.at[pl.ds(i * block, block)], enc_sems.at[i]))
         copies[-1].start()
-    scores = [score_ref[0:1, 0:1]]
-    for msg in msgs:
-        scores.append(jnp.sum(msg[0:1, width:].astype(F32), axis=1, keepdims=True))
-    while len(scores) > 1:
-        scores = [scores[i] + scores[i + 1] for i in range(0, len(scores), 2)]
-    loss_ref[...] = scores[0] / count
     for copy in copies:
         copy.wait()
 
@@ -304,16 +314,17 @@
 
     height = -(-2 * rows // 8) * 8
     mine = (residual_in[0], target[0])
-    own, cutoff = call(
+    *own, cutoff = call(
         load_own,
-        [shape((height, width), BF16), shape((1, features), F32)],
+        [shape((rows, width), BF16)] * 2 + [shape((1, features), F32)],
         [in_hbm(part) for part in (*mine, thresholds)],
         "load_own",
-        scratch=[pltpu.VMEM((rows, width), BF16)] * 2 + [pltpu.VMEM((1, features), jnp.int32), pltpu.SemaphoreType.DMA((3,))],
+        scratch=[pltpu.VMEM((1, features), jnp.int32), pltpu.SemaphoreType.DMA((3,))],
         in_specs=[ANY] * 3,
         bytes_accessed=2 * width * features,
     )
-    (block,) = call(pack, [shape((2 * height, width), BF16)], (own, *(swap(part, "feat", 1) for part in mine)), "pack")
+    got = [swap(part, "feat", 1) for part in mine]
+    (block,) = call(pack, [shape((height, width + half), BF16)], (*own, *got), "pack")
     (encoder,) = call(
         fetch,
         [shape((width, features), BF16)],
@@ -329,18 +340,18 @@
         blocks = [block] + [swap(block, "feat", k) for k in pair]
         bit <<= len(pair) // 2 + 1
         if bit < feats:
-            (block,) = call(stack, [shape((bit * height, width), BF16)], blocks, "stack")
+            (block,) = call(stack, [shape((bit // 2 * height, width + half), BF16)], blocks, "stack")
     x, targets, acts, gate, sparse, pen = call(
         functools.partial(encode, rows, height),
-        [shape((tokens, width), BF16)] * 2
+        [shape((tokens, width), BF16), shape((tokens, half), BF16)]
         + [shape((tokens, features), BF16), shape((tokens, features), F32), shape((tokens, features), F32), shape((8, LANES), F32)],
         (*blocks, encoder, cutoff),
         "encode",
-        limit=48,
         flops=2 * tokens * width * features,
         bytes_accessed=2 * width * features,
     )
-    others = [swap(acts, "layer", k) for k in range(1, layers)]
+    order = exchange_order(layers)
+    others = [swap(acts, "layer", k) for k in order]
     pieces = max(1, features // 256)
     (total,) = call(
         recon_own,
@@ -355,7 +366,7 @@
     )
     send, keep = (
         call(
-            functools.partial(recon_half, theirs),
+            functools.partial(recon_half, theirs, order),
             [shape((tokens, half + LANES), F32)],
             (total, pen, decoder, *others),
             name,
@@ -378,40 +389,42 @@
         (targets, *msgs),
         "error_half",
     )
+    back = (1, 3, 2) if layers == 4 else order
     parts = call(
-        act_first,
+        functools.partial(act_first, back),
         [shape((tokens, features), F32)] * (layers - 1),
         (mine, decoder),
         "act_first",
         flops=tokens * width * features * (sources - 1),
         bytes_accessed=(sources - 1) * width * features,
     )
-    recon, grad, score, *sends = call(
-        functools.partial(act_second, rows, layers - 1),
-        [shape((rows, width), BF16), shape((tokens, width), BF16), shape((8, LANES), F32)]
-        + [shape((tokens, features + LANES), BF16)] * (layers - 1),
-        (mine, swap(mine, "feat", 1), own_rows, pen_all, decoder, *parts),
+    theirs = swap(mine, "feat", 1)
+    grad, score, *sends = call(
+        functools.partial(act_second, rows, back),
+        [shape((tokens, width), BF16), shape((8, LANES), F32)] + [shape((tokens, features + LANES), BF16)] * (layers - 1),
+        (mine, theirs, pen_all, decoder, *parts),
         "act_second",
         flops=tokens * width * features * (sources - 1),
         bytes_accessed=(sources - 1) * width * features,
     )
-    gots = [swap(sends[k - 1], "layer", k) for k in range(1, layers)]
+    gots = [swap(sends[back.index(k)], "layer", k) for k in (2, 3, 1)]
     first, steps, block = sources - 1, max(1, features // 128), 128
     last = sources - first
-    dec_grad, part = call(
-        first_grads,
-        [shape((sources, features, width), BF16), shape((tokens, features), F32)],
-        (grad, decoder, acts, *others[: first - 1]),
+    dec_grad, recon, part = call(
+        functools.partial(first_grads, (0, *order[: first - 1])),
+        [shape((sources, features, width), BF16), shape((rows, width), BF16), shape((tokens, features), F32)],
+        (grad, decoder, own_rows, theirs, acts, *others[: first - 1]),
         "first_grads",
-        scratch=[pltpu.VMEM((first * steps, features // steps, width), BF16), pltpu.SemaphoreType.DMA((first * steps,))],
+        scratch=[pltpu.VMEM((first * steps, features // steps, width), BF16), pltpu.SemaphoreType.DMA((first * steps,))]
+        + [pltpu.VMEM((rows, width), BF16), pltpu.SemaphoreType.DMA(())],
         limit=24,
-        out_specs=[ANY, WHOLE],
+        out_specs=[ANY, ANY, WHOLE],
         flops=2 * tokens * width * features * (first + 1),
         bytes_accessed=2 * first * width * features,
     )
     args = (grad, x, part, gate, sparse, score, *others[first - 1 :], *gots, dec_grad)
     dec_grad, enc_grad, loss = call(
-        functools.partial(last_grads, layers * tokens * width, first, last),
+        functools.partial(last_grads, layers * tokens * width, order[first - 1 :]),
         [shape((sources, features, width), BF16), shape((width, features), BF16), shape((1, 1), F32)],
         args,
         "last_grads",
@@ -420,9 +433,11 @@
             pltpu.SemaphoreType.DMA((last * steps,)),
             pltpu.VMEM((width // block, block, features), BF16),
             pltpu.SemaphoreType.DMA((width // block,)),
+            pltpu.VMEM((1, 1), F32),
+            pltpu.SemaphoreType.DMA(()),
         ],
         in_specs=[WHOLE] * (len(args) - 1) + [ANY],
-        out_specs=[ANY, ANY, WHOLE],
+        out_specs=[ANY] * 3,
         limit=24,
         aliases={len(args) - 1: 0},
         flops=2 * tokens * width * features * (last + 1),

time: 50.4 us -> 48.5 us (0.962)
  Pallas kernels: 25.5 us -> 24.5 us
  starting transfers between devices: 17.3 us -> 16.3 us
    ppermute x16, starting transfers between devices: 17.3 us -> 16.3 us  [swap(): return lax.ppermute(x, axis, [(i, i ^ bits) for i in range(size)])]
    pallas_call x13, Pallas kernels: 25.5 us -> 24.5 us  [call(): pl.pallas_call(body, out_shape=outs, in_specs=in_specs or [WHOLE] * len(a...]
  transfers between devices with their start and end apart: 16 -> 16, of which waited for: 8 -> 7; matrix products, arithmetic and copies ran while one was open for 0% -> 0% of each run, Pallas kernels for 31% -> 32%
where the time goes in v4:
time: 48.5 us; the launch traced here: 48.3 us
  Pallas kernels  24.5 us (51%)
  starting transfers between devices  16.3 us (34%)
  waiting for transfers between devices  6.81 us (14%)
  between operations  0.77 us (2%)
    pallas_call x13, Pallas kernels, call(): pl.pallas_call(body, out_shape=outs, in_specs=in_specs or [WHOLE] * len(a...  24.5 us
    ppermute x16, starting transfers between devices, swap(): return lax.ppermute(x, axis, [(i, i ^ bits) for i in range(size)])  16.3 us
    ppermute x16, waiting for transfers between devices, swap(): return lax.ppermute(x, axis, [(i, i ^ bits) for i in range(size)])  6.81 us
  transfers between devices with their start and end apart: 16, of which 7 were waited for; matrix products, arithmetic and copies ran while one was open for 0% of the time, Pallas kernels for 32%

profile of v4, /device:TPU:0, one launch (start us, length us, event | category | flops | bytes accessed | tf_op | source)
XLA Modules:
  0.0 48.3 jit_solution(9433703409958426749)
XLA Ops:
  0.6 0.5 %collective-permute-start = (bf16[3,2304]{1,0:T(4,128)(2,1)}, bf16[3,2304]{1,0:T(4,128)(2,1)S(1)}, u32[]{:S(2)}, u32[]{:S(2)}) collective-permute-start(bf16[3,2304]{1,0:T(4,128)(2,1)} %bitcast.18), channel_id=1, source_target_pairs={{0,4},{4,0},{8,12},{12,8},{16,20},{20,16},{24,28},{28,24},{1,5},{5... | collective-permute-start | bytes 41480 | tf_op jit(solution)/shard_map/ppermute | solution.py:46
  1.2 1.0 %load_own.1 = (bf16[3,2304]{1,0:T(4,128)(2,1)S(1)}, bf16[3,2304]{1,0:T(4,128)(2,1)S(1)}, f32[1,1024]{1,0:T(1,128)S(1)}) custom-call(bf16[3,2304]{1,0:T(4,128)(2,1)} %bitcast.19, bf16[3,2304]{1,0:T(4,128)(2,1)} %bitcast.21, s32[1,1024]{1,0:T(1,128)} %thr_hbm.1), custom_call_target="tpu_custom_call" | custom-call | bytes 4718592 | tf_op jit(solution)/shard_map/load_own/pallas_call | solution.py:31
  2.6 3.7 %collective-permute-start.4 = (bf16[8,3456]{1,0:T(8,128)(2,1)S(1)}, bf16[8,3456]{1,0:T(8,128)(2,1)S(1)}, u32[]{:S(2)}, u32[]{:S(2)}) collective-permute-start(bf16[8,3456]{1,0:T(8,128)(2,1)S(1)} %pack.1._.refs_0_), channel_id=1, source_target_pairs={{0,24},{4,28},{8,16},{12,20},{16,8},{20,12},{24,0},{28,4},{1,25},{... | collective-permute-start | bytes 165896 | tf_op jit(solution)/shard_map/ppermute | solution.py:46
  6.9 2.3 %fetch.1.refs_4_ = bf16[2304,1024]{1,0:T(8,128)(2,1)S(1)} custom-call(bf16[8,3456]{1,0:T(8,128)(2,1)S(1)} %pack.1._.refs_0_, bf16[2304,1024]{1,0:T(8,128)(2,1)} %bitcast.17), custom_call_target="tpu_custom_call" | custom-call | bytes 9437184 | tf_op jit(solution)/shard_map/fetch/pallas_call | solution.py:31
  9.3 1.1 %collective-permute-done.3.refs_2_ = bf16[8,3456]{1,0:T(8,128)(2,1)S(1)} collective-permute-done((bf16[8,3456]{1,0:T(8,128)(2,1)S(1)}, bf16[8,3456]{1,0:T(8,128)(2,1)S(1)}, u32[]{:S(2)}, u32[]{:S(2)}) %collective-permute-start.3) | collective-permute-done | bytes 55328 | tf_op jit(solution)/shard_map/ppermute | solution.py:46
  10.9 1.1 %encode.1 = (bf16[24,2304]{1,0:T(8,128)(2,1)S(1)}, bf16[24,1152]{1,0:T(8,128)(2,1)S(1)}, bf16[24,1024]{1,0:T(8,128)(2,1)S(1)}, f32[24,1024]{1,0:T(8,128)S(1)}, f...) custom-call(bf16[8,3456]{1,0:T(8,128)(2,1)S(1)} %pack.1._.refs_0_, bf16[8,3456]{1,0:T(8,128)(2,1)S(1)} %collective-permute-done.2.refs_1_, ...), custom_call_target="tpu_custom_call" | custom-call | flops 113246208 | bytes 4718592 | tf_op jit(solution)/shard_map/encode/pallas_call | solution.py:31
  12.1 2.6 %collective-permute-start.7 = (bf16[24,1024]{1,0:T(8,128)(2,1)S(1)}, bf16[24,1024]{1,0:T(8,128)(2,1)S(1)}, u32[]{:S(2)}, u32[]{:S(2)}) collective-permute-start(bf16[24,1024]{1,0:T(8,128)(2,1)S(1)} %get-tuple-element.34.acts_ref.refs_0_), channel_id=1, source_target_pairs={{0,2},{1,3},{2,0},{3,1},{4,6},{5,7},{6,4},{7,5},{8,10},{9,11},{10,... | collective-permute-start | bytes 147464 | tf_op jit(solution)/shard_map/ppermute | solution.py:46
  14.7 1.3 %collective-permute-start.6 = (bf16[24,1024]{1,0:T(8,128)(2,1)S(1)}, bf16[24,1024]{1,0:T(8,128)(2,1)S(1)}, u32[]{:S(2)}, u32[]{:S(2)}) collective-permute-start(bf16[24,1024]{1,0:T(8,128)(2,1)S(1)} %get-tuple-element.34.acts_ref.refs_0_), channel_id=1, source_target_pairs={{0,3},{1,2},{2,1},{3,0},{4,7},{5,6},{6,5},{7,4},{8,11},{9,10},{10,... | collective-permute-start | bytes 147464 | tf_op jit(solution)/shard_map/ppermute | solution.py:46
  16.2 2.7 %recon_own.1.total_ref = f32[24,2304]{1,0:T(8,128)S(1)} custom-call(bf16[24,1024]{1,0:T(8,128)(2,1)S(1)} %get-tuple-element.34.acts_ref.refs_0_, bf16[4,1024,2304]{2,1,0:T(8,128)(2,1)} %bitcast.10), custom_call_target="tpu_custom_call" | custom-call | flops 113246208 | bytes 4718592 | tf_op jit(solution)/shard_map/recon_own/pallas_call | solution.py:31
  18.9 1.7 %collective-permute-done.6.refs_1_.refs_2_ = bf16[24,1024]{1,0:T(8,128)(2,1)S(1)} collective-permute-done((bf16[24,1024]{1,0:T(8,128)(2,1)S(1)}, bf16[24,1024]{1,0:T(8,128)(2,1)S(1)}, u32[]{:S(2)}, u32[]{:S(2)}) %collective-permute-start.6) | collective-permute-done | bytes 49184 | tf_op jit(solution)/shard_map/ppermute | solution.py:46
  20.6 1.3 %recon_send.1 = f32[24,1280]{1,0:T(8,128)S(1)} custom-call(f32[24,2304]{1,0:T(8,128)S(1)} %recon_own.1.total_ref, f32[8,128]{1,0:T(8,128)S(1)} %get-tuple-element.35.pen_ref, bf16[4,1024,2304]{2,1,0:T(8,128)(2,1)S(1)} %bitcast.11, bf16[24,1024]{1,0:T(8,128)(2,1)S(1)} %collective-permute-done.5.refs_0_.refs_1_, ...), custom_call_target="tpu_custom_call" | custom-call | flops 169869312 | bytes 7077888 | tf_op jit(solution)/shard_map/recon_send/pallas_call | solution.py:31
  22.0 1.3 %recon_keep.1.keep_ref = f32[24,1280]{1,0:T(8,128)S(1)} custom-call(f32[24,2304]{1,0:T(8,128)S(1)} %recon_own.1.total_ref, f32[8,128]{1,0:T(8,128)S(1)} %get-tuple-element.35.pen_ref, bf16[4,1024,2304]{2,1,0:T(8,128)(2,1)S(1)} %bitcast.12, bf16[24,1024]{1,0:T(8,128)(2,1)S(1)} %collective-permute-done.5.refs_0_.refs_1_, ...), custom_call_target="tpu_custom_call" | custom-call | flops 169869312 | bytes 7077888 | tf_op jit(solution)/shard_map/recon_keep/pallas_call | solution.py:31
  23.4 1.5 %collective-permute-start.11 = (bf16[24,1280]{1,0:T(8,128)(2,1)S(1)}, bf16[24,1280]{1,0:T(8,128)(2,1)S(1)}, u32[]{:S(2)}, u32[]{:S(2)}) collective-permute-start(bf16[24,1280]{1,0:T(8,128)(2,1)S(1)} %pair_sum.1.refs_0_), channel_id=1, source_target_pairs={{0,24},{4,28},{8,16},{12,20},{16,8},{20,12},{24,0},{28,4},{1,25},{... | collective-permute-start | bytes 184328 | tf_op jit(solution)/shard_map/ppermute | solution.py:46
  24.9 0.6 %collective-permute-start.10 = (bf16[24,1280]{1,0:T(8,128)(2,1)S(1)}, bf16[24,1280]{1,0:T(8,128)(2,1)S(1)}, u32[]{:S(2)}, u32[]{:S(2)}) collective-permute-start(bf16[24,1280]{1,0:T(8,128)(2,1)S(1)} %pair_sum.1.refs_0_), channel_id=1, source_target_pairs={{0,16},{4,20},{8,24},{12,28},{16,0},{20,4},{24,8},{28,12},{1,17},{... | collective-permute-start | bytes 184328 | tf_op jit(solution)/shard_map/ppermute | solution.py:46
  25.6 1.4 %collective-permute-start.9 = (bf16[24,1280]{1,0:T(8,128)(2,1)S(1)}, bf16[24,1280]{1,0:T(8,128)(2,1)S(1)}, u32[]{:S(2)}, u32[]{:S(2)}) collective-permute-start(bf16[24,1280]{1,0:T(8,128)(2,1)S(1)} %pair_sum.1.refs_0_), channel_id=1, source_target_pairs={{0,8},{4,12},{8,0},{12,4},{16,24},{20,28},{24,16},{28,20},{1,9},{5... | collective-permute-start | bytes 184328 | tf_op jit(solution)/shard_map/ppermute | solution.py:46
  26.9 1.9 %collective-permute-done.11.refs_3_ = bf16[24,1280]{1,0:T(8,128)(2,1)S(1)} collective-permute-done((bf16[24,1280]{1,0:T(8,128)(2,1)S(1)}, bf16[24,1280]{1,0:T(8,128)(2,1)S(1)}, u32[]{:S(2)}, u32[]{:S(2)}) %collective-permute-start.11) | collective-permute-done | bytes 61472 | tf_op jit(solution)/shard_map/ppermute | solution.py:46
  28.8 1.2 %collective-permute-done.10.refs_2_ = bf16[24,1280]{1,0:T(8,128)(2,1)S(1)} collective-permute-done((bf16[24,1280]{1,0:T(8,128)(2,1)S(1)}, bf16[24,1280]{1,0:T(8,128)(2,1)S(1)}, u32[]{:S(2)}, u32[]{:S(2)}) %collective-permute-start.10) | collective-permute-done | bytes 61472 | tf_op jit(solution)/shard_map/ppermute | solution.py:46
  30.4 2.0 %act_first.1 = (f32[24,1024]{1,0:T(8,128)S(1)}, f32[24,1024]{1,0:T(8,128)S(1)}, f32[24,1024]{1,0:T(8,128)S(1)}) custom-call(bf16[32,1152]{1,0:T(8,128)(2,1)S(1)} %get-tuple-element.36.mine_ref, bf16[4,1024,2304]{2,1,0:T(8,128)(2,1)S(1)} %bitcast.13), custom_call_target="tpu_custom_call" | custom-call | flops 169869312 | bytes 7077888 | tf_op jit(solution)/shard_map/act_first/pallas_call | solution.py:31
  32.4 2.1 %act_second.1 = (bf16[24,2304]{1,0:T(8,128)(2,1)S(1)}, f32[8,128]{1,0:T(8,128)S(1)}, bf16[24,1152]{1,0:T(8,128)(2,1)S(1)}, bf16[24,1152]{1,0:T(8,128)(2,1)S(1)}, bf16[24,1152]{1,0:T(8,128)(2,1)S(1)}) custom-call(bf16[32,1152]{1,0:T(8,128)(2,1)S(1)} %get-tuple-element.36.mine_ref, bf16[32,1152]{1,0:T(8,128)(2,1)S(1)} %collective-permute-done.12.got_ref, ...), custom_call_target="tpu_custom_call" | custom-call | flops 169869312 | bytes 7077888 | tf_op jit(solution)/shard_map/act_second/pallas_call | solution.py:31
  34.5 1.4 %collective-permute-start.13 = (bf16[24,1152]{1,0:T(8,128)(2,1)S(1)}, bf16[24,1152]{1,0:T(8,128)(2,1)S(1)}, u32[]{:S(2)}, u32[]{:S(2)}) collective-permute-start(bf16[24,1152]{1,0:T(8,128)(2,1)S(1)} %get-tuple-element.48), channel_id=1, source_target_pairs={{0,2},{1,3},{2,0},{3,1},{4,6},{5,7},{6,4},{7,5},{8,10},{9,11},{10,... | collective-permute-start | bytes 165896 | tf_op jit(solution)/shard_map/ppermute | solution.py:46
  35.9 1.1 %collective-permute-start.14 = (bf16[24,1152]{1,0:T(8,128)(2,1)S(1)}, bf16[24,1152]{1,0:T(8,128)(2,1)S(1)}, u32[]{:S(2)}, u32[]{:S(2)}) collective-permute-start(bf16[24,1152]{1,0:T(8,128)(2,1)S(1)} %get-tuple-element.49), channel_id=1, source_target_pairs={{0,3},{1,2},{2,1},{3,0},{4,7},{5,6},{6,5},{7,4},{8,11},{9,10},{10,... | collective-permute-start | bytes 165896 | tf_op jit(solution)/shard_map/ppermute | solution.py:46
  37.0 1.0 %collective-permute-start.15 = (bf16[24,1152]{1,0:T(8,128)(2,1)S(1)}, bf16[24,1152]{1,0:T(8,128)(2,1)S(1)}, u32[]{:S(2)}, u32[]{:S(2)}) collective-permute-start(bf16[24,1152]{1,0:T(8,128)(2,1)S(1)} %get-tuple-element.50), channel_id=1, source_target_pairs={{0,1},{1,0},{2,3},{3,2},{4,5},{5,4},{6,7},{7,6},{8,9},{9,8},{10,11... | collective-permute-start | bytes 165896 | tf_op jit(solution)/shard_map/ppermute | solution.py:46
  38.0 6.1 %first_grads.1 = (bf16[4,1024,2304]{2,1,0:T(8,128)(2,1)}, bf16[3,2304]{1,0:T(4,128)(2,1)}, f32[24,1024]{1,0:T(8,128)S(1)}) custom-call(bf16[24,2304]{1,0:T(8,128)(2,1)S(1)} %get-tuple-element.41.grad_ref, bf16[4,1024,2304]{2,1,0:T(8,128)(2,1)S(1)} %bitcast.15, f32[8,1152]{1,0:T(8,128)S(1)} %get-tuple-element.43.own_ref, ...), custom_call_target="tpu_custom_call" | custom-call | flops 452984832 | bytes 14155776 | tf_op jit(solution)/shard_map/first_grads/pallas_call | solution.py:31
  44.2 4.2 %last_grads.1 = (bf16[4,1024,2304]{2,1,0:T(8,128)(2,1)}, bf16[2304,1024]{1,0:T(8,128)(2,1)}, f32[1,1]{1,0:T(1,128)}) custom-call(bf16[24,2304]{1,0:T(8,128)(2,1)S(1)} %get-tuple-element.41.grad_ref, bf16[24,2304]{1,0:T(8,128)(2,1)S(1)} %get-tuple-element.42.x_ref, f32[24,1024]{1,0:T(8,128)S(1)} %get-tuple-element.44.part_ref, ...), custom_call_target="tpu_custom_call", output_to_operand_aliasing={{0}: (10, {})} | custom-call | flops 226492416 | bytes 9437184 | tf_op jit(solution)/shard_map/last_grads/pallas_call | solution.py:31
  (23 shorter events, 2.3 us)
Async XLA Ops:
  0.6 20.0 %copy-start = (bf16[4,1,1024,2304]{3,2,1,0:T(8,128)(2,1)S(1)}, bf16[4,1,1024,2304]{3,2,1,0:T(8,128)(2,1)}, u32[]{:S(2)}) copy-start(bf16[4,1,1024,2304]{3,2,1,0:T(8,128)(2,1)} %param.8) | copy-start | bytes 56623108
  0.6 1.6 %collective-permute-start = (bf16[3,2304]{1,0:T(4,128)(2,1)}, bf16[3,2304]{1,0:T(4,128)(2,1)S(1)}, u32[]{:S(2)}, u32[]{:S(2)}) collective-permute-start(bf16[3,2304]{1,0:T(4,128)(2,1)} %bitcast.18), channel_id=1, source_target_pairs={{0,4},{4,0},{8,12},{12,8},{16,20},{20,16},{24,28},{28,24},{1,5},{5... | collective-permute-start | bytes 41480 | tf_op jit(solution)/shard_map/ppermute | solution.py:46
  1.2 1.4 %collective-permute-start.1 = (bf16[3,2304]{1,0:T(4,128)(2,1)}, bf16[3,2304]{1,0:T(4,128)(2,1)S(1)}, u32[]{:S(2)}, u32[]{:S(2)}) collective-permute-start(bf16[3,2304]{1,0:T(4,128)(2,1)} %bitcast.20), channel_id=1, source_target_pairs={{0,4},{4,0},{8,12},{12,8},{16,20},{20,16},{24,28},{28,24},{1,5},{5... | collective-permute-start | bytes 41480 | tf_op jit(solution)/shard_map/ppermute | solution.py:46
  2.6 6.7 %collective-permute-start.4 = (bf16[8,3456]{1,0:T(8,128)(2,1)S(1)}, bf16[8,3456]{1,0:T(8,128)(2,1)S(1)}, u32[]{:S(2)}, u32[]{:S(2)}) collective-permute-start(bf16[8,3456]{1,0:T(8,128)(2,1)S(1)} %pack.1._.refs_0_), channel_id=1, source_target_pairs={{0,24},{4,28},{8,16},{12,20},{16,8},{20,12},{24,0},{28,4},{1,25},{... | collective-permute-start | bytes 165896 | tf_op jit(solution)/shard_map/ppermute | solution.py:46
  6.3 4.2 %collective-permute-start.3 = (bf16[8,3456]{1,0:T(8,128)(2,1)S(1)}, bf16[8,3456]{1,0:T(8,128)(2,1)S(1)}, u32[]{:S(2)}, u32[]{:S(2)}) collective-permute-start(bf16[8,3456]{1,0:T(8,128)(2,1)S(1)} %pack.1._.refs_0_), channel_id=1, source_target_pairs={{0,16},{4,20},{8,24},{12,28},{16,0},{20,4},{24,8},{28,12},{1,17},{... | collective-permute-start | bytes 165896 | tf_op jit(solution)/shard_map/ppermute | solution.py:46
  6.8 4.2 %collective-permute-start.2 = (bf16[8,3456]{1,0:T(8,128)(2,1)S(1)}, bf16[8,3456]{1,0:T(8,128)(2,1)S(1)}, u32[]{:S(2)}, u32[]{:S(2)}) collective-permute-start(bf16[8,3456]{1,0:T(8,128)(2,1)S(1)} %pack.1._.refs_0_), channel_id=1, source_target_pairs={{0,8},{4,12},{8,0},{12,4},{16,24},{20,28},{24,16},{28,20},{1,9},{5... | collective-permute-start | bytes 165896 | tf_op jit(solution)/shard_map/ppermute | solution.py:46
  12.1 6.9 %collective-permute-start.7 = (bf16[24,1024]{1,0:T(8,128)(2,1)S(1)}, bf16[24,1024]{1,0:T(8,128)(2,1)S(1)}, u32[]{:S(2)}, u32[]{:S(2)}) collective-permute-start(bf16[24,1024]{1,0:T(8,128)(2,1)S(1)} %get-tuple-element.34.acts_ref.refs_0_), channel_id=1, source_target_pairs={{0,2},{1,3},{2,0},{3,1},{4,6},{5,7},{6,4},{7,5},{8,10},{9,11},{10,... | collective-permute-start | bytes 147464 | tf_op jit(solution)/shard_map/ppermute | solution.py:46
  14.7 6.0 %collective-permute-start.6 = (bf16[24,1024]{1,0:T(8,128)(2,1)S(1)}, bf16[24,1024]{1,0:T(8,128)(2,1)S(1)}, u32[]{:S(2)}, u32[]{:S(2)}) collective-permute-start(bf16[24,1024]{1,0:T(8,128)(2,1)S(1)} %get-tuple-element.34.acts_ref.refs_0_), channel_id=1, source_target_pairs={{0,3},{1,2},{2,1},{3,0},{4,7},{5,6},{6,5},{7,4},{8,11},{9,10},{10,... | collective-permute-start | bytes 147464 | tf_op jit(solution)/shard_map/ppermute | solution.py:46
  16.0 4.6 %collective-permute-start.5 = (bf16[24,1024]{1,0:T(8,128)(2,1)S(1)}, bf16[24,1024]{1,0:T(8,128)(2,1)S(1)}, u32[]{:S(2)}, u32[]{:S(2)}) collective-permute-start(bf16[24,1024]{1,0:T(8,128)(2,1)S(1)} %get-tuple-element.34.acts_ref.refs_0_), channel_id=1, source_target_pairs={{0,1},{1,0},{2,3},{3,2},{4,5},{5,4},{6,7},{7,6},{8,9},{9,8},{10,11... | collective-permute-start | bytes 147464 | tf_op jit(solution)/shard_map/ppermute | solution.py:46
  21.9 1.4 %collective-permute-start.8 = (f32[24,1280]{1,0:T(8,128)S(1)}, f32[24,1280]{1,0:T(8,128)S(1)}, u32[]{:S(2)}, u32[]{:S(2)}) collective-permute-start(f32[24,1280]{1,0:T(8,128)S(1)} %recon_send.1), channel_id=1, source_target_pairs={{0,4},{4,0},{8,12},{12,8},{16,20},{20,16},{24,28},{28,24},{1,5},{5... | collective-permute-start | bytes 368648 | tf_op jit(solution)/shard_map/ppermute | solution.py:46
  23.4 5.4 %collective-permute-start.11 = (bf16[24,1280]{1,0:T(8,128)(2,1)S(1)}, bf16[24,1280]{1,0:T(8,128)(2,1)S(1)}, u32[]{:S(2)}, u32[]{:S(2)}) collective-permute-start(bf16[24,1280]{1,0:T(8,128)(2,1)S(1)} %pair_sum.1.refs_0_), channel_id=1, source_target_pairs={{0,24},{4,28},{8,16},{12,20},{16,8},{20,12},{24,0},{28,4},{1,25},{... | collective-permute-start | bytes 184328 | tf_op jit(solution)/shard_map/ppermute | solution.py:46
  24.9 5.1 %collective-permute-start.10 = (bf16[24,1280]{1,0:T(8,128)(2,1)S(1)}, bf16[24,1280]{1,0:T(8,128)(2,1)S(1)}, u32[]{:S(2)}, u32[]{:S(2)}) collective-permute-start(bf16[24,1280]{1,0:T(8,128)(2,1)S(1)} %pair_sum.1.refs_0_), channel_id=1, source_target_pairs={{0,16},{4,20},{8,24},{12,28},{16,0},{20,4},{24,8},{28,12},{1,17},{... | collective-permute-start | bytes 184328 | tf_op jit(solution)/shard_map/ppermute | solution.py:46
  25.6 4.6 %collective-permute-start.9 = (bf16[24,1280]{1,0:T(8,128)(2,1)S(1)}, bf16[24,1280]{1,0:T(8,128)(2,1)S(1)}, u32[]{:S(2)}, u32[]{:S(2)}) collective-permute-start(bf16[24,1280]{1,0:T(8,128)(2,1)S(1)} %pair_sum.1.refs_0_), channel_id=1, source_target_pairs={{0,8},{4,12},{8,0},{12,4},{16,24},{20,28},{24,16},{28,20},{1,9},{5... | collective-permute-start | bytes 184328 | tf_op jit(solution)/shard_map/ppermute | solution.py:46
  30.3 2.1 %collective-permute-start.12 = (bf16[32,1152]{1,0:T(8,128)(2,1)S(1)}, bf16[32,1152]{1,0:T(8,128)(2,1)S(1)}, u32[]{:S(2)}, u32[]{:S(2)}) collective-permute-start(bf16[32,1152]{1,0:T(8,128)(2,1)S(1)} %get-tuple-element.36.mine_ref), channel_id=1, source_target_pairs={{0,4},{4,0},{8,12},{12,8},{16,20},{20,16},{24,28},{28,24},{1,5},{5... | collective-permute-start | bytes 221192 | tf_op jit(solution)/shard_map/ppermute | solution.py:46
  34.5 9.7 %collective-permute-start.13 = (bf16[24,1152]{1,0:T(8,128)(2,1)S(1)}, bf16[24,1152]{1,0:T(8,128)(2,1)S(1)}, u32[]{:S(2)}, u32[]{:S(2)}) collective-permute-start(bf16[24,1152]{1,0:T(8,128)(2,1)S(1)} %get-tuple-element.48), channel_id=1, source_target_pairs={{0,2},{1,3},{2,0},{3,1},{4,6},{5,7},{6,4},{7,5},{8,10},{9,11},{10,... | collective-permute-start | bytes 165896 | tf_op jit(solution)/shard_map/ppermute | solution.py:46
  35.9 8.2 %collective-permute-start.14 = (bf16[24,1152]{1,0:T(8,128)(2,1)S(1)}, bf16[24,1152]{1,0:T(8,128)(2,1)S(1)}, u32[]{:S(2)}, u32[]{:S(2)}) collective-permute-start(bf16[24,1152]{1,0:T(8,128)(2,1)S(1)} %get-tuple-element.49), channel_id=1, source_target_pairs={{0,3},{1,2},{2,1},{3,0},{4,7},{5,6},{6,5},{7,4},{8,11},{9,10},{10,... | collective-permute-start | bytes 165896 | tf_op jit(solution)/shard_map/ppermute | solution.py:46
  37.0 7.1 %collective-permute-start.15 = (bf16[24,1152]{1,0:T(8,128)(2,1)S(1)}, bf16[24,1152]{1,0:T(8,128)(2,1)S(1)}, u32[]{:S(2)}, u32[]{:S(2)}) collective-permute-start(bf16[24,1152]{1,0:T(8,128)(2,1)S(1)} %get-tuple-element.50), channel_id=1, source_target_pairs={{0,1},{1,0},{2,3},{3,2},{4,5},{5,4},{6,7},{7,6},{8,9},{9,8},{10,11... | collective-permute-start | bytes 165896 | tf_op jit(solution)/shard_map/ppermute | solution.py:46

commit v5 on v4

--- a/solution.py
+++ b/solution.py
@@ -47,7 +47,7 @@
 
 
 def exchange_order(size):
-    return (1, 3, 2) if size == 4 else tuple(range(1, size))
+    return (2, 3, 1) if size == 4 else tuple(range(1, size))
 
 
 def split3(value):
@@ -260,24 +260,16 @@
     return copies
 
 
-def first_grads(order, grad_ref, dec_ref, own_ref, got_ref, *refs):
-    *acts, out_hbm, recon_hbm, part_ref, buf, sems, recon_ref, recon_sem = refs
-    tokens, half = grad_ref.shape[0], grad_ref.shape[1] // 2
-    low = lax.axis_index("feat") % 2 == 0
-    own, extra = own_ref[...], got_ref[tokens:, :].astype(F32)
-    rows = recon_ref.shape[0]
-    recon_ref[:, :half] = jnp.where(low, own, extra)[:rows].astype(BF16)
-    recon_ref[:, half:] = jnp.where(low, extra, own)[:rows].astype(BF16)
-    copies = [pltpu.make_async_copy(recon_ref, recon_hbm, recon_sem)]
-    copies[0].start()
-    copies += write_decoder_grads(order, grad_ref, acts, out_hbm, buf, sems)
+def first_grads(order, grad_ref, dec_ref, *refs):
+    *acts, out_hbm, part_ref, buf, sems = refs
+    copies = write_decoder_grads(order, grad_ref, acts, out_hbm, buf, sems)
     part_ref[...] = act_grad(grad_ref[...], dec_ref[lax.axis_index("layer")])
     for copy in copies:
         copy.wait()
 
 
-def last_grads(count, order, grad_ref, x_ref, part_ref, gate_ref, sparse_ref, score_ref, *refs):
-    *rest, _, dec_hbm, enc_hbm, loss_hbm, dec_buf, dec_sems, enc_buf, enc_sems, loss_ref, loss_sem = refs
+def last_grads(count, order, grad_ref, own_ref, got_ref, x_ref, part_ref, gate_ref, sparse_ref, score_ref, *refs):
+    *rest, _, dec_hbm, enc_hbm, loss_hbm, recon_hbm, dec_buf, dec_sems, enc_buf, enc_sems, loss_ref, loss_sem, recon_ref, recon_sem = refs
     acts, msgs = rest[: len(order)], rest[len(order) :]
     copies = write_decoder_grads(order, grad_ref, acts, dec_hbm, dec_buf, dec_sems)
     width = part_ref.shape[1]
@@ -300,6 +292,14 @@
         enc_buf[i] = jnp.dot(turned[span], pre, preferred_element_type=F32).astype(BF16)
         copies.append(pltpu.make_async_copy(enc_buf.at[i], enc_hbm.at[pl.ds(i * block, block)], enc_sems.at[i]))
         copies[-1].start()
+    tokens, half = grad_ref.shape[0], grad_ref.shape[1] // 2
+    low = lax.axis_index("feat") % 2 == 0
+    own, extra = own_ref[...], got_ref[tokens:, :].astype(F32)
+    rows = recon_ref.shape[0]
+    recon_ref[:, :half] = jnp.where(low, own, extra)[:rows].astype(BF16)
+    recon_ref[:, half:] = jnp.where(low, extra, own)[:rows].astype(BF16)
+    copies.append(pltpu.make_async_copy(recon_ref, recon_hbm, recon_sem))
+    copies[-1].start()
     for copy in copies:
         copy.wait()
 
@@ -350,7 +350,8 @@
         flops=2 * tokens * width * features,
         bytes_accessed=2 * width * features,
     )
-    order = exchange_order(layers)
+    back = exchange_order(layers)
+    order = back[::-1]
     others = [swap(acts, "layer", k) for k in order]
     pieces = max(1, features // 256)
     (total,) = call(
@@ -389,7 +390,6 @@
         (targets, *msgs),
         "error_half",
     )
-    back = (1, 3, 2) if layers == 4 else order
     parts = call(
         functools.partial(act_first, back),
         [shape((tokens, features), F32)] * (layers - 1),
@@ -407,25 +407,24 @@
         flops=tokens * width * features * (sources - 1),
         bytes_accessed=(sources - 1) * width * features,
     )
-    gots = [swap(sends[back.index(k)], "layer", k) for k in (2, 3, 1)]
+    gots = [swap(send, "layer", k) for send, k in zip(sends, back)]
     first, steps, block = sources - 1, max(1, features // 128), 128
     last = sources - first
-    dec_grad, recon, part = call(
+    dec_grad, part = call(
         functools.partial(first_grads, (0, *order[: first - 1])),
-        [shape((sources, features, width), BF16), shape((rows, width), BF16), shape((tokens, features), F32)],
-        (grad, decoder, own_rows, theirs, acts, *others[: first - 1]),
+        [shape((sources, features, width), BF16), shape((tokens, features), F32)],
+        (grad, decoder, acts, *others[: first - 1]),
         "first_grads",
-        scratch=[pltpu.VMEM((first * steps, features // steps, width), BF16), pltpu.SemaphoreType.DMA((first * steps,))]
-        + [pltpu.VMEM((rows, width), BF16), pltpu.SemaphoreType.DMA(())],
+        scratch=[pltpu.VMEM((first * steps, features // steps, width), BF16), pltpu.SemaphoreType.DMA((first * steps,))],
         limit=24,
-        out_specs=[ANY, ANY, WHOLE],
+        out_specs=[ANY, WHOLE],
         flops=2 * tokens * width * features * (first + 1),
         bytes_accessed=2 * first * width * features,
     )
-    args = (grad, x, part, gate, sparse, score, *others[first - 1 :], *gots, dec_grad)
-    dec_grad, enc_grad, loss = call(
+    args = (grad, own_rows, theirs, x, part, gate, sparse, score, *others[first - 1 :], *gots, dec_grad)
+    dec_grad, enc_grad, loss, recon = call(
         functools.partial(last_grads, layers * tokens * width, order[first - 1 :]),
-        [shape((sources, features, width), BF16), shape((width, features), BF16), shape((1, 1), F32)],
+        [shape((sources, features, width), BF16), shape((width, features), BF16), shape((1, 1), F32), shape((rows, width), BF16)],
         args,
         "last_grads",
         scratch=[
@@ -435,9 +434,11 @@
             pltpu.SemaphoreType.DMA((width // block,)),
             pltpu.VMEM((1, 1), F32),
             pltpu.SemaphoreType.DMA(()),
+            pltpu.VMEM((rows, width), BF16),
+            pltpu.SemaphoreType.DMA(()),
         ],
         in_specs=[WHOLE] * (len(args) - 1) + [ANY],
-        out_specs=[ANY] * 3,
+        out_specs=[ANY] * 4,
         limit=24,
         aliases={len(args) - 1: 0},
         flops=2 * tokens * width * features * (last + 1),

time: 48.5 us -> 48 us (0.990)
  Pallas kernels: 24.5 us -> 24 us
    pallas_call x13, Pallas kernels: 24.5 us -> 24 us  [call(): pl.pallas_call(body, out_shape=outs, in_specs=in_specs or [WHOLE] * len(a...]
  transfers between devices with their start and end apart: 16 -> 16, of which waited for: 7 -> 7; matrix products, arithmetic and copies ran while one was open for 0% -> 0% of each run, Pallas kernels for 32% -> 31%
where the time goes in v5:
time: 48 us; the launch traced here: 47.8 us
  Pallas kernels  24 us (50%)
  starting transfers between devices  16.3 us (34%)
  waiting for transfers between devices  6.81 us (14%)
  between operations  0.77 us (2%)
    pallas_call x13, Pallas kernels, call(): pl.pallas_call(body, out_shape=outs, in_specs=in_specs or [WHOLE] * len(a...  24 us
    ppermute x16, starting transfers between devices, swap(): return lax.ppermute(x, axis, [(i, i ^ bits) for i in range(size)])  16.3 us
    ppermute x16, waiting for transfers between devices, swap(): return lax.ppermute(x, axis, [(i, i ^ bits) for i in range(size)])  6.81 us
  transfers between devices with their start and end apart: 16, of which 7 were waited for; matrix products, arithmetic and copies ran while one was open for 0% of the time, Pallas kernels for 31%

profile of v5, /device:TPU:0, one launch (start us, length us, event | category | flops | bytes accessed | tf_op | source)
XLA Modules:
  0.0 47.8 jit_solution(7917093930608872849)
XLA Ops:
  0.6 0.5 %collective-permute-start = (bf16[3,2304]{1,0:T(4,128)(2,1)}, bf16[3,2304]{1,0:T(4,128)(2,1)S(1)}, u32[]{:S(2)}, u32[]{:S(2)}) collective-permute-start(bf16[3,2304]{1,0:T(4,128)(2,1)} %bitcast.18), channel_id=1, source_target_pairs={{0,4},{4,0},{8,12},{12,8},{16,20},{20,16},{24,28},{28,24},{1,5},{5... | collective-permute-start | bytes 41480 | tf_op jit(solution)/shard_map/ppermute | solution.py:46
  1.2 1.0 %load_own.1 = (bf16[3,2304]{1,0:T(4,128)(2,1)S(1)}, bf16[3,2304]{1,0:T(4,128)(2,1)S(1)}, f32[1,1024]{1,0:T(1,128)S(1)}) custom-call(bf16[3,2304]{1,0:T(4,128)(2,1)} %bitcast.19, bf16[3,2304]{1,0:T(4,128)(2,1)} %bitcast.21, s32[1,1024]{1,0:T(1,128)} %thr_hbm.1), custom_call_target="tpu_custom_call" | custom-call | bytes 4718592 | tf_op jit(solution)/shard_map/load_own/pallas_call | solution.py:31
  2.6 3.7 %collective-permute-start.4 = (bf16[8,3456]{1,0:T(8,128)(2,1)S(1)}, bf16[8,3456]{1,0:T(8,128)(2,1)S(1)}, u32[]{:S(2)}, u32[]{:S(2)}) collective-permute-start(bf16[8,3456]{1,0:T(8,128)(2,1)S(1)} %pack.1._.refs_0_), channel_id=1, source_target_pairs={{0,24},{4,28},{8,16},{12,20},{16,8},{20,12},{24,0},{28,4},{1,25},{... | collective-permute-start | bytes 165896 | tf_op jit(solution)/shard_map/ppermute | solution.py:46
  6.9 2.3 %fetch.1.refs_4_ = bf16[2304,1024]{1,0:T(8,128)(2,1)S(1)} custom-call(bf16[8,3456]{1,0:T(8,128)(2,1)S(1)} %pack.1._.refs_0_, bf16[2304,1024]{1,0:T(8,128)(2,1)} %bitcast.17), custom_call_target="tpu_custom_call" | custom-call | bytes 9437184 | tf_op jit(solution)/shard_map/fetch/pallas_call | solution.py:31
  9.3 1.1 %collective-permute-done.3.refs_2_ = bf16[8,3456]{1,0:T(8,128)(2,1)S(1)} collective-permute-done((bf16[8,3456]{1,0:T(8,128)(2,1)S(1)}, bf16[8,3456]{1,0:T(8,128)(2,1)S(1)}, u32[]{:S(2)}, u32[]{:S(2)}) %collective-permute-start.3) | collective-permute-done | bytes 55328 | tf_op jit(solution)/shard_map/ppermute | solution.py:46
  10.9 1.1 %encode.1 = (bf16[24,2304]{1,0:T(8,128)(2,1)S(1)}, bf16[24,1152]{1,0:T(8,128)(2,1)S(1)}, bf16[24,1024]{1,0:T(8,128)(2,1)S(1)}, f32[24,1024]{1,0:T(8,128)S(1)}, f...) custom-call(bf16[8,3456]{1,0:T(8,128)(2,1)S(1)} %pack.1._.refs_0_, bf16[8,3456]{1,0:T(8,128)(2,1)S(1)} %collective-permute-done.2.refs_1_, ...), custom_call_target="tpu_custom_call" | custom-call | flops 113246208 | bytes 4718592 | tf_op jit(solution)/shard_map/encode/pallas_call | solution.py:31
  12.1 2.6 %collective-permute-start.7 = (bf16[24,1024]{1,0:T(8,128)(2,1)S(1)}, bf16[24,1024]{1,0:T(8,128)(2,1)S(1)}, u32[]{:S(2)}, u32[]{:S(2)}) collective-permute-start(bf16[24,1024]{1,0:T(8,128)(2,1)S(1)} %get-tuple-element.34.acts_ref.refs_0_), channel_id=1, source_target_pairs={{0,2},{1,3},{2,0},{3,1},{4,6},{5,7},{6,4},{7,5},{8,10},{9,11},{10,... | collective-permute-start | bytes 147464 | tf_op jit(solution)/shard_map/ppermute | solution.py:46
  14.7 1.3 %collective-permute-start.6 = (bf16[24,1024]{1,0:T(8,128)(2,1)S(1)}, bf16[24,1024]{1,0:T(8,128)(2,1)S(1)}, u32[]{:S(2)}, u32[]{:S(2)}) collective-permute-start(bf16[24,1024]{1,0:T(8,128)(2,1)S(1)} %get-tuple-element.34.acts_ref.refs_0_), channel_id=1, source_target_pairs={{0,3},{1,2},{2,1},{3,0},{4,7},{5,6},{6,5},{7,4},{8,11},{9,10},{10,... | collective-permute-start | bytes 147464 | tf_op jit(solution)/shard_map/ppermute | solution.py:46
  16.2 2.7 %recon_own.1.total_ref = f32[24,2304]{1,0:T(8,128)S(1)} custom-call(bf16[24,1024]{1,0:T(8,128)(2,1)S(1)} %get-tuple-element.34.acts_ref.refs_0_, bf16[4,1024,2304]{2,1,0:T(8,128)(2,1)} %bitcast.10), custom_call_target="tpu_custom_call" | custom-call | flops 113246208 | bytes 4718592 | tf_op jit(solution)/shard_map/recon_own/pallas_call | solution.py:31
  18.9 1.7 %collective-permute-done.6.refs_1_.refs_2_ = bf16[24,1024]{1,0:T(8,128)(2,1)S(1)} collective-permute-done((bf16[24,1024]{1,0:T(8,128)(2,1)S(1)}, bf16[24,1024]{1,0:T(8,128)(2,1)S(1)}, u32[]{:S(2)}, u32[]{:S(2)}) %collective-permute-start.6) | collective-permute-done | bytes 49184 | tf_op jit(solution)/shard_map/ppermute | solution.py:46
  20.6 1.3 %recon_send.1 = f32[24,1280]{1,0:T(8,128)S(1)} custom-call(f32[24,2304]{1,0:T(8,128)S(1)} %recon_own.1.total_ref, f32[8,128]{1,0:T(8,128)S(1)} %get-tuple-element.35.pen_ref, bf16[4,1024,2304]{2,1,0:T(8,128)(2,1)S(1)} %bitcast.11, bf16[24,1024]{1,0:T(8,128)(2,1)S(1)} %collective-permute-done.5.refs_0_.refs_1_, ...), custom_call_target="tpu_custom_call" | custom-call | flops 169869312 | bytes 7077888 | tf_op jit(solution)/shard_map/recon_send/pallas_call | solution.py:31
  22.0 1.3 %recon_keep.1.keep_ref = f32[24,1280]{1,0:T(8,128)S(1)} custom-call(f32[24,2304]{1,0:T(8,128)S(1)} %recon_own.1.total_ref, f32[8,128]{1,0:T(8,128)S(1)} %get-tuple-element.35.pen_ref, bf16[4,1024,2304]{2,1,0:T(8,128)(2,1)S(1)} %bitcast.12, bf16[24,1024]{1,0:T(8,128)(2,1)S(1)} %collective-permute-done.5.refs_0_.refs_1_, ...), custom_call_target="tpu_custom_call" | custom-call | flops 169869312 | bytes 7077888 | tf_op jit(solution)/shard_map/recon_keep/pallas_call | solution.py:31
  23.4 1.5 %collective-permute-start.11 = (bf16[24,1280]{1,0:T(8,128)(2,1)S(1)}, bf16[24,1280]{1,0:T(8,128)(2,1)S(1)}, u32[]{:S(2)}, u32[]{:S(2)}) collective-permute-start(bf16[24,1280]{1,0:T(8,128)(2,1)S(1)} %pair_sum.1.refs_0_), channel_id=1, source_target_pairs={{0,24},{4,28},{8,16},{12,20},{16,8},{20,12},{24,0},{28,4},{1,25},{... | collective-permute-start | bytes 184328 | tf_op jit(solution)/shard_map/ppermute | solution.py:46
  24.9 0.6 %collective-permute-start.10 = (bf16[24,1280]{1,0:T(8,128)(2,1)S(1)}, bf16[24,1280]{1,0:T(8,128)(2,1)S(1)}, u32[]{:S(2)}, u32[]{:S(2)}) collective-permute-start(bf16[24,1280]{1,0:T(8,128)(2,1)S(1)} %pair_sum.1.refs_0_), channel_id=1, source_target_pairs={{0,16},{4,20},{8,24},{12,28},{16,0},{20,4},{24,8},{28,12},{1,17},{... | collective-permute-start | bytes 184328 | tf_op jit(solution)/shard_map/ppermute | solution.py:46
  25.6 1.4 %collective-permute-start.9 = (bf16[24,1280]{1,0:T(8,128)(2,1)S(1)}, bf16[24,1280]{1,0:T(8,128)(2,1)S(1)}, u32[]{:S(2)}, u32[]{:S(2)}) collective-permute-start(bf16[24,1280]{1,0:T(8,128)(2,1)S(1)} %pair_sum.1.refs_0_), channel_id=1, source_target_pairs={{0,8},{4,12},{8,0},{12,4},{16,24},{20,28},{24,16},{28,20},{1,9},{5... | collective-permute-start | bytes 184328 | tf_op jit(solution)/shard_map/ppermute | solution.py:46
  26.9 1.9 %collective-permute-done.11.refs_3_ = bf16[24,1280]{1,0:T(8,128)(2,1)S(1)} collective-permute-done((bf16[24,1280]{1,0:T(8,128)(2,1)S(1)}, bf16[24,1280]{1,0:T(8,128)(2,1)S(1)}, u32[]{:S(2)}, u32[]{:S(2)}) %collective-permute-start.11) | collective-permute-done | bytes 61472 | tf_op jit(solution)/shard_map/ppermute | solution.py:46
  28.8 1.2 %collective-permute-done.10.refs_2_ = bf16[24,1280]{1,0:T(8,128)(2,1)S(1)} collective-permute-done((bf16[24,1280]{1,0:T(8,128)(2,1)S(1)}, bf16[24,1280]{1,0:T(8,128)(2,1)S(1)}, u32[]{:S(2)}, u32[]{:S(2)}) %collective-permute-start.10) | collective-permute-done | bytes 61472 | tf_op jit(solution)/shard_map/ppermute | solution.py:46
  30.4 2.0 %act_first.1 = (f32[24,1024]{1,0:T(8,128)S(1)}, f32[24,1024]{1,0:T(8,128)S(1)}, f32[24,1024]{1,0:T(8,128)S(1)}) custom-call(bf16[32,1152]{1,0:T(8,128)(2,1)S(1)} %get-tuple-element.36.mine_ref, bf16[4,1024,2304]{2,1,0:T(8,128)(2,1)S(1)} %bitcast.13), custom_call_target="tpu_custom_call" | custom-call | flops 169869312 | bytes 7077888 | tf_op jit(solution)/shard_map/act_first/pallas_call | solution.py:31
  32.4 2.1 %act_second.1 = (bf16[24,2304]{1,0:T(8,128)(2,1)S(1)}, f32[8,128]{1,0:T(8,128)S(1)}, bf16[24,1152]{1,0:T(8,128)(2,1)S(1)}, bf16[24,1152]{1,0:T(8,128)(2,1)S(1)}, bf16[24,1152]{1,0:T(8,128)(2,1)S(1)}) custom-call(bf16[32,1152]{1,0:T(8,128)(2,1)S(1)} %get-tuple-element.36.mine_ref, bf16[32,1152]{1,0:T(8,128)(2,1)S(1)} %collective-permute-done.12.got_ref, ...), custom_call_target="tpu_custom_call" | custom-call | flops 169869312 | bytes 7077888 | tf_op jit(solution)/shard_map/act_second/pallas_call | solution.py:31
  34.5 1.4 %collective-permute-start.13 = (bf16[24,1152]{1,0:T(8,128)(2,1)S(1)}, bf16[24,1152]{1,0:T(8,128)(2,1)S(1)}, u32[]{:S(2)}, u32[]{:S(2)}) collective-permute-start(bf16[24,1152]{1,0:T(8,128)(2,1)S(1)} %get-tuple-element.48), channel_id=1, source_target_pairs={{0,2},{1,3},{2,0},{3,1},{4,6},{5,7},{6,4},{7,5},{8,10},{9,11},{10,... | collective-permute-start | bytes 165896 | tf_op jit(solution)/shard_map/ppermute | solution.py:46
  35.9 1.1 %collective-permute-start.14 = (bf16[24,1152]{1,0:T(8,128)(2,1)S(1)}, bf16[24,1152]{1,0:T(8,128)(2,1)S(1)}, u32[]{:S(2)}, u32[]{:S(2)}) collective-permute-start(bf16[24,1152]{1,0:T(8,128)(2,1)S(1)} %get-tuple-element.49), channel_id=1, source_target_pairs={{0,3},{1,2},{2,1},{3,0},{4,7},{5,6},{6,5},{7,4},{8,11},{9,10},{10,... | collective-permute-start | bytes 165896 | tf_op jit(solution)/shard_map/ppermute | solution.py:46
  37.0 1.0 %collective-permute-start.15 = (bf16[24,1152]{1,0:T(8,128)(2,1)S(1)}, bf16[24,1152]{1,0:T(8,128)(2,1)S(1)}, u32[]{:S(2)}, u32[]{:S(2)}) collective-permute-start(bf16[24,1152]{1,0:T(8,128)(2,1)S(1)} %get-tuple-element.50), channel_id=1, source_target_pairs={{0,1},{1,0},{2,3},{3,2},{4,5},{5,4},{6,7},{7,6},{8,9},{9,8},{10,11... | collective-permute-start | bytes 165896 | tf_op jit(solution)/shard_map/ppermute | solution.py:46
  38.0 5.6 %first_grads.1 = (bf16[4,1024,2304]{2,1,0:T(8,128)(2,1)}, f32[24,1024]{1,0:T(8,128)S(1)}) custom-call(bf16[24,2304]{1,0:T(8,128)(2,1)S(1)} %get-tuple-element.41.grad_ref, bf16[4,1024,2304]{2,1,0:T(8,128)(2,1)S(1)} %bitcast.15, bf16[24,1024]{1,0:T(8,128)(2,1)S(1)} %get-tuple-element.34.acts_ref.refs_0_, ...), custom_call_target="tpu_custom_call" | custom-call | flops 452984832 | bytes 14155776 | tf_op jit(solution)/shard_map/first_grads/pallas_call | solution.py:31
  43.6 4.2 %last_grads.1 = (bf16[4,1024,2304]{2,1,0:T(8,128)(2,1)}, bf16[2304,1024]{1,0:T(8,128)(2,1)}, f32[1,1]{1,0:T(1,128)}, bf16[3,2304]{1,0:T(4,128)(2,1)}) custom-call(bf16[24,2304]{1,0:T(8,128)(2,1)S(1)} %get-tuple-element.41.grad_ref, f32[8,1152]{1,0:T(8,128)S(1)} %get-tuple-element.42.own_ref, ...), custom_call_target="tpu_custom_call", output_to_operand_aliasing={{0}: (12, {})} | custom-call | flops 226492416 | bytes 9437184 | tf_op jit(solution)/shard_map/last_grads/pallas_call | solution.py:31
  (23 shorter events, 2.3 us)
Async XLA Ops:
  0.6 20.0 %copy-start = (bf16[4,1,1024,2304]{3,2,1,0:T(8,128)(2,1)S(1)}, bf16[4,1,1024,2304]{3,2,1,0:T(8,128)(2,1)}, u32[]{:S(2)}) copy-start(bf16[4,1,1024,2304]{3,2,1,0:T(8,128)(2,1)} %param.8) | copy-start | bytes 56623108
  0.6 1.6 %collective-permute-start = (bf16[3,2304]{1,0:T(4,128)(2,1)}, bf16[3,2304]{1,0:T(4,128)(2,1)S(1)}, u32[]{:S(2)}, u32[]{:S(2)}) collective-permute-start(bf16[3,2304]{1,0:T(4,128)(2,1)} %bitcast.18), channel_id=1, source_target_pairs={{0,4},{4,0},{8,12},{12,8},{16,20},{20,16},{24,28},{28,24},{1,5},{5... | collective-permute-start | bytes 41480 | tf_op jit(solution)/shard_map/ppermute | solution.py:46
  1.2 1.4 %collective-permute-start.1 = (bf16[3,2304]{1,0:T(4,128)(2,1)}, bf16[3,2304]{1,0:T(4,128)(2,1)S(1)}, u32[]{:S(2)}, u32[]{:S(2)}) collective-permute-start(bf16[3,2304]{1,0:T(4,128)(2,1)} %bitcast.20), channel_id=1, source_target_pairs={{0,4},{4,0},{8,12},{12,8},{16,20},{20,16},{24,28},{28,24},{1,5},{5... | collective-permute-start | bytes 41480 | tf_op jit(solution)/shard_map/ppermute | solution.py:46
  2.6 6.7 %collective-permute-start.4 = (bf16[8,3456]{1,0:T(8,128)(2,1)S(1)}, bf16[8,3456]{1,0:T(8,128)(2,1)S(1)}, u32[]{:S(2)}, u32[]{:S(2)}) collective-permute-start(bf16[8,3456]{1,0:T(8,128)(2,1)S(1)} %pack.1._.refs_0_), channel_id=1, source_target_pairs={{0,24},{4,28},{8,16},{12,20},{16,8},{20,12},{24,0},{28,4},{1,25},{... | collective-permute-start | bytes 165896 | tf_op jit(solution)/shard_map/ppermute | solution.py:46
  6.3 4.2 %collective-permute-start.3 = (bf16[8,3456]{1,0:T(8,128)(2,1)S(1)}, bf16[8,3456]{1,0:T(8,128)(2,1)S(1)}, u32[]{:S(2)}, u32[]{:S(2)}) collective-permute-start(bf16[8,3456]{1,0:T(8,128)(2,1)S(1)} %pack.1._.refs_0_), channel_id=1, source_target_pairs={{0,16},{4,20},{8,24},{12,28},{16,0},{20,4},{24,8},{28,12},{1,17},{... | collective-permute-start | bytes 165896 | tf_op jit(solution)/shard_map/ppermute | solution.py:46
  6.8 4.2 %collective-permute-start.2 = (bf16[8,3456]{1,0:T(8,128)(2,1)S(1)}, bf16[8,3456]{1,0:T(8,128)(2,1)S(1)}, u32[]{:S(2)}, u32[]{:S(2)}) collective-permute-start(bf16[8,3456]{1,0:T(8,128)(2,1)S(1)} %pack.1._.refs_0_), channel_id=1, source_target_pairs={{0,8},{4,12},{8,0},{12,4},{16,24},{20,28},{24,16},{28,20},{1,9},{5... | collective-permute-start | bytes 165896 | tf_op jit(solution)/shard_map/ppermute | solution.py:46
  12.1 6.9 %collective-permute-start.7 = (bf16[24,1024]{1,0:T(8,128)(2,1)S(1)}, bf16[24,1024]{1,0:T(8,128)(2,1)S(1)}, u32[]{:S(2)}, u32[]{:S(2)}) collective-permute-start(bf16[24,1024]{1,0:T(8,128)(2,1)S(1)} %get-tuple-element.34.acts_ref.refs_0_), channel_id=1, source_target_pairs={{0,2},{1,3},{2,0},{3,1},{4,6},{5,7},{6,4},{7,5},{8,10},{9,11},{10,... | collective-permute-start | bytes 147464 | tf_op jit(solution)/shard_map/ppermute | solution.py:46
  14.7 6.0 %collective-permute-start.6 = (bf16[24,1024]{1,0:T(8,128)(2,1)S(1)}, bf16[24,1024]{1,0:T(8,128)(2,1)S(1)}, u32[]{:S(2)}, u32[]{:S(2)}) collective-permute-start(bf16[24,1024]{1,0:T(8,128)(2,1)S(1)} %get-tuple-element.34.acts_ref.refs_0_), channel_id=1, source_target_pairs={{0,3},{1,2},{2,1},{3,0},{4,7},{5,6},{6,5},{7,4},{8,11},{9,10},{10,... | collective-permute-start | bytes 147464 | tf_op jit(solution)/shard_map/ppermute | solution.py:46
  16.0 4.6 %collective-permute-start.5 = (bf16[24,1024]{1,0:T(8,128)(2,1)S(1)}, bf16[24,1024]{1,0:T(8,128)(2,1)S(1)}, u32[]{:S(2)}, u32[]{:S(2)}) collective-permute-start(bf16[24,1024]{1,0:T(8,128)(2,1)S(1)} %get-tuple-element.34.acts_ref.refs_0_), channel_id=1, source_target_pairs={{0,1},{1,0},{2,3},{3,2},{4,5},{5,4},{6,7},{7,6},{8,9},{9,8},{10,11... | collective-permute-start | bytes 147464 | tf_op jit(solution)/shard_map/ppermute | solution.py:46
  21.9 1.4 %collective-permute-start.8 = (f32[24,1280]{1,0:T(8,128)S(1)}, f32[24,1280]{1,0:T(8,128)S(1)}, u32[]{:S(2)}, u32[]{:S(2)}) collective-permute-start(f32[24,1280]{1,0:T(8,128)S(1)} %recon_send.1), channel_id=1, source_target_pairs={{0,4},{4,0},{8,12},{12,8},{16,20},{20,16},{24,28},{28,24},{1,5},{5... | collective-permute-start | bytes 368648 | tf_op jit(solution)/shard_map/ppermute | solution.py:46
  23.4 5.4 %collective-permute-start.11 = (bf16[24,1280]{1,0:T(8,128)(2,1)S(1)}, bf16[24,1280]{1,0:T(8,128)(2,1)S(1)}, u32[]{:S(2)}, u32[]{:S(2)}) collective-permute-start(bf16[24,1280]{1,0:T(8,128)(2,1)S(1)} %pair_sum.1.refs_0_), channel_id=1, source_target_pairs={{0,24},{4,28},{8,16},{12,20},{16,8},{20,12},{24,0},{28,4},{1,25},{... | collective-permute-start | bytes 184328 | tf_op jit(solution)/shard_map/ppermute | solution.py:46
  24.9 5.1 %collective-permute-start.10 = (bf16[24,1280]{1,0:T(8,128)(2,1)S(1)}, bf16[24,1280]{1,0:T(8,128)(2,1)S(1)}, u32[]{:S(2)}, u32[]{:S(2)}) collective-permute-start(bf16[24,1280]{1,0:T(8,128)(2,1)S(1)} %pair_sum.1.refs_0_), channel_id=1, source_target_pairs={{0,16},{4,20},{8,24},{12,28},{16,0},{20,4},{24,8},{28,12},{1,17},{... | collective-permute-start | bytes 184328 | tf_op jit(solution)/shard_map/ppermute | solution.py:46
  25.6 4.6 %collective-permute-start.9 = (bf16[24,1280]{1,0:T(8,128)(2,1)S(1)}, bf16[24,1280]{1,0:T(8,128)(2,1)S(1)}, u32[]{:S(2)}, u32[]{:S(2)}) collective-permute-start(bf16[24,1280]{1,0:T(8,128)(2,1)S(1)} %pair_sum.1.refs_0_), channel_id=1, source_target_pairs={{0,8},{4,12},{8,0},{12,4},{16,24},{20,28},{24,16},{28,20},{1,9},{5... | collective-permute-start | bytes 184328 | tf_op jit(solution)/shard_map/ppermute | solution.py:46
  30.3 2.1 %collective-permute-start.12 = (bf16[32,1152]{1,0:T(8,128)(2,1)S(1)}, bf16[32,1152]{1,0:T(8,128)(2,1)S(1)}, u32[]{:S(2)}, u32[]{:S(2)}) collective-permute-start(bf16[32,1152]{1,0:T(8,128)(2,1)S(1)} %get-tuple-element.36.mine_ref), channel_id=1, source_target_pairs={{0,4},{4,0},{8,12},{12,8},{16,20},{20,16},{24,28},{28,24},{1,5},{5... | collective-permute-start | bytes 221192 | tf_op jit(solution)/shard_map/ppermute | solution.py:46
  34.5 9.2 %collective-permute-start.13 = (bf16[24,1152]{1,0:T(8,128)(2,1)S(1)}, bf16[24,1152]{1,0:T(8,128)(2,1)S(1)}, u32[]{:S(2)}, u32[]{:S(2)}) collective-permute-start(bf16[24,1152]{1,0:T(8,128)(2,1)S(1)} %get-tuple-element.48), channel_id=1, source_target_pairs={{0,2},{1,3},{2,0},{3,1},{4,6},{5,7},{6,4},{7,5},{8,10},{9,11},{10,... | collective-permute-start | bytes 165896 | tf_op jit(solution)/shard_map/ppermute | solution.py:46
  35.9 7.7 %collective-permute-start.14 = (bf16[24,1152]{1,0:T(8,128)(2,1)S(1)}, bf16[24,1152]{1,0:T(8,128)(2,1)S(1)}, u32[]{:S(2)}, u32[]{:S(2)}) collective-permute-start(bf16[24,1152]{1,0:T(8,128)(2,1)S(1)} %get-tuple-element.49), channel_id=1, source_target_pairs={{0,3},{1,2},{2,1},{3,0},{4,7},{5,6},{6,5},{7,4},{8,11},{9,10},{10,... | collective-permute-start | bytes 165896 | tf_op jit(solution)/shard_map/ppermute | solution.py:46
  37.0 6.6 %collective-permute-start.15 = (bf16[24,1152]{1,0:T(8,128)(2,1)S(1)}, bf16[24,1152]{1,0:T(8,128)(2,1)S(1)}, u32[]{:S(2)}, u32[]{:S(2)}) collective-permute-start(bf16[24,1152]{1,0:T(8,128)(2,1)S(1)} %get-tuple-element.50), channel_id=1, source_target_pairs={{0,1},{1,0},{2,3},{3,2},{4,5},{5,4},{6,7},{7,6},{8,9},{9,8},{10,11... | collective-permute-start | bytes 165896 | tf_op jit(solution)/shard_map/ppermute | solution.py:46

commit v6 on v5

--- a/solution.py
+++ b/solution.py
@@ -160,9 +160,11 @@
 
 def pair_sum(keep_ref, got_ref, msg_ref):
     half = keep_ref.shape[1] - LANES
-    msg_ref[:, :half] = (keep_ref[:, :half] + got_ref[:, :half]).astype(BF16)
+    for i in range(keep_ref.shape[0] // 8):
+        rows, columns = slice(8 * i, 8 * i + 8), slice(i * half, (i + 1) * half)
+        msg_ref[:, columns] = (keep_ref[rows, :half] + got_ref[rows, :half]).astype(BF16)
     pen = keep_ref[0:1, half : half + 1] + got_ref[0:1, half : half + 1]
-    msg_ref[:, half:] = spread3(pen, (keep_ref.shape[0], LANES))
+    msg_ref[:, -LANES:] = spread3(pen, (8, LANES))
 
 
 def sum_messages(refs):
@@ -173,11 +175,10 @@
 
 
 def group_sum(*refs):
-    half = refs[0].shape[1] - LANES
     total = sum_messages(refs[:-1])
-    refs[-1][:, :half] = total[:, :half].astype(BF16)
-    pen = jnp.sum(total[0:1, half:], axis=1, keepdims=True)
-    refs[-1][:, half:] = spread3(pen, (total.shape[0], LANES))
+    refs[-1][:, :-LANES] = total[:, :-LANES].astype(BF16)
+    pen = jnp.sum(total[0:1, -LANES:], axis=1, keepdims=True)
+    refs[-1][:, -LANES:] = spread3(pen, (8, LANES))
 
 
 def pick_rows(device, rows, tokens):
@@ -191,7 +192,7 @@
     tokens, half = target_ref.shape
     me = lax.axis_index("feat")
     total = sum_messages(msgs)
-    recon = total[:, :half]
+    recon = jnp.concatenate([total[:, i * half : (i + 1) * half] for i in range(tokens // 8)], axis=0)
     error = recon - target_ref[...].astype(F32)
     squares = jnp.sum(jnp.sum(error * error, axis=1, keepdims=True), axis=0, keepdims=True)
     narrow = recon.astype(BF16)
@@ -202,7 +203,7 @@
     parts = jnp.concatenate([parts, jnp.zeros((8, half - LANES), F32)], axis=1)
     out_ref[:tokens, :] = (error / ERROR_SCALE).astype(BF16)
     out_ref[tokens:, :] = jnp.where(row < rows, theirs, jnp.where(row == rows, parts, 0.0)).astype(BF16)
-    pen = jnp.sum(total[0:1, half:], axis=1, keepdims=True)
+    pen = jnp.sum(total[0:1, -LANES:], axis=1, keepdims=True)
     pen_ref[...] = jnp.broadcast_to(pen, pen_ref.shape)
 
 
@@ -210,26 +211,31 @@
     return lax.dot_general(dec, grad, NT, preferred_element_type=F32).T
 
 
-def act_half(grad, dec_ref, source, theirs):
-    half = grad.shape[1]
-    span = pl.ds(pl.multiple_of((lax.axis_index("feat") + theirs) % 2 * half, half), half)
-    return act_grad(grad, dec_ref[source, :, span])
+def act_split(width):
+    early = width // 2 // 256 * 256
+    return early, width - early
 
 
 def act_first(order, mine_ref, dec_ref, *outs):
-    tokens = outs[0].shape[0]
-    me = lax.axis_index("layer")
+    tokens, width = outs[0].shape[0], dec_ref.shape[2]
+    early, late = act_split(width)
+    side, me = lax.axis_index("feat") % 2, lax.axis_index("layer")
+    span = pl.ds(pl.multiple_of(side * late, LANES), early)
+    grad = jnp.where(side == 0, mine_ref[:tokens, :early], mine_ref[:tokens, width // 2 - early :])
     for k, out_ref in zip(order, outs):
-        out_ref[...] = act_half(mine_ref[:tokens, :], dec_ref, me ^ k, 0)
+        out_ref[...] = act_grad(grad, dec_ref[me ^ k, :, span])
 
 
 def act_second(rows, order, mine_ref, got_ref, pen_ref, dec_ref, *refs):
     parts = refs[: len(order)]
     grad_ref, score_ref, *msgs = refs[len(order) :]
     tokens, half = grad_ref.shape[0], grad_ref.shape[1] // 2
-    low = lax.axis_index("feat") % 2 == 0
-    me = lax.axis_index("layer")
+    side, me = lax.axis_index("feat") % 2, lax.axis_index("layer")
     mine, got = mine_ref[:tokens, :], got_ref[:tokens, :]
+    grad_ref[:, :half] = jnp.where(side == 0, mine, got)
+    grad_ref[:, half:] = jnp.where(side == 0, got, mine)
+    early, late = act_split(2 * half)
+    span = pl.ds(pl.multiple_of((1 - side) * early, LANES), late)
     extra = got_ref[tokens:, :].astype(F32)
     mine_extra = mine_ref[tokens:, :].astype(F32)
     squares = jnp.sum(mine_extra[rows : rows + 1, :LANES], axis=1, keepdims=True)
@@ -238,10 +244,8 @@
     score_ref[...] = jnp.broadcast_to(score, score_ref.shape)
     width = dec_ref.shape[1]
     for k, part_ref, msg in zip(order, parts, msgs):
-        msg[:, :width] = (part_ref[...] + act_half(got, dec_ref, me ^ k, 1)).astype(BF16)
+        msg[:, :width] = (part_ref[...] + act_grad(grad_ref[:, span], dec_ref[me ^ k, :, span])).astype(BF16)
         msg[:, width:] = spread3(score, (tokens, LANES))
-    grad_ref[:, :half] = jnp.where(low, mine, got)
-    grad_ref[:, half:] = jnp.where(low, got, mine)
 
 
 def write_decoder_grads(order, grad_ref, acts, out_hbm, buf, sems):
@@ -271,7 +275,7 @@
 def last_grads(count, order, grad_ref, own_ref, got_ref, x_ref, part_ref, gate_ref, sparse_ref, score_ref, *refs):
     *rest, _, dec_hbm, enc_hbm, loss_hbm, recon_hbm, dec_buf, dec_sems, enc_buf, enc_sems, loss_ref, loss_sem, recon_ref, recon_sem = refs
     acts, msgs = rest[: len(order)], rest[len(order) :]
-    copies = write_decoder_grads(order, grad_ref, acts, dec_hbm, dec_buf, dec_sems)
+    copies = []
     width = part_ref.shape[1]
     scores = [score_ref[0:1, 0:1]]
     for msg in msgs:
@@ -292,6 +296,7 @@
         enc_buf[i] = jnp.dot(turned[span], pre, preferred_element_type=F32).astype(BF16)
         copies.append(pltpu.make_async_copy(enc_buf.at[i], enc_hbm.at[pl.ds(i * block, block)], enc_sems.at[i]))
         copies[-1].start()
+    copies += write_decoder_grads(order, grad_ref, acts, dec_hbm, dec_buf, dec_sems)
     tokens, half = grad_ref.shape[0], grad_ref.shape[1] // 2
     low = lax.axis_index("feat") % 2 == 0
     own, extra = own_ref[...], got_ref[tokens:, :].astype(F32)
@@ -376,14 +381,14 @@
         )[0]
         for theirs, name in ((1, "recon_send"), (0, "recon_keep"))
     )
-    (msg,) = call(pair_sum, [shape((tokens, half + LANES), BF16)], (keep, swap(send, "feat", 1)), "pair_sum")
+    (msg,) = call(pair_sum, [shape((8, tokens // 8 * half + LANES), BF16)], (keep, swap(send, "feat", 1)), "pair_sum")
     bit = 2
     while bit < feats:
         pair = (bit, 2 * bit, 3 * bit) if 2 * bit < feats else (bit,)
         msgs = [msg] + [swap(msg, "feat", k) for k in pair]
         bit <<= len(pair) // 2 + 1
         if bit < feats:
-            (msg,) = call(group_sum, [shape((tokens, half + LANES), BF16)], msgs, "group_sum")
+            (msg,) = call(group_sum, [shape(msg.shape, BF16)], msgs, "group_sum")
     mine, own_rows, pen_all = call(
         functools.partial(error_half, rows),
         [shape((tokens + 8, half), BF16), shape((8, half), F32), shape((8, LANES), F32)],

time: 48 us -> 47.8 us (level)
  no operation moved by 1% of the time
where the time goes in v6:
time: 47.8 us; the launch traced here: 47.6 us
  Pallas kernels  23.9 us (50%)
  starting transfers between devices  16.3 us (34%)
  waiting for transfers between devices  6.64 us (14%)
  between operations  0.78 us (2%)
    pallas_call x13, Pallas kernels, call(): pl.pallas_call(body, out_shape=outs, in_specs=in_specs or [WHOLE] * len(a...  23.9 us
    ppermute x16, starting transfers between devices, swap(): return lax.ppermute(x, axis, [(i, i ^ bits) for i in range(size)])  16.3 us
    ppermute x16, waiting for transfers between devices, swap(): return lax.ppermute(x, axis, [(i, i ^ bits) for i in range(size)])  6.64 us
  transfers between devices with their start and end apart: 16, of which 7 were waited for; matrix products, arithmetic and copies ran while one was open for 0% of the time, Pallas kernels for 31%

profile of v6, /device:TPU:0, one launch (start us, length us, event | category | flops | bytes accessed | tf_op | source)
XLA Modules:
  0.0 47.6 jit_solution(10353801709132447389)
XLA Ops:
  0.6 0.5 %collective-permute-start = (bf16[3,2304]{1,0:T(4,128)(2,1)}, bf16[3,2304]{1,0:T(4,128)(2,1)S(1)}, u32[]{:S(2)}, u32[]{:S(2)}) collective-permute-start(bf16[3,2304]{1,0:T(4,128)(2,1)} %bitcast.18), channel_id=1, source_target_pairs={{0,4},{4,0},{8,12},{12,8},{16,20},{20,16},{24,28},{28,24},{1,5},{5... | collective-permute-start | bytes 41480 | tf_op jit(solution)/shard_map/ppermute | solution.py:46
  1.2 1.0 %load_own.1 = (bf16[3,2304]{1,0:T(4,128)(2,1)S(1)}, bf16[3,2304]{1,0:T(4,128)(2,1)S(1)}, f32[1,1024]{1,0:T(1,128)S(1)}) custom-call(bf16[3,2304]{1,0:T(4,128)(2,1)} %bitcast.19, bf16[3,2304]{1,0:T(4,128)(2,1)} %bitcast.21, s32[1,1024]{1,0:T(1,128)} %thr_hbm.1), custom_call_target="tpu_custom_call" | custom-call | bytes 4718592 | tf_op jit(solution)/shard_map/load_own/pallas_call | solution.py:31
  2.6 3.7 %collective-permute-start.4 = (bf16[8,3456]{1,0:T(8,128)(2,1)S(1)}, bf16[8,3456]{1,0:T(8,128)(2,1)S(1)}, u32[]{:S(2)}, u32[]{:S(2)}) collective-permute-start(bf16[8,3456]{1,0:T(8,128)(2,1)S(1)} %pack.1._.refs_0_), channel_id=1, source_target_pairs={{0,24},{4,28},{8,16},{12,20},{16,8},{20,12},{24,0},{28,4},{1,25},{... | collective-permute-start | bytes 165896 | tf_op jit(solution)/shard_map/ppermute | solution.py:46
  6.9 2.3 %fetch.1.refs_4_ = bf16[2304,1024]{1,0:T(8,128)(2,1)S(1)} custom-call(bf16[8,3456]{1,0:T(8,128)(2,1)S(1)} %pack.1._.refs_0_, bf16[2304,1024]{1,0:T(8,128)(2,1)} %bitcast.17), custom_call_target="tpu_custom_call" | custom-call | bytes 9437184 | tf_op jit(solution)/shard_map/fetch/pallas_call | solution.py:31
  9.3 1.1 %collective-permute-done.3.refs_2_ = bf16[8,3456]{1,0:T(8,128)(2,1)S(1)} collective-permute-done((bf16[8,3456]{1,0:T(8,128)(2,1)S(1)}, bf16[8,3456]{1,0:T(8,128)(2,1)S(1)}, u32[]{:S(2)}, u32[]{:S(2)}) %collective-permute-start.3) | collective-permute-done | bytes 55328 | tf_op jit(solution)/shard_map/ppermute | solution.py:46
  10.9 1.1 %encode.1 = (bf16[24,2304]{1,0:T(8,128)(2,1)S(1)}, bf16[24,1152]{1,0:T(8,128)(2,1)S(1)}, bf16[24,1024]{1,0:T(8,128)(2,1)S(1)}, f32[24,1024]{1,0:T(8,128)S(1)}, f...) custom-call(bf16[8,3456]{1,0:T(8,128)(2,1)S(1)} %pack.1._.refs_0_, bf16[8,3456]{1,0:T(8,128)(2,1)S(1)} %collective-permute-done.2.refs_1_, ...), custom_call_target="tpu_custom_call" | custom-call | flops 113246208 | bytes 4718592 | tf_op jit(solution)/shard_map/encode/pallas_call | solution.py:31
  12.1 2.6 %collective-permute-start.7 = (bf16[24,1024]{1,0:T(8,128)(2,1)S(1)}, bf16[24,1024]{1,0:T(8,128)(2,1)S(1)}, u32[]{:S(2)}, u32[]{:S(2)}) collective-permute-start(bf16[24,1024]{1,0:T(8,128)(2,1)S(1)} %get-tuple-element.34.acts_ref.refs_0_), channel_id=1, source_target_pairs={{0,2},{1,3},{2,0},{3,1},{4,6},{5,7},{6,4},{7,5},{8,10},{9,11},{10,... | collective-permute-start | bytes 147464 | tf_op jit(solution)/shard_map/ppermute | solution.py:46
  14.7 1.3 %collective-permute-start.6 = (bf16[24,1024]{1,0:T(8,128)(2,1)S(1)}, bf16[24,1024]{1,0:T(8,128)(2,1)S(1)}, u32[]{:S(2)}, u32[]{:S(2)}) collective-permute-start(bf16[24,1024]{1,0:T(8,128)(2,1)S(1)} %get-tuple-element.34.acts_ref.refs_0_), channel_id=1, source_target_pairs={{0,3},{1,2},{2,1},{3,0},{4,7},{5,6},{6,5},{7,4},{8,11},{9,10},{10,... | collective-permute-start | bytes 147464 | tf_op jit(solution)/shard_map/ppermute | solution.py:46
  16.2 2.7 %recon_own.1.total_ref = f32[24,2304]{1,0:T(8,128)S(1)} custom-call(bf16[24,1024]{1,0:T(8,128)(2,1)S(1)} %get-tuple-element.34.acts_ref.refs_0_, bf16[4,1024,2304]{2,1,0:T(8,128)(2,1)} %bitcast.10), custom_call_target="tpu_custom_call" | custom-call | flops 113246208 | bytes 4718592 | tf_op jit(solution)/shard_map/recon_own/pallas_call | solution.py:31
  18.9 1.7 %collective-permute-done.6.refs_1_.refs_2_ = bf16[24,1024]{1,0:T(8,128)(2,1)S(1)} collective-permute-done((bf16[24,1024]{1,0:T(8,128)(2,1)S(1)}, bf16[24,1024]{1,0:T(8,128)(2,1)S(1)}, u32[]{:S(2)}, u32[]{:S(2)}) %collective-permute-start.6) | collective-permute-done | bytes 49184 | tf_op jit(solution)/shard_map/ppermute | solution.py:46
  20.6 1.3 %recon_send.1 = f32[24,1280]{1,0:T(8,128)S(1)} custom-call(f32[24,2304]{1,0:T(8,128)S(1)} %recon_own.1.total_ref, f32[8,128]{1,0:T(8,128)S(1)} %get-tuple-element.35.pen_ref, bf16[4,1024,2304]{2,1,0:T(8,128)(2,1)S(1)} %bitcast.11, bf16[24,1024]{1,0:T(8,128)(2,1)S(1)} %collective-permute-done.5.refs_0_.refs_1_, ...), custom_call_target="tpu_custom_call" | custom-call | flops 169869312 | bytes 7077888 | tf_op jit(solution)/shard_map/recon_send/pallas_call | solution.py:31
  22.0 1.3 %recon_keep.1.keep_ref = f32[24,1280]{1,0:T(8,128)S(1)} custom-call(f32[24,2304]{1,0:T(8,128)S(1)} %recon_own.1.total_ref, f32[8,128]{1,0:T(8,128)S(1)} %get-tuple-element.35.pen_ref, bf16[4,1024,2304]{2,1,0:T(8,128)(2,1)S(1)} %bitcast.12, bf16[24,1024]{1,0:T(8,128)(2,1)S(1)} %collective-permute-done.5.refs_0_.refs_1_, ...), custom_call_target="tpu_custom_call" | custom-call | flops 169869312 | bytes 7077888 | tf_op jit(solution)/shard_map/recon_keep/pallas_call | solution.py:31
  23.4 1.5 %collective-permute-start.11 = (bf16[8,3584]{1,0:T(8,128)(2,1)S(1)}, bf16[8,3584]{1,0:T(8,128)(2,1)S(1)}, u32[]{:S(2)}, u32[]{:S(2)}) collective-permute-start(bf16[8,3584]{1,0:T(8,128)(2,1)S(1)} %pair_sum.1.refs_0_), channel_id=1, source_target_pairs={{0,24},{4,28},{8,16},{12,20},{16,8},{20,12},{24,0},{28,4},{1,25},{... | collective-permute-start | bytes 172040 | tf_op jit(solution)/shard_map/ppermute | solution.py:46
  24.9 0.6 %collective-permute-start.10 = (bf16[8,3584]{1,0:T(8,128)(2,1)S(1)}, bf16[8,3584]{1,0:T(8,128)(2,1)S(1)}, u32[]{:S(2)}, u32[]{:S(2)}) collective-permute-start(bf16[8,3584]{1,0:T(8,128)(2,1)S(1)} %pair_sum.1.refs_0_), channel_id=1, source_target_pairs={{0,16},{4,20},{8,24},{12,28},{16,0},{20,4},{24,8},{28,12},{1,17},{... | collective-permute-start | bytes 172040 | tf_op jit(solution)/shard_map/ppermute | solution.py:46
  25.6 1.4 %collective-permute-start.9 = (bf16[8,3584]{1,0:T(8,128)(2,1)S(1)}, bf16[8,3584]{1,0:T(8,128)(2,1)S(1)}, u32[]{:S(2)}, u32[]{:S(2)}) collective-permute-start(bf16[8,3584]{1,0:T(8,128)(2,1)S(1)} %pair_sum.1.refs_0_), channel_id=1, source_target_pairs={{0,8},{4,12},{8,0},{12,4},{16,24},{20,28},{24,16},{28,20},{1,9},{5... | collective-permute-start | bytes 172040 | tf_op jit(solution)/shard_map/ppermute | solution.py:46
  26.9 1.8 %collective-permute-done.11.refs_3_ = bf16[8,3584]{1,0:T(8,128)(2,1)S(1)} collective-permute-done((bf16[8,3584]{1,0:T(8,128)(2,1)S(1)}, bf16[8,3584]{1,0:T(8,128)(2,1)S(1)}, u32[]{:S(2)}, u32[]{:S(2)}) %collective-permute-start.11) | collective-permute-done | bytes 57376 | tf_op jit(solution)/shard_map/ppermute | solution.py:46
  28.7 1.1 %collective-permute-done.10.refs_2_ = bf16[8,3584]{1,0:T(8,128)(2,1)S(1)} collective-permute-done((bf16[8,3584]{1,0:T(8,128)(2,1)S(1)}, bf16[8,3584]{1,0:T(8,128)(2,1)S(1)}, u32[]{:S(2)}, u32[]{:S(2)}) %collective-permute-start.10) | collective-permute-done | bytes 57376 | tf_op jit(solution)/shard_map/ppermute | solution.py:46
  30.2 1.8 %act_first.1 = (f32[24,1024]{1,0:T(8,128)S(1)}, f32[24,1024]{1,0:T(8,128)S(1)}, f32[24,1024]{1,0:T(8,128)S(1)}) custom-call(bf16[32,1152]{1,0:T(8,128)(2,1)S(1)} %get-tuple-element.36.mine_ref, bf16[4,1024,2304]{2,1,0:T(8,128)(2,1)S(1)} %bitcast.13), custom_call_target="tpu_custom_call" | custom-call | flops 169869312 | bytes 7077888 | tf_op jit(solution)/shard_map/act_first/pallas_call | solution.py:31
  32.0 2.3 %act_second.1 = (bf16[24,2304]{1,0:T(8,128)(2,1)S(1)}, f32[8,128]{1,0:T(8,128)S(1)}, bf16[24,1152]{1,0:T(8,128)(2,1)S(1)}, bf16[24,1152]{1,0:T(8,128)(2,1)S(1)}, bf16[24,1152]{1,0:T(8,128)(2,1)S(1)}) custom-call(bf16[32,1152]{1,0:T(8,128)(2,1)S(1)} %get-tuple-element.36.mine_ref, bf16[32,1152]{1,0:T(8,128)(2,1)S(1)} %collective-permute-done.12.got_ref, ...), custom_call_target="tpu_custom_call" | custom-call | flops 169869312 | bytes 7077888 | tf_op jit(solution)/shard_map/act_second/pallas_call | solution.py:31
  34.3 1.6 %collective-permute-start.13 = (bf16[24,1152]{1,0:T(8,128)(2,1)S(1)}, bf16[24,1152]{1,0:T(8,128)(2,1)S(1)}, u32[]{:S(2)}, u32[]{:S(2)}) collective-permute-start(bf16[24,1152]{1,0:T(8,128)(2,1)S(1)} %get-tuple-element.48), channel_id=1, source_target_pairs={{0,2},{1,3},{2,0},{3,1},{4,6},{5,7},{6,4},{7,5},{8,10},{9,11},{10,... | collective-permute-start | bytes 165896 | tf_op jit(solution)/shard_map/ppermute | solution.py:46
  35.9 1.0 %collective-permute-start.14 = (bf16[24,1152]{1,0:T(8,128)(2,1)S(1)}, bf16[24,1152]{1,0:T(8,128)(2,1)S(1)}, u32[]{:S(2)}, u32[]{:S(2)}) collective-permute-start(bf16[24,1152]{1,0:T(8,128)(2,1)S(1)} %get-tuple-element.49), channel_id=1, source_target_pairs={{0,3},{1,2},{2,1},{3,0},{4,7},{5,6},{6,5},{7,4},{8,11},{9,10},{10,... | collective-permute-start | bytes 165896 | tf_op jit(solution)/shard_map/ppermute | solution.py:46
  36.9 1.0 %collective-permute-start.15 = (bf16[24,1152]{1,0:T(8,128)(2,1)S(1)}, bf16[24,1152]{1,0:T(8,128)(2,1)S(1)}, u32[]{:S(2)}, u32[]{:S(2)}) collective-permute-start(bf16[24,1152]{1,0:T(8,128)(2,1)S(1)} %get-tuple-element.50), channel_id=1, source_target_pairs={{0,1},{1,0},{2,3},{3,2},{4,5},{5,4},{6,7},{7,6},{8,9},{9,8},{10,11... | collective-permute-start | bytes 165896 | tf_op jit(solution)/shard_map/ppermute | solution.py:46
  37.9 5.6 %first_grads.1 = (bf16[4,1024,2304]{2,1,0:T(8,128)(2,1)}, f32[24,1024]{1,0:T(8,128)S(1)}) custom-call(bf16[24,2304]{1,0:T(8,128)(2,1)S(1)} %get-tuple-element.41.grad_ref, bf16[4,1024,2304]{2,1,0:T(8,128)(2,1)S(1)} %bitcast.15, bf16[24,1024]{1,0:T(8,128)(2,1)S(1)} %get-tuple-element.34.acts_ref.refs_0_, ...), custom_call_target="tpu_custom_call" | custom-call | flops 452984832 | bytes 14155776 | tf_op jit(solution)/shard_map/first_grads/pallas_call | solution.py:31
  43.5 4.1 %last_grads.1 = (bf16[4,1024,2304]{2,1,0:T(8,128)(2,1)}, bf16[2304,1024]{1,0:T(8,128)(2,1)}, f32[1,1]{1,0:T(1,128)}, bf16[3,2304]{1,0:T(4,128)(2,1)}) custom-call(bf16[24,2304]{1,0:T(8,128)(2,1)S(1)} %get-tuple-element.41.grad_ref, f32[8,1152]{1,0:T(8,128)S(1)} %get-tuple-element.42.own_ref, ...), custom_call_target="tpu_custom_call", output_to_operand_aliasing={{0}: (12, {})} | custom-call | flops 226492416 | bytes 9437184 | tf_op jit(solution)/shard_map/last_grads/pallas_call | solution.py:31
  (23 shorter events, 2.3 us)
Async XLA Ops:
  0.6 20.0 %copy-start = (bf16[4,1,1024,2304]{3,2,1,0:T(8,128)(2,1)S(1)}, bf16[4,1,1024,2304]{3,2,1,0:T(8,128)(2,1)}, u32[]{:S(2)}) copy-start(bf16[4,1,1024,2304]{3,2,1,0:T(8,128)(2,1)} %param.8) | copy-start | bytes 56623108
  0.6 1.6 %collective-permute-start = (bf16[3,2304]{1,0:T(4,128)(2,1)}, bf16[3,2304]{1,0:T(4,128)(2,1)S(1)}, u32[]{:S(2)}, u32[]{:S(2)}) collective-permute-start(bf16[3,2304]{1,0:T(4,128)(2,1)} %bitcast.18), channel_id=1, source_target_pairs={{0,4},{4,0},{8,12},{12,8},{16,20},{20,16},{24,28},{28,24},{1,5},{5... | collective-permute-start | bytes 41480 | tf_op jit(solution)/shard_map/ppermute | solution.py:46
  1.2 1.4 %collective-permute-start.1 = (bf16[3,2304]{1,0:T(4,128)(2,1)}, bf16[3,2304]{1,0:T(4,128)(2,1)S(1)}, u32[]{:S(2)}, u32[]{:S(2)}) collective-permute-start(bf16[3,2304]{1,0:T(4,128)(2,1)} %bitcast.20), channel_id=1, source_target_pairs={{0,4},{4,0},{8,12},{12,8},{16,20},{20,16},{24,28},{28,24},{1,5},{5... | collective-permute-start | bytes 41480 | tf_op jit(solution)/shard_map/ppermute | solution.py:46
  2.6 6.7 %collective-permute-start.4 = (bf16[8,3456]{1,0:T(8,128)(2,1)S(1)}, bf16[8,3456]{1,0:T(8,128)(2,1)S(1)}, u32[]{:S(2)}, u32[]{:S(2)}) collective-permute-start(bf16[8,3456]{1,0:T(8,128)(2,1)S(1)} %pack.1._.refs_0_), channel_id=1, source_target_pairs={{0,24},{4,28},{8,16},{12,20},{16,8},{20,12},{24,0},{28,4},{1,25},{... | collective-permute-start | bytes 165896 | tf_op jit(solution)/shard_map/ppermute | solution.py:46
  6.3 4.2 %collective-permute-start.3 = (bf16[8,3456]{1,0:T(8,128)(2,1)S(1)}, bf16[8,3456]{1,0:T(8,128)(2,1)S(1)}, u32[]{:S(2)}, u32[]{:S(2)}) collective-permute-start(bf16[8,3456]{1,0:T(8,128)(2,1)S(1)} %pack.1._.refs_0_), channel_id=1, source_target_pairs={{0,16},{4,20},{8,24},{12,28},{16,0},{20,4},{24,8},{28,12},{1,17},{... | collective-permute-start | bytes 165896 | tf_op jit(solution)/shard_map/ppermute | solution.py:46
  6.8 4.2 %collective-permute-start.2 = (bf16[8,3456]{1,0:T(8,128)(2,1)S(1)}, bf16[8,3456]{1,0:T(8,128)(2,1)S(1)}, u32[]{:S(2)}, u32[]{:S(2)}) collective-permute-start(bf16[8,3456]{1,0:T(8,128)(2,1)S(1)} %pack.1._.refs_0_), channel_id=1, source_target_pairs={{0,8},{4,12},{8,0},{12,4},{16,24},{20,28},{24,16},{28,20},{1,9},{5... | collective-permute-start | bytes 165896 | tf_op jit(solution)/shard_map/ppermute | solution.py:46
  12.1 6.9 %collective-permute-start.7 = (bf16[24,1024]{1,0:T(8,128)(2,1)S(1)}, bf16[24,1024]{1,0:T(8,128)(2,1)S(1)}, u32[]{:S(2)}, u32[]{:S(2)}) collective-permute-start(bf16[24,1024]{1,0:T(8,128)(2,1)S(1)} %get-tuple-element.34.acts_ref.refs_0_), channel_id=1, source_target_pairs={{0,2},{1,3},{2,0},{3,1},{4,6},{5,7},{6,4},{7,5},{8,10},{9,11},{10,... | collective-permute-start | bytes 147464 | tf_op jit(solution)/shard_map/ppermute | solution.py:46
  14.7 6.0 %collective-permute-start.6 = (bf16[24,1024]{1,0:T(8,128)(2,1)S(1)}, bf16[24,1024]{1,0:T(8,128)(2,1)S(1)}, u32[]{:S(2)}, u32[]{:S(2)}) collective-permute-start(bf16[24,1024]{1,0:T(8,128)(2,1)S(1)} %get-tuple-element.34.acts_ref.refs_0_), channel_id=1, source_target_pairs={{0,3},{1,2},{2,1},{3,0},{4,7},{5,6},{6,5},{7,4},{8,11},{9,10},{10,... | collective-permute-start | bytes 147464 | tf_op jit(solution)/shard_map/ppermute | solution.py:46
  16.0 4.6 %collective-permute-start.5 = (bf16[24,1024]{1,0:T(8,128)(2,1)S(1)}, bf16[24,1024]{1,0:T(8,128)(2,1)S(1)}, u32[]{:S(2)}, u32[]{:S(2)}) collective-permute-start(bf16[24,1024]{1,0:T(8,128)(2,1)S(1)} %get-tuple-element.34.acts_ref.refs_0_), channel_id=1, source_target_pairs={{0,1},{1,0},{2,3},{3,2},{4,5},{5,4},{6,7},{7,6},{8,9},{9,8},{10,11... | collective-permute-start | bytes 147464 | tf_op jit(solution)/shard_map/ppermute | solution.py:46
  21.9 1.4 %collective-permute-start.8 = (f32[24,1280]{1,0:T(8,128)S(1)}, f32[24,1280]{1,0:T(8,128)S(1)}, u32[]{:S(2)}, u32[]{:S(2)}) collective-permute-start(f32[24,1280]{1,0:T(8,128)S(1)} %recon_send.1), channel_id=1, source_target_pairs={{0,4},{4,0},{8,12},{12,8},{16,20},{20,16},{24,28},{28,24},{1,5},{5... | collective-permute-start | bytes 368648 | tf_op jit(solution)/shard_map/ppermute | solution.py:46
  23.4 5.3 %collective-permute-start.11 = (bf16[8,3584]{1,0:T(8,128)(2,1)S(1)}, bf16[8,3584]{1,0:T(8,128)(2,1)S(1)}, u32[]{:S(2)}, u32[]{:S(2)}) collective-permute-start(bf16[8,3584]{1,0:T(8,128)(2,1)S(1)} %pair_sum.1.refs_0_), channel_id=1, source_target_pairs={{0,24},{4,28},{8,16},{12,20},{16,8},{20,12},{24,0},{28,4},{1,25},{... | collective-permute-start | bytes 172040 | tf_op jit(solution)/shard_map/ppermute | solution.py:46
  24.9 4.9 %collective-permute-start.10 = (bf16[8,3584]{1,0:T(8,128)(2,1)S(1)}, bf16[8,3584]{1,0:T(8,128)(2,1)S(1)}, u32[]{:S(2)}, u32[]{:S(2)}) collective-permute-start(bf16[8,3584]{1,0:T(8,128)(2,1)S(1)} %pair_sum.1.refs_0_), channel_id=1, source_target_pairs={{0,16},{4,20},{8,24},{12,28},{16,0},{20,4},{24,8},{28,12},{1,17},{... | collective-permute-start | bytes 172040 | tf_op jit(solution)/shard_map/ppermute | solution.py:46
  25.6 4.4 %collective-permute-start.9 = (bf16[8,3584]{1,0:T(8,128)(2,1)S(1)}, bf16[8,3584]{1,0:T(8,128)(2,1)S(1)}, u32[]{:S(2)}, u32[]{:S(2)}) collective-permute-start(bf16[8,3584]{1,0:T(8,128)(2,1)S(1)} %pair_sum.1.refs_0_), channel_id=1, source_target_pairs={{0,8},{4,12},{8,0},{12,4},{16,24},{20,28},{24,16},{28,20},{1,9},{5... | collective-permute-start | bytes 172040 | tf_op jit(solution)/shard_map/ppermute | solution.py:46
  30.1 1.9 %collective-permute-start.12 = (bf16[32,1152]{1,0:T(8,128)(2,1)S(1)}, bf16[32,1152]{1,0:T(8,128)(2,1)S(1)}, u32[]{:S(2)}, u32[]{:S(2)}) collective-permute-start(bf16[32,1152]{1,0:T(8,128)(2,1)S(1)} %get-tuple-element.36.mine_ref), channel_id=1, source_target_pairs={{0,4},{4,0},{8,12},{12,8},{16,20},{20,16},{24,28},{28,24},{1,5},{5... | collective-permute-start | bytes 221192 | tf_op jit(solution)/shard_map/ppermute | solution.py:46
  34.3 9.1 %collective-permute-start.13 = (bf16[24,1152]{1,0:T(8,128)(2,1)S(1)}, bf16[24,1152]{1,0:T(8,128)(2,1)S(1)}, u32[]{:S(2)}, u32[]{:S(2)}) collective-permute-start(bf16[24,1152]{1,0:T(8,128)(2,1)S(1)} %get-tuple-element.48), channel_id=1, source_target_pairs={{0,2},{1,3},{2,0},{3,1},{4,6},{5,7},{6,4},{7,5},{8,10},{9,11},{10,... | collective-permute-start | bytes 165896 | tf_op jit(solution)/shard_map/ppermute | solution.py:46
  35.9 7.6 %collective-permute-start.14 = (bf16[24,1152]{1,0:T(8,128)(2,1)S(1)}, bf16[24,1152]{1,0:T(8,128)(2,1)S(1)}, u32[]{:S(2)}, u32[]{:S(2)}) collective-permute-start(bf16[24,1152]{1,0:T(8,128)(2,1)S(1)} %get-tuple-element.49), channel_id=1, source_target_pairs={{0,3},{1,2},{2,1},{3,0},{4,7},{5,6},{6,5},{7,4},{8,11},{9,10},{10,... | collective-permute-start | bytes 165896 | tf_op jit(solution)/shard_map/ppermute | solution.py:46
  36.9 6.6 %collective-permute-start.15 = (bf16[24,1152]{1,0:T(8,128)(2,1)S(1)}, bf16[24,1152]{1,0:T(8,128)(2,1)S(1)}, u32[]{:S(2)}, u32[]{:S(2)}) collective-permute-start(bf16[24,1152]{1,0:T(8,128)(2,1)S(1)} %get-tuple-element.50), channel_id=1, source_target_pairs={{0,1},{1,0},{2,3},{3,2},{4,5},{5,4},{6,7},{7,6},{8,9},{9,8},{10,11... | collective-permute-start | bytes 165896 | tf_op jit(solution)/shard_map/ppermute | solution.py:46

commit v7 on v6

--- a/solution.py
+++ b/solution.py
@@ -111,7 +111,7 @@
 
 
 def encode(rows, height, *refs):
-    *block_refs, enc_ref, cutoff_ref, x_ref, target_ref, acts_ref, gate_ref, sparse_ref, pen_ref = refs
+    *block_refs, enc_ref, cutoff_ref, x_ref, target_ref, acts_ref, gate_ref = refs
     tokens = x_ref.shape[0]
     blocks = jnp.concatenate([ref[...] for ref in block_refs], axis=0)
     gathered = gather_rows(rows, height, tokens, blocks)
@@ -122,16 +122,10 @@
     firing = preact > cutoff_ref[...]
     acts = jnp.where(firing, preact, 0.0).astype(BF16)
     acts_ref[...] = acts
-    wide = acts.astype(F32)
-    magnitude = jnp.sum(jnp.abs(wide), axis=0, keepdims=True) / tokens
-    sign = jnp.where(wide > 0, 1.0, jnp.where(wide < 0, -1.0, 0.0))
     gate_ref[...] = firing.astype(F32)
-    sparse_ref[...] = 2.0 * PENALTY_WEIGHT * magnitude * sign / tokens
-    pen = jnp.sum(magnitude * magnitude, axis=1, keepdims=True)
-    pen_ref[...] = jnp.broadcast_to(pen, pen_ref.shape)
-
-
-def recon_own(acts_ref, dec_hbm, total_ref, buf, sems):
+
+
+def recon_own(acts_ref, dec_hbm, total_ref, sparse_ref, pen_ref, buf, sems):
     me = lax.axis_index("layer")
     pieces = buf.shape[0]
     block = buf.shape[1]
@@ -139,6 +133,13 @@
     for i in range(pieces):
         copies.append(pltpu.make_async_copy(dec_hbm.at[me, pl.ds(i * block, block)], buf.at[i], sems.at[i]))
         copies[-1].start()
+    tokens = acts_ref.shape[0]
+    wide = acts_ref[...].astype(F32)
+    magnitude = jnp.sum(jnp.abs(wide), axis=0, keepdims=True) / tokens
+    sign = jnp.where(wide > 0, 1.0, jnp.where(wide < 0, -1.0, 0.0))
+    sparse_ref[...] = 2.0 * PENALTY_WEIGHT * magnitude * sign / tokens
+    pen = jnp.sum(magnitude * magnitude, axis=1, keepdims=True)
+    pen_ref[...] = jnp.broadcast_to(pen, pen_ref.shape)
     total = jnp.zeros(total_ref.shape, F32)
     for i in range(pieces):
         copies[i].wait()
@@ -346,10 +347,10 @@
         bit <<= len(pair) // 2 + 1
         if bit < feats:
             (block,) = call(stack, [shape((bit // 2 * height, width + half), BF16)], blocks, "stack")
-    x, targets, acts, gate, sparse, pen = call(
+    x, targets, acts, gate = call(
         functools.partial(encode, rows, height),
         [shape((tokens, width), BF16), shape((tokens, half), BF16)]
-        + [shape((tokens, features), BF16), shape((tokens, features), F32), shape((tokens, features), F32), shape((8, LANES), F32)],
+        + [shape((tokens, features), BF16), shape((tokens, features), F32)],
         (*blocks, encoder, cutoff),
         "encode",
         flops=2 * tokens * width * features,
@@ -359,9 +360,9 @@
     order = back[::-1]
     others = [swap(acts, "layer", k) for k in order]
     pieces = max(1, features // 256)
-    (total,) = call(
+    total, sparse, pen = call(
         recon_own,
-        [shape((tokens, width), F32)],
+        [shape((tokens, width), F32), shape((tokens, features), F32), shape((8, LANES), F32)],
         (acts, in_hbm(decoder)),
         "recon_own",
         scratch=[pltpu.VMEM((pieces, features // pieces, width), BF16), pltpu.SemaphoreType.DMA((pieces,))],

time: 47.8 us -> 47.7 us (level)
  no operation moved by 1% of the time
where the time goes in v7:
time: 47.7 us; the launch traced here: 47.5 us
  Pallas kernels  23.8 us (50%)
  starting transfers between devices  16.3 us (34%)
  waiting for transfers between devices  6.62 us (14%)
  between operations  0.78 us (2%)
    pallas_call x13, Pallas kernels, call(): pl.pallas_call(body, out_shape=outs, in_specs=in_specs or [WHOLE] * len(a...  23.8 us
    ppermute x16, starting transfers between devices, swap(): return lax.ppermute(x, axis, [(i, i ^ bits) for i in range(size)])  16.3 us
    ppermute x16, waiting for transfers between devices, swap(): return lax.ppermute(x, axis, [(i, i ^ bits) for i in range(size)])  6.62 us
  transfers between devices with their start and end apart: 16, of which 7 were waited for; matrix products, arithmetic and copies ran while one was open for 0% of the time, Pallas kernels for 31%

profile of v7, /device:TPU:0, one launch (start us, length us, event | category | flops | bytes accessed | tf_op | source)
XLA Modules:
  0.0 47.5 jit_solution(15254715387888695077)
XLA Ops:
  0.6 0.5 %collective-permute-start = (bf16[3,2304]{1,0:T(4,128)(2,1)}, bf16[3,2304]{1,0:T(4,128)(2,1)S(1)}, u32[]{:S(2)}, u32[]{:S(2)}) collective-permute-start(bf16[3,2304]{1,0:T(4,128)(2,1)} %bitcast.18), channel_id=1, source_target_pairs={{0,4},{4,0},{8,12},{12,8},{16,20},{20,16},{24,28},{28,24},{1,5},{5... | collective-permute-start | bytes 41480 | tf_op jit(solution)/shard_map/ppermute | solution.py:46
  1.2 1.0 %load_own.1 = (bf16[3,2304]{1,0:T(4,128)(2,1)S(1)}, bf16[3,2304]{1,0:T(4,128)(2,1)S(1)}, f32[1,1024]{1,0:T(1,128)S(1)}) custom-call(bf16[3,2304]{1,0:T(4,128)(2,1)} %bitcast.19, bf16[3,2304]{1,0:T(4,128)(2,1)} %bitcast.21, s32[1,1024]{1,0:T(1,128)} %thr_hbm.1), custom_call_target="tpu_custom_call" | custom-call | bytes 4718592 | tf_op jit(solution)/shard_map/load_own/pallas_call | solution.py:31
  2.6 3.7 %collective-permute-start.4 = (bf16[8,3456]{1,0:T(8,128)(2,1)S(1)}, bf16[8,3456]{1,0:T(8,128)(2,1)S(1)}, u32[]{:S(2)}, u32[]{:S(2)}) collective-permute-start(bf16[8,3456]{1,0:T(8,128)(2,1)S(1)} %pack.1._.refs_0_), channel_id=1, source_target_pairs={{0,24},{4,28},{8,16},{12,20},{16,8},{20,12},{24,0},{28,4},{1,25},{... | collective-permute-start | bytes 165896 | tf_op jit(solution)/shard_map/ppermute | solution.py:46
  6.9 2.3 %fetch.1.refs_4_ = bf16[2304,1024]{1,0:T(8,128)(2,1)S(1)} custom-call(bf16[8,3456]{1,0:T(8,128)(2,1)S(1)} %pack.1._.refs_0_, bf16[2304,1024]{1,0:T(8,128)(2,1)} %bitcast.17), custom_call_target="tpu_custom_call" | custom-call | bytes 9437184 | tf_op jit(solution)/shard_map/fetch/pallas_call | solution.py:31
  9.3 1.1 %collective-permute-done.3.refs_2_ = bf16[8,3456]{1,0:T(8,128)(2,1)S(1)} collective-permute-done((bf16[8,3456]{1,0:T(8,128)(2,1)S(1)}, bf16[8,3456]{1,0:T(8,128)(2,1)S(1)}, u32[]{:S(2)}, u32[]{:S(2)}) %collective-permute-start.3) | collective-permute-done | bytes 55328 | tf_op jit(solution)/shard_map/ppermute | solution.py:46
  10.9 1.0 %encode.1 = (bf16[24,2304]{1,0:T(8,128)(2,1)S(1)}, bf16[24,1152]{1,0:T(8,128)(2,1)S(1)}, bf16[24,1024]{1,0:T(8,128)(2,1)S(1)}, f32[24,1024]{1,0:T(8,128)S(1)}) custom-call(bf16[8,3456]{1,0:T(8,128)(2,1)S(1)} %pack.1._.refs_0_, bf16[8,3456]{1,0:T(8,128)(2,1)S(1)} %collective-permute-done.2.refs_1_, bf16[8,3456]{1,0:T(8,128)(2,1)S(1)} %collective-permute-done.3.refs_2_, ...), custom_call_target="tpu_custom_call" | custom-call | flops 113246208 | bytes 4718592 | tf_op jit(solution)/shard_map/encode/pallas_call | solution.py:31
  12.0 2.6 %collective-permute-start.7 = (bf16[24,1024]{1,0:T(8,128)(2,1)S(1)}, bf16[24,1024]{1,0:T(8,128)(2,1)S(1)}, u32[]{:S(2)}, u32[]{:S(2)}) collective-permute-start(bf16[24,1024]{1,0:T(8,128)(2,1)S(1)} %get-tuple-element.35.acts_ref.refs_0_), channel_id=1, source_target_pairs={{0,2},{1,3},{2,0},{3,1},{4,6},{5,7},{6,4},{7,5},{8,10},{9,11},{10,... | collective-permute-start | bytes 147464 | tf_op jit(solution)/shard_map/ppermute | solution.py:46
  14.6 1.3 %collective-permute-start.6 = (bf16[24,1024]{1,0:T(8,128)(2,1)S(1)}, bf16[24,1024]{1,0:T(8,128)(2,1)S(1)}, u32[]{:S(2)}, u32[]{:S(2)}) collective-permute-start(bf16[24,1024]{1,0:T(8,128)(2,1)S(1)} %get-tuple-element.35.acts_ref.refs_0_), channel_id=1, source_target_pairs={{0,3},{1,2},{2,1},{3,0},{4,7},{5,6},{6,5},{7,4},{8,11},{9,10},{10,... | collective-permute-start | bytes 147464 | tf_op jit(solution)/shard_map/ppermute | solution.py:46
  16.1 2.7 %recon_own.1 = (f32[24,2304]{1,0:T(8,128)S(1)}, f32[24,1024]{1,0:T(8,128)S(1)}, f32[8,128]{1,0:T(8,128)S(1)}) custom-call(bf16[24,1024]{1,0:T(8,128)(2,1)S(1)} %get-tuple-element.35.acts_ref.refs_0_, bf16[4,1024,2304]{2,1,0:T(8,128)(2,1)} %bitcast.10), custom_call_target="tpu_custom_call" | custom-call | flops 113246208 | bytes 4718592 | tf_op jit(solution)/shard_map/recon_own/pallas_call | solution.py:31
  18.9 1.7 %collective-permute-done.6.refs_1_.refs_2_ = bf16[24,1024]{1,0:T(8,128)(2,1)S(1)} collective-permute-done((bf16[24,1024]{1,0:T(8,128)(2,1)S(1)}, bf16[24,1024]{1,0:T(8,128)(2,1)S(1)}, u32[]{:S(2)}, u32[]{:S(2)}) %collective-permute-start.6) | collective-permute-done | bytes 49184 | tf_op jit(solution)/shard_map/ppermute | solution.py:46
  20.5 1.3 %recon_send.1 = f32[24,1280]{1,0:T(8,128)S(1)} custom-call(f32[24,2304]{1,0:T(8,128)S(1)} %get-tuple-element.36.total_ref, f32[8,128]{1,0:T(8,128)S(1)} %get-tuple-element.37.pen_ref, bf16[4,1024,2304]{2,1,0:T(8,128)(2,1)S(1)} %bitcast.11, bf16[24,1024]{1,0:T(8,128)(2,1)S(1)} %collective-permute-done.5.refs_0_.refs_1_, ...), custom_call_target="tpu_custom_call" | custom-call | flops 169869312 | bytes 7077888 | tf_op jit(solution)/shard_map/recon_send/pallas_call | solution.py:31
  21.9 1.3 %recon_keep.1.keep_ref = f32[24,1280]{1,0:T(8,128)S(1)} custom-call(f32[24,2304]{1,0:T(8,128)S(1)} %get-tuple-element.36.total_ref, f32[8,128]{1,0:T(8,128)S(1)} %get-tuple-element.37.pen_ref, bf16[4,1024,2304]{2,1,0:T(8,128)(2,1)S(1)} %bitcast.12, bf16[24,1024]{1,0:T(8,128)(2,1)S(1)} %collective-permute-done.5.refs_0_.refs_1_, ...), custom_call_target="tpu_custom_call" | custom-call | flops 169869312 | bytes 7077888 | tf_op jit(solution)/shard_map/recon_keep/pallas_call | solution.py:31
  23.3 1.5 %collective-permute-start.11 = (bf16[8,3584]{1,0:T(8,128)(2,1)S(1)}, bf16[8,3584]{1,0:T(8,128)(2,1)S(1)}, u32[]{:S(2)}, u32[]{:S(2)}) collective-permute-start(bf16[8,3584]{1,0:T(8,128)(2,1)S(1)} %pair_sum.1.refs_0_), channel_id=1, source_target_pairs={{0,24},{4,28},{8,16},{12,20},{16,8},{20,12},{24,0},{28,4},{1,25},{... | collective-permute-start | bytes 172040 | tf_op jit(solution)/shard_map/ppermute | solution.py:46
  24.8 0.6 %collective-permute-start.10 = (bf16[8,3584]{1,0:T(8,128)(2,1)S(1)}, bf16[8,3584]{1,0:T(8,128)(2,1)S(1)}, u32[]{:S(2)}, u32[]{:S(2)}) collective-permute-start(bf16[8,3584]{1,0:T(8,128)(2,1)S(1)} %pair_sum.1.refs_0_), channel_id=1, source_target_pairs={{0,16},{4,20},{8,24},{12,28},{16,0},{20,4},{24,8},{28,12},{1,17},{... | collective-permute-start | bytes 172040 | tf_op jit(solution)/shard_map/ppermute | solution.py:46
  25.5 1.4 %collective-permute-start.9 = (bf16[8,3584]{1,0:T(8,128)(2,1)S(1)}, bf16[8,3584]{1,0:T(8,128)(2,1)S(1)}, u32[]{:S(2)}, u32[]{:S(2)}) collective-permute-start(bf16[8,3584]{1,0:T(8,128)(2,1)S(1)} %pair_sum.1.refs_0_), channel_id=1, source_target_pairs={{0,8},{4,12},{8,0},{12,4},{16,24},{20,28},{24,16},{28,20},{1,9},{5... | collective-permute-start | bytes 172040 | tf_op jit(solution)/shard_map/ppermute | solution.py:46
  26.8 1.8 %collective-permute-done.11.refs_3_ = bf16[8,3584]{1,0:T(8,128)(2,1)S(1)} collective-permute-done((bf16[8,3584]{1,0:T(8,128)(2,1)S(1)}, bf16[8,3584]{1,0:T(8,128)(2,1)S(1)}, u32[]{:S(2)}, u32[]{:S(2)}) %collective-permute-start.11) | collective-permute-done | bytes 57376 | tf_op jit(solution)/shard_map/ppermute | solution.py:46
  28.7 1.1 %collective-permute-done.10.refs_2_ = bf16[8,3584]{1,0:T(8,128)(2,1)S(1)} collective-permute-done((bf16[8,3584]{1,0:T(8,128)(2,1)S(1)}, bf16[8,3584]{1,0:T(8,128)(2,1)S(1)}, u32[]{:S(2)}, u32[]{:S(2)}) %collective-permute-start.10) | collective-permute-done | bytes 57376 | tf_op jit(solution)/shard_map/ppermute | solution.py:46
  30.1 1.8 %act_first.1 = (f32[24,1024]{1,0:T(8,128)S(1)}, f32[24,1024]{1,0:T(8,128)S(1)}, f32[24,1024]{1,0:T(8,128)S(1)}) custom-call(bf16[32,1152]{1,0:T(8,128)(2,1)S(1)} %get-tuple-element.38.mine_ref, bf16[4,1024,2304]{2,1,0:T(8,128)(2,1)S(1)} %bitcast.13), custom_call_target="tpu_custom_call" | custom-call | flops 169869312 | bytes 7077888 | tf_op jit(solution)/shard_map/act_first/pallas_call | solution.py:31
  31.9 2.3 %act_second.1 = (bf16[24,2304]{1,0:T(8,128)(2,1)S(1)}, f32[8,128]{1,0:T(8,128)S(1)}, bf16[24,1152]{1,0:T(8,128)(2,1)S(1)}, bf16[24,1152]{1,0:T(8,128)(2,1)S(1)}, bf16[24,1152]{1,0:T(8,128)(2,1)S(1)}) custom-call(bf16[32,1152]{1,0:T(8,128)(2,1)S(1)} %get-tuple-element.38.mine_ref, bf16[32,1152]{1,0:T(8,128)(2,1)S(1)} %collective-permute-done.12.got_ref, ...), custom_call_target="tpu_custom_call" | custom-call | flops 169869312 | bytes 7077888 | tf_op jit(solution)/shard_map/act_second/pallas_call | solution.py:31
  34.2 1.6 %collective-permute-start.13 = (bf16[24,1152]{1,0:T(8,128)(2,1)S(1)}, bf16[24,1152]{1,0:T(8,128)(2,1)S(1)}, u32[]{:S(2)}, u32[]{:S(2)}) collective-permute-start(bf16[24,1152]{1,0:T(8,128)(2,1)S(1)} %get-tuple-element.50), channel_id=1, source_target_pairs={{0,2},{1,3},{2,0},{3,1},{4,6},{5,7},{6,4},{7,5},{8,10},{9,11},{10,... | collective-permute-start | bytes 165896 | tf_op jit(solution)/shard_map/ppermute | solution.py:46
  35.8 1.0 %collective-permute-start.14 = (bf16[24,1152]{1,0:T(8,128)(2,1)S(1)}, bf16[24,1152]{1,0:T(8,128)(2,1)S(1)}, u32[]{:S(2)}, u32[]{:S(2)}) collective-permute-start(bf16[24,1152]{1,0:T(8,128)(2,1)S(1)} %get-tuple-element.51), channel_id=1, source_target_pairs={{0,3},{1,2},{2,1},{3,0},{4,7},{5,6},{6,5},{7,4},{8,11},{9,10},{10,... | collective-permute-start | bytes 165896 | tf_op jit(solution)/shard_map/ppermute | solution.py:46
  36.8 1.0 %collective-permute-start.15 = (bf16[24,1152]{1,0:T(8,128)(2,1)S(1)}, bf16[24,1152]{1,0:T(8,128)(2,1)S(1)}, u32[]{:S(2)}, u32[]{:S(2)}) collective-permute-start(bf16[24,1152]{1,0:T(8,128)(2,1)S(1)} %get-tuple-element.52), channel_id=1, source_target_pairs={{0,1},{1,0},{2,3},{3,2},{4,5},{5,4},{6,7},{7,6},{8,9},{9,8},{10,11... | collective-permute-start | bytes 165896 | tf_op jit(solution)/shard_map/ppermute | solution.py:46
  37.8 5.6 %first_grads.1 = (bf16[4,1024,2304]{2,1,0:T(8,128)(2,1)}, f32[24,1024]{1,0:T(8,128)S(1)}) custom-call(bf16[24,2304]{1,0:T(8,128)(2,1)S(1)} %get-tuple-element.43.grad_ref, bf16[4,1024,2304]{2,1,0:T(8,128)(2,1)S(1)} %bitcast.15, bf16[24,1024]{1,0:T(8,128)(2,1)S(1)} %get-tuple-element.35.acts_ref.refs_0_, ...), custom_call_target="tpu_custom_call" | custom-call | flops 452984832 | bytes 14155776 | tf_op jit(solution)/shard_map/first_grads/pallas_call | solution.py:31
  43.4 4.1 %last_grads.1 = (bf16[4,1024,2304]{2,1,0:T(8,128)(2,1)}, bf16[2304,1024]{1,0:T(8,128)(2,1)}, f32[1,1]{1,0:T(1,128)}, bf16[3,2304]{1,0:T(4,128)(2,1)}) custom-call(bf16[24,2304]{1,0:T(8,128)(2,1)S(1)} %get-tuple-element.43.grad_ref, f32[8,1152]{1,0:T(8,128)S(1)} %get-tuple-element.44.own_ref, ...), custom_call_target="tpu_custom_call", output_to_operand_aliasing={{0}: (12, {})} | custom-call | flops 226492416 | bytes 9437184 | tf_op jit(solution)/shard_map/last_grads/pallas_call | solution.py:31
  (23 shorter events, 2.3 us)
Async XLA Ops:
  0.6 19.9 %copy-start = (bf16[4,1,1024,2304]{3,2,1,0:T(8,128)(2,1)S(1)}, bf16[4,1,1024,2304]{3,2,1,0:T(8,128)(2,1)}, u32[]{:S(2)}) copy-start(bf16[4,1,1024,2304]{3,2,1,0:T(8,128)(2,1)} %param.8) | copy-start | bytes 56623108
  0.6 1.6 %collective-permute-start = (bf16[3,2304]{1,0:T(4,128)(2,1)}, bf16[3,2304]{1,0:T(4,128)(2,1)S(1)}, u32[]{:S(2)}, u32[]{:S(2)}) collective-permute-start(bf16[3,2304]{1,0:T(4,128)(2,1)} %bitcast.18), channel_id=1, source_target_pairs={{0,4},{4,0},{8,12},{12,8},{16,20},{20,16},{24,28},{28,24},{1,5},{5... | collective-permute-start | bytes 41480 | tf_op jit(solution)/shard_map/ppermute | solution.py:46
  1.2 1.4 %collective-permute-start.1 = (bf16[3,2304]{1,0:T(4,128)(2,1)}, bf16[3,2304]{1,0:T(4,128)(2,1)S(1)}, u32[]{:S(2)}, u32[]{:S(2)}) collective-permute-start(bf16[3,2304]{1,0:T(4,128)(2,1)} %bitcast.20), channel_id=1, source_target_pairs={{0,4},{4,0},{8,12},{12,8},{16,20},{20,16},{24,28},{28,24},{1,5},{5... | collective-permute-start | bytes 41480 | tf_op jit(solution)/shard_map/ppermute | solution.py:46
  2.6 6.7 %collective-permute-start.4 = (bf16[8,3456]{1,0:T(8,128)(2,1)S(1)}, bf16[8,3456]{1,0:T(8,128)(2,1)S(1)}, u32[]{:S(2)}, u32[]{:S(2)}) collective-permute-start(bf16[8,3456]{1,0:T(8,128)(2,1)S(1)} %pack.1._.refs_0_), channel_id=1, source_target_pairs={{0,24},{4,28},{8,16},{12,20},{16,8},{20,12},{24,0},{28,4},{1,25},{... | collective-permute-start | bytes 165896 | tf_op jit(solution)/shard_map/ppermute | solution.py:46
  6.3 4.2 %collective-permute-start.3 = (bf16[8,3456]{1,0:T(8,128)(2,1)S(1)}, bf16[8,3456]{1,0:T(8,128)(2,1)S(1)}, u32[]{:S(2)}, u32[]{:S(2)}) collective-permute-start(bf16[8,3456]{1,0:T(8,128)(2,1)S(1)} %pack.1._.refs_0_), channel_id=1, source_target_pairs={{0,16},{4,20},{8,24},{12,28},{16,0},{20,4},{24,8},{28,12},{1,17},{... | collective-permute-start | bytes 165896 | tf_op jit(solution)/shard_map/ppermute | solution.py:46
  6.8 4.2 %collective-permute-start.2 = (bf16[8,3456]{1,0:T(8,128)(2,1)S(1)}, bf16[8,3456]{1,0:T(8,128)(2,1)S(1)}, u32[]{:S(2)}, u32[]{:S(2)}) collective-permute-start(bf16[8,3456]{1,0:T(8,128)(2,1)S(1)} %pack.1._.refs_0_), channel_id=1, source_target_pairs={{0,8},{4,12},{8,0},{12,4},{16,24},{20,28},{24,16},{28,20},{1,9},{5... | collective-permute-start | bytes 165896 | tf_op jit(solution)/shard_map/ppermute | solution.py:46
  12.0 6.9 %collective-permute-start.7 = (bf16[24,1024]{1,0:T(8,128)(2,1)S(1)}, bf16[24,1024]{1,0:T(8,128)(2,1)S(1)}, u32[]{:S(2)}, u32[]{:S(2)}) collective-permute-start(bf16[24,1024]{1,0:T(8,128)(2,1)S(1)} %get-tuple-element.35.acts_ref.refs_0_), channel_id=1, source_target_pairs={{0,2},{1,3},{2,0},{3,1},{4,6},{5,7},{6,4},{7,5},{8,10},{9,11},{10,... | collective-permute-start | bytes 147464 | tf_op jit(solution)/shard_map/ppermute | solution.py:46
  14.6 6.0 %collective-permute-start.6 = (bf16[24,1024]{1,0:T(8,128)(2,1)S(1)}, bf16[24,1024]{1,0:T(8,128)(2,1)S(1)}, u32[]{:S(2)}, u32[]{:S(2)}) collective-permute-start(bf16[24,1024]{1,0:T(8,128)(2,1)S(1)} %get-tuple-element.35.acts_ref.refs_0_), channel_id=1, source_target_pairs={{0,3},{1,2},{2,1},{3,0},{4,7},{5,6},{6,5},{7,4},{8,11},{9,10},{10,... | collective-permute-start | bytes 147464 | tf_op jit(solution)/shard_map/ppermute | solution.py:46
  15.9 4.6 %collective-permute-start.5 = (bf16[24,1024]{1,0:T(8,128)(2,1)S(1)}, bf16[24,1024]{1,0:T(8,128)(2,1)S(1)}, u32[]{:S(2)}, u32[]{:S(2)}) collective-permute-start(bf16[24,1024]{1,0:T(8,128)(2,1)S(1)} %get-tuple-element.35.acts_ref.refs_0_), channel_id=1, source_target_pairs={{0,1},{1,0},{2,3},{3,2},{4,5},{5,4},{6,7},{7,6},{8,9},{9,8},{10,11... | collective-permute-start | bytes 147464 | tf_op jit(solution)/shard_map/ppermute | solution.py:46
  21.8 1.4 %collective-permute-start.8 = (f32[24,1280]{1,0:T(8,128)S(1)}, f32[24,1280]{1,0:T(8,128)S(1)}, u32[]{:S(2)}, u32[]{:S(2)}) collective-permute-start(f32[24,1280]{1,0:T(8,128)S(1)} %recon_send.1), channel_id=1, source_target_pairs={{0,4},{4,0},{8,12},{12,8},{16,20},{20,16},{24,28},{28,24},{1,5},{5... | collective-permute-start | bytes 368648 | tf_op jit(solution)/shard_map/ppermute | solution.py:46
  23.3 5.3 %collective-permute-start.11 = (bf16[8,3584]{1,0:T(8,128)(2,1)S(1)}, bf16[8,3584]{1,0:T(8,128)(2,1)S(1)}, u32[]{:S(2)}, u32[]{:S(2)}) collective-permute-start(bf16[8,3584]{1,0:T(8,128)(2,1)S(1)} %pair_sum.1.refs_0_), channel_id=1, source_target_pairs={{0,24},{4,28},{8,16},{12,20},{16,8},{20,12},{24,0},{28,4},{1,25},{... | collective-permute-start | bytes 172040 | tf_op jit(solution)/shard_map/ppermute | solution.py:46
  24.8 4.9 %collective-permute-start.10 = (bf16[8,3584]{1,0:T(8,128)(2,1)S(1)}, bf16[8,3584]{1,0:T(8,128)(2,1)S(1)}, u32[]{:S(2)}, u32[]{:S(2)}) collective-permute-start(bf16[8,3584]{1,0:T(8,128)(2,1)S(1)} %pair_sum.1.refs_0_), channel_id=1, source_target_pairs={{0,16},{4,20},{8,24},{12,28},{16,0},{20,4},{24,8},{28,12},{1,17},{... | collective-permute-start | bytes 172040 | tf_op jit(solution)/shard_map/ppermute | solution.py:46
  25.5 4.4 %collective-permute-start.9 = (bf16[8,3584]{1,0:T(8,128)(2,1)S(1)}, bf16[8,3584]{1,0:T(8,128)(2,1)S(1)}, u32[]{:S(2)}, u32[]{:S(2)}) collective-permute-start(bf16[8,3584]{1,0:T(8,128)(2,1)S(1)} %pair_sum.1.refs_0_), channel_id=1, source_target_pairs={{0,8},{4,12},{8,0},{12,4},{16,24},{20,28},{24,16},{28,20},{1,9},{5... | collective-permute-start | bytes 172040 | tf_op jit(solution)/shard_map/ppermute | solution.py:46
  30.0 1.9 %collective-permute-start.12 = (bf16[32,1152]{1,0:T(8,128)(2,1)S(1)}, bf16[32,1152]{1,0:T(8,128)(2,1)S(1)}, u32[]{:S(2)}, u32[]{:S(2)}) collective-permute-start(bf16[32,1152]{1,0:T(8,128)(2,1)S(1)} %get-tuple-element.38.mine_ref), channel_id=1, source_target_pairs={{0,4},{4,0},{8,12},{12,8},{16,20},{20,16},{24,28},{28,24},{1,5},{5... | collective-permute-start | bytes 221192 | tf_op jit(solution)/shard_map/ppermute | solution.py:46
  34.2 9.1 %collective-permute-start.13 = (bf16[24,1152]{1,0:T(8,128)(2,1)S(1)}, bf16[24,1152]{1,0:T(8,128)(2,1)S(1)}, u32[]{:S(2)}, u32[]{:S(2)}) collective-permute-start(bf16[24,1152]{1,0:T(8,128)(2,1)S(1)} %get-tuple-element.50), channel_id=1, source_target_pairs={{0,2},{1,3},{2,0},{3,1},{4,6},{5,7},{6,4},{7,5},{8,10},{9,11},{10,... | collective-permute-start | bytes 165896 | tf_op jit(solution)/shard_map/ppermute | solution.py:46
  35.8 7.6 %collective-permute-start.14 = (bf16[24,1152]{1,0:T(8,128)(2,1)S(1)}, bf16[24,1152]{1,0:T(8,128)(2,1)S(1)}, u32[]{:S(2)}, u32[]{:S(2)}) collective-permute-start(bf16[24,1152]{1,0:T(8,128)(2,1)S(1)} %get-tuple-element.51), channel_id=1, source_target_pairs={{0,3},{1,2},{2,1},{3,0},{4,7},{5,6},{6,5},{7,4},{8,11},{9,10},{10,... | collective-permute-start | bytes 165896 | tf_op jit(solution)/shard_map/ppermute | solution.py:46
  36.8 6.6 %collective-permute-start.15 = (bf16[24,1152]{1,0:T(8,128)(2,1)S(1)}, bf16[24,1152]{1,0:T(8,128)(2,1)S(1)}, u32[]{:S(2)}, u32[]{:S(2)}) collective-permute-start(bf16[24,1152]{1,0:T(8,128)(2,1)S(1)} %get-tuple-element.52), channel_id=1, source_target_pairs={{0,1},{1,0},{2,3},{3,2},{4,5},{5,4},{6,7},{7,6},{8,9},{9,8},{10,11... | collective-permute-start | bytes 165896 | tf_op jit(solution)/shard_map/ppermute | solution.py:46

commit v8 on v6

--- a/solution.py
+++ b/solution.py
@@ -358,7 +358,7 @@
     back = exchange_order(layers)
     order = back[::-1]
     others = [swap(acts, "layer", k) for k in order]
-    pieces = max(1, features // 256)
+    pieces = max(1, features // 512)
     (total,) = call(
         recon_own,
         [shape((tokens, width), F32)],

time: 47.8 us -> 47.8 us (level)
  waiting for transfers between devices: 6.64 us -> 6.02 us
  Pallas kernels: 23.9 us -> 24.5 us
    pallas_call x13, Pallas kernels: 23.9 us -> 24.5 us  [call(): pl.pallas_call(body, out_shape=outs, in_specs=in_specs or [WHOLE] * len(a...]
    ppermute x16, waiting for transfers between devices: 6.64 us -> 6.02 us  [swap(): return lax.ppermute(x, axis, [(i, i ^ bits) for i in range(size)])]
  transfers between devices with their start and end apart: 16 -> 16, of which waited for: 7 -> 7; matrix products, arithmetic and copies ran while one was open for 0% -> 0% of each run, Pallas kernels for 31% -> 32%
where the time goes in v8:
time: 47.8 us; the launch traced here: 47.6 us
  Pallas kernels  24.5 us (51%)
  starting transfers between devices  16.3 us (34%)
  waiting for transfers between devices  6.02 us (13%)
  between operations  0.78 us (2%)
    pallas_call x13, Pallas kernels, call(): pl.pallas_call(body, out_shape=outs, in_specs=in_specs or [WHOLE] * len(a...  24.5 us
    ppermute x16, starting transfers between devices, swap(): return lax.ppermute(x, axis, [(i, i ^ bits) for i in range(size)])  16.3 us
    ppermute x16, waiting for transfers between devices, swap(): return lax.ppermute(x, axis, [(i, i ^ bits) for i in range(size)])  6.02 us
  transfers between devices with their start and end apart: 16, of which 7 were waited for; matrix products, arithmetic and copies ran while one was open for 0% of the time, Pallas kernels for 32%

profile of v8, /device:TPU:0, one launch (start us, length us, event | category | flops | bytes accessed | tf_op | source)
XLA Modules:
  0.0 47.6 jit_solution(1518704285485500545)
XLA Ops:
  0.6 0.5 %collective-permute-start = (bf16[3,2304]{1,0:T(4,128)(2,1)}, bf16[3,2304]{1,0:T(4,128)(2,1)S(1)}, u32[]{:S(2)}, u32[]{:S(2)}) collective-permute-start(bf16[3,2304]{1,0:T(4,128)(2,1)} %bitcast.18), channel_id=1, source_target_pairs={{0,4},{4,0},{8,12},{12,8},{16,20},{20,16},{24,28},{28,24},{1,5},{5... | collective-permute-start | bytes 41480 | tf_op jit(solution)/shard_map/ppermute | solution.py:46
  1.2 1.0 %load_own.1 = (bf16[3,2304]{1,0:T(4,128)(2,1)S(1)}, bf16[3,2304]{1,0:T(4,128)(2,1)S(1)}, f32[1,1024]{1,0:T(1,128)S(1)}) custom-call(bf16[3,2304]{1,0:T(4,128)(2,1)} %bitcast.19, bf16[3,2304]{1,0:T(4,128)(2,1)} %bitcast.21, s32[1,1024]{1,0:T(1,128)} %thr_hbm.1), custom_call_target="tpu_custom_call" | custom-call | bytes 4718592 | tf_op jit(solution)/shard_map/load_own/pallas_call | solution.py:31
  2.6 3.7 %collective-permute-start.4 = (bf16[8,3456]{1,0:T(8,128)(2,1)S(1)}, bf16[8,3456]{1,0:T(8,128)(2,1)S(1)}, u32[]{:S(2)}, u32[]{:S(2)}) collective-permute-start(bf16[8,3456]{1,0:T(8,128)(2,1)S(1)} %pack.1._.refs_0_), channel_id=1, source_target_pairs={{0,24},{4,28},{8,16},{12,20},{16,8},{20,12},{24,0},{28,4},{1,25},{... | collective-permute-start | bytes 165896 | tf_op jit(solution)/shard_map/ppermute | solution.py:46
  6.3 0.5 %collective-permute-start.3 = (bf16[8,3456]{1,0:T(8,128)(2,1)S(1)}, bf16[8,3456]{1,0:T(8,128)(2,1)S(1)}, u32[]{:S(2)}, u32[]{:S(2)}) collective-permute-start(bf16[8,3456]{1,0:T(8,128)(2,1)S(1)} %pack.1._.refs_0_), channel_id=1, source_target_pairs={{0,16},{4,20},{8,24},{12,28},{16,0},{20,4},{24,8},{28,12},{1,17},{... | collective-permute-start | bytes 165896 | tf_op jit(solution)/shard_map/ppermute | solution.py:46
  6.9 2.3 %fetch.1.refs_4_ = bf16[2304,1024]{1,0:T(8,128)(2,1)S(1)} custom-call(bf16[8,3456]{1,0:T(8,128)(2,1)S(1)} %pack.1._.refs_0_, bf16[2304,1024]{1,0:T(8,128)(2,1)} %bitcast.17), custom_call_target="tpu_custom_call" | custom-call | bytes 9437184 | tf_op jit(solution)/shard_map/fetch/pallas_call | solution.py:31
  9.3 1.1 %collective-permute-done.3.refs_2_ = bf16[8,3456]{1,0:T(8,128)(2,1)S(1)} collective-permute-done((bf16[8,3456]{1,0:T(8,128)(2,1)S(1)}, bf16[8,3456]{1,0:T(8,128)(2,1)S(1)}, u32[]{:S(2)}, u32[]{:S(2)}) %collective-permute-start.3) | collective-permute-done | bytes 55328 | tf_op jit(solution)/shard_map/ppermute | solution.py:46
  10.9 1.1 %encode.1 = (bf16[24,2304]{1,0:T(8,128)(2,1)S(1)}, bf16[24,1152]{1,0:T(8,128)(2,1)S(1)}, bf16[24,1024]{1,0:T(8,128)(2,1)S(1)}, f32[24,1024]{1,0:T(8,128)S(1)}, f...) custom-call(bf16[8,3456]{1,0:T(8,128)(2,1)S(1)} %pack.1._.refs_0_, bf16[8,3456]{1,0:T(8,128)(2,1)S(1)} %collective-permute-done.2.refs_1_, ...), custom_call_target="tpu_custom_call" | custom-call | flops 113246208 | bytes 4718592 | tf_op jit(solution)/shard_map/encode/pallas_call | solution.py:31
  12.1 2.6 %collective-permute-start.7 = (bf16[24,1024]{1,0:T(8,128)(2,1)S(1)}, bf16[24,1024]{1,0:T(8,128)(2,1)S(1)}, u32[]{:S(2)}, u32[]{:S(2)}) collective-permute-start(bf16[24,1024]{1,0:T(8,128)(2,1)S(1)} %get-tuple-element.34.acts_ref.refs_0_), channel_id=1, source_target_pairs={{0,2},{1,3},{2,0},{3,1},{4,6},{5,7},{6,4},{7,5},{8,10},{9,11},{10,... | collective-permute-start | bytes 147464 | tf_op jit(solution)/shard_map/ppermute | solution.py:46
  14.7 1.3 %collective-permute-start.6 = (bf16[24,1024]{1,0:T(8,128)(2,1)S(1)}, bf16[24,1024]{1,0:T(8,128)(2,1)S(1)}, u32[]{:S(2)}, u32[]{:S(2)}) collective-permute-start(bf16[24,1024]{1,0:T(8,128)(2,1)S(1)} %get-tuple-element.34.acts_ref.refs_0_), channel_id=1, source_target_pairs={{0,3},{1,2},{2,1},{3,0},{4,7},{5,6},{6,5},{7,4},{8,11},{9,10},{10,... | collective-permute-start | bytes 147464 | tf_op jit(solution)/shard_map/ppermute | solution.py:46
  16.2 3.3 %recon_own.1.total_ref = f32[24,2304]{1,0:T(8,128)S(1)} custom-call(bf16[24,1024]{1,0:T(8,128)(2,1)S(1)} %get-tuple-element.34.acts_ref.refs_0_, bf16[4,1024,2304]{2,1,0:T(8,128)(2,1)} %bitcast.10), custom_call_target="tpu_custom_call" | custom-call | flops 113246208 | bytes 4718592 | tf_op jit(solution)/shard_map/recon_own/pallas_call | solution.py:31
  19.6 1.1 %collective-permute-done.6.refs_1_.refs_2_ = bf16[24,1024]{1,0:T(8,128)(2,1)S(1)} collective-permute-done((bf16[24,1024]{1,0:T(8,128)(2,1)S(1)}, bf16[24,1024]{1,0:T(8,128)(2,1)S(1)}, u32[]{:S(2)}, u32[]{:S(2)}) %collective-permute-start.6) | collective-permute-done | bytes 49184 | tf_op jit(solution)/shard_map/ppermute | solution.py:46
  20.6 1.3 %recon_send.1 = f32[24,1280]{1,0:T(8,128)S(1)} custom-call(f32[24,2304]{1,0:T(8,128)S(1)} %recon_own.1.total_ref, f32[8,128]{1,0:T(8,128)S(1)} %get-tuple-element.35.pen_ref, bf16[4,1024,2304]{2,1,0:T(8,128)(2,1)S(1)} %bitcast.11, bf16[24,1024]{1,0:T(8,128)(2,1)S(1)} %collective-permute-done.5.refs_0_.refs_1_, ...), custom_call_target="tpu_custom_call" | custom-call | flops 169869312 | bytes 7077888 | tf_op jit(solution)/shard_map/recon_send/pallas_call | solution.py:31
  22.0 1.3 %recon_keep.1.keep_ref = f32[24,1280]{1,0:T(8,128)S(1)} custom-call(f32[24,2304]{1,0:T(8,128)S(1)} %recon_own.1.total_ref, f32[8,128]{1,0:T(8,128)S(1)} %get-tuple-element.35.pen_ref, bf16[4,1024,2304]{2,1,0:T(8,128)(2,1)S(1)} %bitcast.12, bf16[24,1024]{1,0:T(8,128)(2,1)S(1)} %collective-permute-done.5.refs_0_.refs_1_, ...), custom_call_target="tpu_custom_call" | custom-call | flops 169869312 | bytes 7077888 | tf_op jit(solution)/shard_map/recon_keep/pallas_call | solution.py:31
  23.4 1.5 %collective-permute-start.11 = (bf16[8,3584]{1,0:T(8,128)(2,1)S(1)}, bf16[8,3584]{1,0:T(8,128)(2,1)S(1)}, u32[]{:S(2)}, u32[]{:S(2)}) collective-permute-start(bf16[8,3584]{1,0:T(8,128)(2,1)S(1)} %pair_sum.1.refs_0_), channel_id=1, source_target_pairs={{0,24},{4,28},{8,16},{12,20},{16,8},{20,12},{24,0},{28,4},{1,25},{... | collective-permute-start | bytes 172040 | tf_op jit(solution)/shard_map/ppermute | solution.py:46
  24.9 0.6 %collective-permute-start.10 = (bf16[8,3584]{1,0:T(8,128)(2,1)S(1)}, bf16[8,3584]{1,0:T(8,128)(2,1)S(1)}, u32[]{:S(2)}, u32[]{:S(2)}) collective-permute-start(bf16[8,3584]{1,0:T(8,128)(2,1)S(1)} %pair_sum.1.refs_0_), channel_id=1, source_target_pairs={{0,16},{4,20},{8,24},{12,28},{16,0},{20,4},{24,8},{28,12},{1,17},{... | collective-permute-start | bytes 172040 | tf_op jit(solution)/shard_map/ppermute | solution.py:46
  25.6 1.4 %collective-permute-start.9 = (bf16[8,3584]{1,0:T(8,128)(2,1)S(1)}, bf16[8,3584]{1,0:T(8,128)(2,1)S(1)}, u32[]{:S(2)}, u32[]{:S(2)}) collective-permute-start(bf16[8,3584]{1,0:T(8,128)(2,1)S(1)} %pair_sum.1.refs_0_), channel_id=1, source_target_pairs={{0,8},{4,12},{8,0},{12,4},{16,24},{20,28},{24,16},{28,20},{1,9},{5... | collective-permute-start | bytes 172040 | tf_op jit(solution)/shard_map/ppermute | solution.py:46
  26.9 1.8 %collective-permute-done.11.refs_3_ = bf16[8,3584]{1,0:T(8,128)(2,1)S(1)} collective-permute-done((bf16[8,3584]{1,0:T(8,128)(2,1)S(1)}, bf16[8,3584]{1,0:T(8,128)(2,1)S(1)}, u32[]{:S(2)}, u32[]{:S(2)}) %collective-permute-start.11) | collective-permute-done | bytes 57376 | tf_op jit(solution)/shard_map/ppermute | solution.py:46
  28.7 1.1 %collective-permute-done.10.refs_2_ = bf16[8,3584]{1,0:T(8,128)(2,1)S(1)} collective-permute-done((bf16[8,3584]{1,0:T(8,128)(2,1)S(1)}, bf16[8,3584]{1,0:T(8,128)(2,1)S(1)}, u32[]{:S(2)}, u32[]{:S(2)}) %collective-permute-start.10) | collective-permute-done | bytes 57376 | tf_op jit(solution)/shard_map/ppermute | solution.py:46
  30.2 1.8 %act_first.1 = (f32[24,1024]{1,0:T(8,128)S(1)}, f32[24,1024]{1,0:T(8,128)S(1)}, f32[24,1024]{1,0:T(8,128)S(1)}) custom-call(bf16[32,1152]{1,0:T(8,128)(2,1)S(1)} %get-tuple-element.36.mine_ref, bf16[4,1024,2304]{2,1,0:T(8,128)(2,1)S(1)} %bitcast.13), custom_call_target="tpu_custom_call" | custom-call | flops 169869312 | bytes 7077888 | tf_op jit(solution)/shard_map/act_first/pallas_call | solution.py:31
  32.0 2.3 %act_second.1 = (bf16[24,2304]{1,0:T(8,128)(2,1)S(1)}, f32[8,128]{1,0:T(8,128)S(1)}, bf16[24,1152]{1,0:T(8,128)(2,1)S(1)}, bf16[24,1152]{1,0:T(8,128)(2,1)S(1)}, bf16[24,1152]{1,0:T(8,128)(2,1)S(1)}) custom-call(bf16[32,1152]{1,0:T(8,128)(2,1)S(1)} %get-tuple-element.36.mine_ref, bf16[32,1152]{1,0:T(8,128)(2,1)S(1)} %collective-permute-done.12.got_ref, ...), custom_call_target="tpu_custom_call" | custom-call | flops 169869312 | bytes 7077888 | tf_op jit(solution)/shard_map/act_second/pallas_call | solution.py:31
  34.3 1.8 %collective-permute-start.13 = (bf16[24,1152]{1,0:T(8,128)(2,1)S(1)}, bf16[24,1152]{1,0:T(8,128)(2,1)S(1)}, u32[]{:S(2)}, u32[]{:S(2)}) collective-permute-start(bf16[24,1152]{1,0:T(8,128)(2,1)S(1)} %get-tuple-element.48), channel_id=1, source_target_pairs={{0,2},{1,3},{2,0},{3,1},{4,6},{5,7},{6,4},{7,5},{8,10},{9,11},{10,... | collective-permute-start | bytes 165896 | tf_op jit(solution)/shard_map/ppermute | solution.py:46
  36.1 1.3 %collective-permute-start.14 = (bf16[24,1152]{1,0:T(8,128)(2,1)S(1)}, bf16[24,1152]{1,0:T(8,128)(2,1)S(1)}, u32[]{:S(2)}, u32[]{:S(2)}) collective-permute-start(bf16[24,1152]{1,0:T(8,128)(2,1)S(1)} %get-tuple-element.49), channel_id=1, source_target_pairs={{0,3},{1,2},{2,1},{3,0},{4,7},{5,6},{6,5},{7,4},{8,11},{9,10},{10,... | collective-permute-start | bytes 165896 | tf_op jit(solution)/shard_map/ppermute | solution.py:46
  37.9 5.6 %first_grads.1 = (bf16[4,1024,2304]{2,1,0:T(8,128)(2,1)}, f32[24,1024]{1,0:T(8,128)S(1)}) custom-call(bf16[24,2304]{1,0:T(8,128)(2,1)S(1)} %get-tuple-element.41.grad_ref, bf16[4,1024,2304]{2,1,0:T(8,128)(2,1)S(1)} %bitcast.15, bf16[24,1024]{1,0:T(8,128)(2,1)S(1)} %get-tuple-element.34.acts_ref.refs_0_, ...), custom_call_target="tpu_custom_call" | custom-call | flops 452984832 | bytes 14155776 | tf_op jit(solution)/shard_map/first_grads/pallas_call | solution.py:31
  43.5 4.1 %last_grads.1 = (bf16[4,1024,2304]{2,1,0:T(8,128)(2,1)}, bf16[2304,1024]{1,0:T(8,128)(2,1)}, f32[1,1]{1,0:T(1,128)}, bf16[3,2304]{1,0:T(4,128)(2,1)}) custom-call(bf16[24,2304]{1,0:T(8,128)(2,1)S(1)} %get-tuple-element.41.grad_ref, f32[8,1152]{1,0:T(8,128)S(1)} %get-tuple-element.42.own_ref, ...), custom_call_target="tpu_custom_call", output_to_operand_aliasing={{0}: (12, {})} | custom-call | flops 226492416 | bytes 9437184 | tf_op jit(solution)/shard_map/last_grads/pallas_call | solution.py:31
  (23 shorter events, 2.1 us)
Async XLA Ops:
  0.6 20.0 %copy-start = (bf16[4,1,1024,2304]{3,2,1,0:T(8,128)(2,1)S(1)}, bf16[4,1,1024,2304]{3,2,1,0:T(8,128)(2,1)}, u32[]{:S(2)}) copy-start(bf16[4,1,1024,2304]{3,2,1,0:T(8,128)(2,1)} %param.8) | copy-start | bytes 56623108
  0.6 1.6 %collective-permute-start = (bf16[3,2304]{1,0:T(4,128)(2,1)}, bf16[3,2304]{1,0:T(4,128)(2,1)S(1)}, u32[]{:S(2)}, u32[]{:S(2)}) collective-permute-start(bf16[3,2304]{1,0:T(4,128)(2,1)} %bitcast.18), channel_id=1, source_target_pairs={{0,4},{4,0},{8,12},{12,8},{16,20},{20,16},{24,28},{28,24},{1,5},{5... | collective-permute-start | bytes 41480 | tf_op jit(solution)/shard_map/ppermute | solution.py:46
  1.2 1.4 %collective-permute-start.1 = (bf16[3,2304]{1,0:T(4,128)(2,1)}, bf16[3,2304]{1,0:T(4,128)(2,1)S(1)}, u32[]{:S(2)}, u32[]{:S(2)}) collective-permute-start(bf16[3,2304]{1,0:T(4,128)(2,1)} %bitcast.20), channel_id=1, source_target_pairs={{0,4},{4,0},{8,12},{12,8},{16,20},{20,16},{24,28},{28,24},{1,5},{5... | collective-permute-start | bytes 41480 | tf_op jit(solution)/shard_map/ppermute | solution.py:46
  2.6 6.7 %collective-permute-start.4 = (bf16[8,3456]{1,0:T(8,128)(2,1)S(1)}, bf16[8,3456]{1,0:T(8,128)(2,1)S(1)}, u32[]{:S(2)}, u32[]{:S(2)}) collective-permute-start(bf16[8,3456]{1,0:T(8,128)(2,1)S(1)} %pack.1._.refs_0_), channel_id=1, source_target_pairs={{0,24},{4,28},{8,16},{12,20},{16,8},{20,12},{24,0},{28,4},{1,25},{... | collective-permute-start | bytes 165896 | tf_op jit(solution)/shard_map/ppermute | solution.py:46
  6.3 4.2 %collective-permute-start.3 = (bf16[8,3456]{1,0:T(8,128)(2,1)S(1)}, bf16[8,3456]{1,0:T(8,128)(2,1)S(1)}, u32[]{:S(2)}, u32[]{:S(2)}) collective-permute-start(bf16[8,3456]{1,0:T(8,128)(2,1)S(1)} %pack.1._.refs_0_), channel_id=1, source_target_pairs={{0,16},{4,20},{8,24},{12,28},{16,0},{20,4},{24,8},{28,12},{1,17},{... | collective-permute-start | bytes 165896 | tf_op jit(solution)/shard_map/ppermute | solution.py:46
  6.8 4.2 %collective-permute-start.2 = (bf16[8,3456]{1,0:T(8,128)(2,1)S(1)}, bf16[8,3456]{1,0:T(8,128)(2,1)S(1)}, u32[]{:S(2)}, u32[]{:S(2)}) collective-permute-start(bf16[8,3456]{1,0:T(8,128)(2,1)S(1)} %pack.1._.refs_0_), channel_id=1, source_target_pairs={{0,8},{4,12},{8,0},{12,4},{16,24},{20,28},{24,16},{28,20},{1,9},{5... | collective-permute-start | bytes 165896 | tf_op jit(solution)/shard_map/ppermute | solution.py:46
  12.1 7.5 %collective-permute-start.7 = (bf16[24,1024]{1,0:T(8,128)(2,1)S(1)}, bf16[24,1024]{1,0:T(8,128)(2,1)S(1)}, u32[]{:S(2)}, u32[]{:S(2)}) collective-permute-start(bf16[24,1024]{1,0:T(8,128)(2,1)S(1)} %get-tuple-element.34.acts_ref.refs_0_), channel_id=1, source_target_pairs={{0,2},{1,3},{2,0},{3,1},{4,6},{5,7},{6,4},{7,5},{8,10},{9,11},{10,... | collective-permute-start | bytes 147464 | tf_op jit(solution)/shard_map/ppermute | solution.py:46
  14.7 6.0 %collective-permute-start.6 = (bf16[24,1024]{1,0:T(8,128)(2,1)S(1)}, bf16[24,1024]{1,0:T(8,128)(2,1)S(1)}, u32[]{:S(2)}, u32[]{:S(2)}) collective-permute-start(bf16[24,1024]{1,0:T(8,128)(2,1)S(1)} %get-tuple-element.34.acts_ref.refs_0_), channel_id=1, source_target_pairs={{0,3},{1,2},{2,1},{3,0},{4,7},{5,6},{6,5},{7,4},{8,11},{9,10},{10,... | collective-permute-start | bytes 147464 | tf_op jit(solution)/shard_map/ppermute | solution.py:46
  16.0 4.6 %collective-permute-start.5 = (bf16[24,1024]{1,0:T(8,128)(2,1)S(1)}, bf16[24,1024]{1,0:T(8,128)(2,1)S(1)}, u32[]{:S(2)}, u32[]{:S(2)}) collective-permute-start(bf16[24,1024]{1,0:T(8,128)(2,1)S(1)} %get-tuple-element.34.acts_ref.refs_0_), channel_id=1, source_target_pairs={{0,1},{1,0},{2,3},{3,2},{4,5},{5,4},{6,7},{7,6},{8,9},{9,8},{10,11... | collective-permute-start | bytes 147464 | tf_op jit(solution)/shard_map/ppermute | solution.py:46
  21.9 1.4 %collective-permute-start.8 = (f32[24,1280]{1,0:T(8,128)S(1)}, f32[24,1280]{1,0:T(8,128)S(1)}, u32[]{:S(2)}, u32[]{:S(2)}) collective-permute-start(f32[24,1280]{1,0:T(8,128)S(1)} %recon_send.1), channel_id=1, source_target_pairs={{0,4},{4,0},{8,12},{12,8},{16,20},{20,16},{24,28},{28,24},{1,5},{5... | collective-permute-start | bytes 368648 | tf_op jit(solution)/shard_map/ppermute | solution.py:46
  23.4 5.3 %collective-permute-start.11 = (bf16[8,3584]{1,0:T(8,128)(2,1)S(1)}, bf16[8,3584]{1,0:T(8,128)(2,1)S(1)}, u32[]{:S(2)}, u32[]{:S(2)}) collective-permute-start(bf16[8,3584]{1,0:T(8,128)(2,1)S(1)} %pair_sum.1.refs_0_), channel_id=1, source_target_pairs={{0,24},{4,28},{8,16},{12,20},{16,8},{20,12},{24,0},{28,4},{1,25},{... | collective-permute-start | bytes 172040 | tf_op jit(solution)/shard_map/ppermute | solution.py:46
  24.9 4.9 %collective-permute-start.10 = (bf16[8,3584]{1,0:T(8,128)(2,1)S(1)}, bf16[8,3584]{1,0:T(8,128)(2,1)S(1)}, u32[]{:S(2)}, u32[]{:S(2)}) collective-permute-start(bf16[8,3584]{1,0:T(8,128)(2,1)S(1)} %pair_sum.1.refs_0_), channel_id=1, source_target_pairs={{0,16},{4,20},{8,24},{12,28},{16,0},{20,4},{24,8},{28,12},{1,17},{... | collective-permute-start | bytes 172040 | tf_op jit(solution)/shard_map/ppermute | solution.py:46
  25.6 4.4 %collective-permute-start.9 = (bf16[8,3584]{1,0:T(8,128)(2,1)S(1)}, bf16[8,3584]{1,0:T(8,128)(2,1)S(1)}, u32[]{:S(2)}, u32[]{:S(2)}) collective-permute-start(bf16[8,3584]{1,0:T(8,128)(2,1)S(1)} %pair_sum.1.refs_0_), channel_id=1, source_target_pairs={{0,8},{4,12},{8,0},{12,4},{16,24},{20,28},{24,16},{28,20},{1,9},{5... | collective-permute-start | bytes 172040 | tf_op jit(solution)/shard_map/ppermute | solution.py:46
  30.1 1.9 %collective-permute-start.12 = (bf16[32,1152]{1,0:T(8,128)(2,1)S(1)}, bf16[32,1152]{1,0:T(8,128)(2,1)S(1)}, u32[]{:S(2)}, u32[]{:S(2)}) collective-permute-start(bf16[32,1152]{1,0:T(8,128)(2,1)S(1)} %get-tuple-element.36.mine_ref), channel_id=1, source_target_pairs={{0,4},{4,0},{8,12},{12,8},{16,20},{20,16},{24,28},{28,24},{1,5},{5... | collective-permute-start | bytes 221192 | tf_op jit(solution)/shard_map/ppermute | solution.py:46
  34.3 9.1 %collective-permute-start.13 = (bf16[24,1152]{1,0:T(8,128)(2,1)S(1)}, bf16[24,1152]{1,0:T(8,128)(2,1)S(1)}, u32[]{:S(2)}, u32[]{:S(2)}) collective-permute-start(bf16[24,1152]{1,0:T(8,128)(2,1)S(1)} %get-tuple-element.48), channel_id=1, source_target_pairs={{0,2},{1,3},{2,0},{3,1},{4,6},{5,7},{6,4},{7,5},{8,10},{9,11},{10,... | collective-permute-start | bytes 165896 | tf_op jit(solution)/shard_map/ppermute | solution.py:46
  36.1 7.3 %collective-permute-start.14 = (bf16[24,1152]{1,0:T(8,128)(2,1)S(1)}, bf16[24,1152]{1,0:T(8,128)(2,1)S(1)}, u32[]{:S(2)}, u32[]{:S(2)}) collective-permute-start(bf16[24,1152]{1,0:T(8,128)(2,1)S(1)} %get-tuple-element.49), channel_id=1, source_target_pairs={{0,3},{1,2},{2,1},{3,0},{4,7},{5,6},{6,5},{7,4},{8,11},{9,10},{10,... | collective-permute-start | bytes 165896 | tf_op jit(solution)/shard_map/ppermute | solution.py:46
  37.5 6.0 %collective-permute-start.15 = (bf16[24,1152]{1,0:T(8,128)(2,1)S(1)}, bf16[24,1152]{1,0:T(8,128)(2,1)S(1)}, u32[]{:S(2)}, u32[]{:S(2)}) collective-permute-start(bf16[24,1152]{1,0:T(8,128)(2,1)S(1)} %get-tuple-element.50), channel_id=1, source_target_pairs={{0,1},{1,0},{2,3},{3,2},{4,5},{5,4},{6,7},{7,6},{8,9},{9,8},{10,11... | collective-permute-start | bytes 165896 | tf_op jit(solution)/shard_map/ppermute | solution.py:46
